TPU v7x, 32 devices: a whole 2x2x4 slice. The times are simulated.
32 devices in a mesh: rows: 4 (over z), seq: 8 (over y, x, core).
Axes of the slice: x: 2, y: 2, z: 4, core: 2. Of those that a mesh axis runs over, the one named last changes fastest.
Arguments:
- tokens: bfloat16 [4, 2048, 2048], P('rows', 'seq'), may hold values from -6 to 6
- segments: int32 [4, 2048], P('rows', 'seq'), may hold values from 0 to 4, as said below
- positions: int32 [4, 2048], P('rows', 'seq'), may hold values from 0 to 4095, as said below
- cotangent: bfloat16 [4, 2048, 2048], P('rows', 'seq'), may hold values from -6 to 6
- gain_attn: bfloat16 [2048], P(('rows', 'seq')), may hold values from 0.099609375 to 1.8984375
- query_key_value_weight: bfloat16 [2048, 2304], P(('rows', 'seq')), may hold values from -0.1875 to 0.1875
- gain_q: bfloat16 [64], replicated, may hold values from 0.099609375 to 1.8984375
- gain_k: bfloat16 [64], replicated, may hold values from 0.099609375 to 1.8984375
- w_out: bfloat16 [1536, 2048], P(None, ('rows', 'seq')), may hold values from -2 to 2
- gain_ffn: bfloat16 [2048], P(('rows', 'seq')), may hold values from 0.099609375 to 1.8984375
- w_gate: bfloat16 [2048, 4096], P('rows', 'seq'), may hold values from -0.125 to 0.125
- w_up: bfloat16 [2048, 4096], P('rows', 'seq'), may hold values from -0.125 to 0.125
- w_down: bfloat16 [4096, 2048], P('seq', 'rows'), may hold values from -0.09375 to 0.09375
Outputs:
- layer_out: bfloat16 [4, 2048, 2048], P('rows', 'seq')
- grad_tokens: float32 [4, 2048, 2048], P('rows', 'seq')
- grad_gain_attn: float32 [2048], P(('rows', 'seq'))
- grad_w_qkv: float32 [2048, 2304], P(('rows', 'seq'))
- grad_gain_q: float32 [64], replicated
- grad_gain_k: float32 [64], replicated
- grad_w_out: float32 [1536, 2048], P(None, ('rows', 'seq'))
- grad_gain_ffn: float32 [2048], P(('rows', 'seq'))
- grad_w_gate: float32 [2048, 4096], P('rows', 'seq')
- grad_w_up: float32 [2048, 4096], P('rows', 'seq')
- grad_w_down: float32 [4096, 2048], P('seq', 'rows')
Inputs may be any that keep to these rules, and one draw needn't show every extreme that they name: `segments`: along a row segment numbers never fall, and every row holds all of them. Within a document positions rise by one from token to token; every row's first document starts at 0.
All inputs are finite; a program needn't handle non-finite values.
Results may differ from a plain program's by a relative error of at most 0.023.
Values may be sent and summed in bfloat16 or wider, within the bound.
A program may use at most 320 MiB of HBM per device.

v0:
```python
import math

import jax
import jax.numpy as jnp
from jax import lax
from jax.sharding import PartitionSpec as P

QUERY_HEADS = 24
KEY_VALUE_HEADS = 6
HEAD_SIZE = 64


EPSILON = 1e-06
THETA = 10000.0
NEGATIVE_FILLER = -1e30


def rotary_tables(positions):
    half_size = HEAD_SIZE // 2
    inverse = jnp.exp(-math.log(THETA) * jnp.arange(half_size, dtype=jnp.float32) * 2.0 / HEAD_SIZE)
    angles = positions.astype(jnp.float32)[:, None] * inverse[None, :]
    angles = jnp.concatenate([angles, angles], axis=1)
    return (jnp.cos(angles)[:, None, :], jnp.sin(angles)[:, None, :])


def rotate_half(vector):
    first_half = vector[..., : HEAD_SIZE // 2]
    second_half = vector[..., HEAD_SIZE // 2 :]
    return jnp.concatenate([-second_half, first_half], axis=-1)


def rotate_back(vector):
    first_half = vector[..., : HEAD_SIZE // 2]
    second_half = vector[..., HEAD_SIZE // 2 :]
    return jnp.concatenate([second_half, -first_half], axis=-1)


def apply_rotary(vector, cosine_lookup, sine_lookup):
    return vector * cosine_lookup + rotate_half(vector) * sine_lookup


def undo_rotary(gradient, cosine_lookup, sine_lookup):
    return gradient * cosine_lookup + rotate_back(gradient * sine_lookup)


def norm_back(grad_normed, values_in, inv_rms, gain):
    scaled = grad_normed * gain.astype(jnp.float32)
    gain_grad = jnp.sum(grad_normed * values_in * inv_rms, axis=0)
    input_grad = inv_rms * scaled - values_in * inv_rms**3 * jnp.mean(
        scaled * values_in, axis=-1, keepdims=True
    )
    return (input_grad, gain_grad)


def head_norm_back(grad_normed, values_in, inv_rms, gain):
    scaled = grad_normed * gain
    gain_grad = jnp.sum(grad_normed * values_in * inv_rms, axis=(0, 1))
    input_grad = inv_rms * scaled - values_in * inv_rms**3 * jnp.mean(
        scaled * values_in, axis=-1, keepdims=True
    )
    return (input_grad, gain_grad)


def head_inverse(values_in):
    return lax.rsqrt(jnp.mean(values_in * values_in, axis=-1, keepdims=True) + EPSILON)


def body(
    tokens,
    segments,
    positions,
    cotangent,
    gain_attn,
    query_key_value_weight,
    gain_q,
    gain_k,
    w_out,
    gain_ffn,
    w_gate,
    w_up,
    w_down,
):
    query_total_width = QUERY_HEADS * HEAD_SIZE
    key_value_width = KEY_VALUE_HEADS * HEAD_SIZE
    query_group_count = QUERY_HEADS // KEY_VALUE_HEADS
    head_scale_factor = HEAD_SIZE ** (-0.5)
    gain_one, qkv_weight, out_weight, gain_two = (
        lax.all_gather(gain_attn, ("rows", "seq"), axis=0, tiled=True),
        lax.all_gather(query_key_value_weight, ("rows", "seq"), axis=0, tiled=True),
        lax.all_gather(w_out, ("rows", "seq"), axis=1, tiled=True),
        lax.all_gather(gain_ffn, ("rows", "seq"), axis=0, tiled=True),
    )
    gate_slab, up_slab, down_slab = (
        lax.all_gather(w_gate, "rows", axis=0, tiled=True),
        lax.all_gather(w_up, "rows", axis=0, tiled=True),
        lax.all_gather(w_down, "rows", axis=1, tiled=True),
    )
    query_gain = gain_q.astype(jnp.float32)
    key_norm_weight = gain_k.astype(jnp.float32)
    inputs = tokens[0].astype(jnp.float32)
    sharded_row_slice = inputs.shape[0]
    row_length = sharded_row_slice * lax.axis_size("seq")
    query_index = lax.axis_index("seq") * sharded_row_slice + jnp.arange(
        sharded_row_slice, dtype=jnp.int32
    )
    segment_low = segments[0].astype(jnp.bfloat16)
    cosine_lookup, sine_lookup = rotary_tables(positions[0])
    inv_rms_one = lax.rsqrt(jnp.mean(inputs * inputs, axis=-1, keepdims=True) + EPSILON)
    normed = (inputs * inv_rms_one * gain_one.astype(jnp.float32)).astype(jnp.bfloat16)
    projection_output = jnp.dot(normed, qkv_weight, preferred_element_type=jnp.float32)
    query_raw = projection_output[:, :query_total_width].reshape(
        sharded_row_slice, QUERY_HEADS, HEAD_SIZE
    )
    unnormed_key = projection_output[
        :, query_total_width : query_total_width + key_value_width
    ].reshape(sharded_row_slice, KEY_VALUE_HEADS, HEAD_SIZE)
    query_inv = head_inverse(query_raw)
    key_inv = head_inverse(unnormed_key)
    query_rows = apply_rotary(query_raw * query_inv * query_gain, cosine_lookup, sine_lookup)
    keys_rot = apply_rotary(unnormed_key * key_inv * key_norm_weight, cosine_lookup, sine_lookup)
    query_reduced_precision = (
        (query_rows * head_scale_factor)
        .astype(jnp.bfloat16)
        .reshape(sharded_row_slice, KEY_VALUE_HEADS, query_group_count, HEAD_SIZE)
    )
    key_value = jnp.concatenate(
        [
            keys_rot.reshape(sharded_row_slice, key_value_width),
            projection_output[:, query_total_width + key_value_width :],
        ],
        axis=1,
    ).astype(jnp.bfloat16)
    block_extent = min(sharded_row_slice, 512)

    def key_blocks(shard_piece):
        block_pair_step, piece_segments = shard_piece
        count_of_blocks = block_pair_step.shape[1] // block_extent
        key_value_blocks = block_pair_step[0].reshape(
            count_of_blocks, block_extent, 2, KEY_VALUE_HEADS, HEAD_SIZE
        )
        blocks_seg = piece_segments[0].reshape(count_of_blocks, block_extent)
        blocks_index = jnp.arange(count_of_blocks * block_extent, dtype=jnp.int32).reshape(
            count_of_blocks, block_extent
        )
        return (key_value_blocks, blocks_seg, blocks_index)

    def allowed_mask(block_seg, block_index):
        return (block_index[None, None, None, :] <= query_index[:, None, None, None]) & (
            block_seg[None, None, None, :] == segment_low[:, None, None, None]
        )

    initial = (
        jnp.full(
            (sharded_row_slice, KEY_VALUE_HEADS, query_group_count), NEGATIVE_FILLER, jnp.float32
        ),
        jnp.zeros((sharded_row_slice, KEY_VALUE_HEADS, query_group_count), jnp.float32),
        jnp.zeros((sharded_row_slice, KEY_VALUE_HEADS, query_group_count, HEAD_SIZE), jnp.float32),
    )

    def forward_one_block(block_state, key_block):
        running_max, running_sum, running_acc = block_state
        block_kv, block_seg, block_index = key_block
        scores = jnp.einsum(
            "tgmd,ngd->tgmn",
            query_reduced_precision,
            block_kv[:, 0],
            preferred_element_type=jnp.float32,
        )
        allowed = allowed_mask(block_seg, block_index)
        masked = jnp.where(allowed, scores, NEGATIVE_FILLER)
        new_max = jnp.maximum(running_max, jnp.max(masked, axis=-1))
        weights = jnp.where(allowed, jnp.exp(masked - new_max[..., None]), 0.0)
        factor = jnp.exp(running_max - new_max)
        running_sum = running_sum * factor + jnp.sum(weights, axis=-1)
        running_acc = running_acc * factor[..., None] + jnp.einsum(
            "tgmn,ngd->tgmd",
            weights.astype(jnp.bfloat16),
            block_kv[:, 1],
            preferred_element_type=jnp.float32,
        )
        return ((new_max, running_sum, running_acc), None)

    final_state, unused = lax.scan(
        forward_one_block,
        initial,
        key_blocks(
            (
                lax.all_gather(key_value[None], "seq", axis=1, tiled=True),
                lax.all_gather(segment_low[None], "seq", axis=1, tiled=True),
            )
        ),
    )
    running_max, running_sum, running_acc = final_state
    attention_output = running_acc / running_sum[..., None]
    log_total = running_max + jnp.log(running_sum)
    merged = attention_output.reshape(sharded_row_slice, query_total_width).astype(jnp.bfloat16)
    residual = inputs + jnp.dot(merged, out_weight, preferred_element_type=jnp.float32)
    inv_rms_two = lax.rsqrt(jnp.mean(residual * residual, axis=-1, keepdims=True) + EPSILON)
    normed_two = (residual * inv_rms_two * gain_two.astype(jnp.float32)).astype(jnp.bfloat16)
    gate_full, up_full, down_full = (
        lax.all_gather(gate_slab, "seq", axis=1, tiled=True),
        lax.all_gather(up_slab, "seq", axis=1, tiled=True),
        lax.all_gather(down_slab, "seq", axis=0, tiled=True),
    )
    gate_act = jnp.dot(normed_two, gate_full, preferred_element_type=jnp.float32)
    up_act = jnp.dot(normed_two, up_full, preferred_element_type=jnp.float32)
    hidden = (jax.nn.silu(gate_act) * up_act).astype(jnp.bfloat16)
    branch = jnp.dot(hidden, down_full, preferred_element_type=jnp.float32)
    output_rows = residual + branch
    out_grad = cotangent[0].astype(jnp.float32)
    out_grad_low = cotangent[0]
    hidden_grad = jnp.dot(out_grad_low, down_full.T, preferred_element_type=jnp.float32)
    sigmoid_gate = jax.nn.sigmoid(gate_act)
    gate_grad = (
        hidden_grad * up_act * sigmoid_gate * (1.0 + gate_act * (1.0 - sigmoid_gate))
    ).astype(jnp.bfloat16)
    up_grad = (hidden_grad * gate_act * sigmoid_gate).astype(jnp.bfloat16)
    gate_grad, up_grad = (gate_grad, up_grad)
    normed_two_grad = jnp.dot(gate_grad, gate_full.T, preferred_element_type=jnp.float32) + jnp.dot(
        up_grad, up_full.T, preferred_element_type=jnp.float32
    )
    gate_wgrad, up_wgrad, down_wgrad = (
        lax.psum_scatter(
            jnp.dot(normed_two.T, gate_grad, preferred_element_type=jnp.float32).astype(
                jnp.bfloat16
            ),
            "seq",
            scatter_dimension=1,
            tiled=True,
        ).astype(jnp.float32),
        lax.psum_scatter(
            jnp.dot(normed_two.T, up_grad, preferred_element_type=jnp.float32).astype(jnp.bfloat16),
            "seq",
            scatter_dimension=1,
            tiled=True,
        ).astype(jnp.float32),
        lax.psum_scatter(
            jnp.dot(hidden.T, out_grad_low, preferred_element_type=jnp.float32).astype(
                jnp.bfloat16
            ),
            "seq",
            scatter_dimension=0,
            tiled=True,
        ).astype(jnp.float32),
    )
    grad_gate, grad_up, grad_down = (
        lax.psum_scatter(
            gate_wgrad.astype(jnp.bfloat16), "rows", scatter_dimension=0, tiled=True
        ).astype(jnp.float32),
        lax.psum_scatter(
            up_wgrad.astype(jnp.bfloat16), "rows", scatter_dimension=0, tiled=True
        ).astype(jnp.float32),
        lax.psum_scatter(
            down_wgrad.astype(jnp.bfloat16), "rows", scatter_dimension=1, tiled=True
        ).astype(jnp.float32),
    )
    residual_norm_grad, gain_two_grad = norm_back(normed_two_grad, residual, inv_rms_two, gain_two)
    residual_grad = out_grad + residual_norm_grad
    branch_grad = residual_grad.astype(jnp.bfloat16)
    out_wgrad = jnp.dot(merged.T, branch_grad, preferred_element_type=jnp.float32)
    attended_grad = (
        jnp.dot(branch_grad, out_weight.T, preferred_element_type=jnp.float32)
        .astype(jnp.bfloat16)
        .reshape(sharded_row_slice, KEY_VALUE_HEADS, query_group_count, HEAD_SIZE)
    )
    row_delta = jnp.sum(attended_grad.astype(jnp.float32) * attention_output, axis=-1)
    start_grads = (
        jnp.zeros((sharded_row_slice, KEY_VALUE_HEADS, query_group_count, HEAD_SIZE), jnp.float32),
        jnp.zeros((row_length, 2 * key_value_width), jnp.float32),
    )

    def backward_one_block(block_state, key_block):
        query_grad, key_value_gradient = block_state
        block_kv, block_seg, block_index = key_block
        scores = jnp.einsum(
            "tgmd,ngd->tgmn",
            query_reduced_precision,
            block_kv[:, 0],
            preferred_element_type=jnp.float32,
        )
        allowed = allowed_mask(block_seg, block_index)
        probabilities = jnp.where(
            allowed,
            jnp.exp(jnp.where(allowed, scores, NEGATIVE_FILLER) - log_total[..., None]),
            0.0,
        )
        prob_grad = jnp.einsum(
            "tgmd,ngd->tgmn", attended_grad, block_kv[:, 1], preferred_element_type=jnp.float32
        )
        score_grad = (probabilities * (prob_grad - row_delta[..., None])).astype(jnp.bfloat16)
        query_grad = query_grad + jnp.einsum(
            "tgmn,ngd->tgmd", score_grad, block_kv[:, 0], preferred_element_type=jnp.float32
        )
        key_grad = jnp.einsum(
            "tgmn,tgmd->ngd",
            score_grad,
            query_reduced_precision,
            preferred_element_type=jnp.float32,
        )
        value_grad = jnp.einsum(
            "tgmn,tgmd->ngd",
            probabilities.astype(jnp.bfloat16),
            attended_grad,
            preferred_element_type=jnp.float32,
        )
        fresh_rows = jnp.concatenate(
            [
                key_grad.reshape(block_extent, key_value_width),
                value_grad.reshape(block_extent, key_value_width),
            ],
            axis=1,
        )
        row_start = block_index[0]
        current = lax.dynamic_slice_in_dim(key_value_gradient, row_start, block_extent, 0)
        key_value_gradient = lax.dynamic_update_slice_in_dim(
            key_value_gradient, current + fresh_rows, row_start, 0
        )
        return ((query_grad, key_value_gradient), None)

    final_state, unused = lax.scan(
        backward_one_block,
        start_grads,
        key_blocks(
            (
                lax.all_gather(key_value[None], "seq", axis=1, tiled=True),
                lax.all_gather(segment_low[None], "seq", axis=1, tiled=True),
            )
        ),
    )
    query_grad, kv_grad_all = final_state
    key_value_gradient = lax.psum_scatter(
        kv_grad_all[None].astype(jnp.bfloat16), "seq", scatter_dimension=1, tiled=True
    ).astype(jnp.float32)[0]
    query_normed_grad = undo_rotary(
        query_grad.reshape(sharded_row_slice, QUERY_HEADS, HEAD_SIZE) * head_scale_factor,
        cosine_lookup,
        sine_lookup,
    )
    key_normed_grad = undo_rotary(
        key_value_gradient[:, :key_value_width].reshape(
            sharded_row_slice, KEY_VALUE_HEADS, HEAD_SIZE
        ),
        cosine_lookup,
        sine_lookup,
    )
    query_raw_grad, query_gain_grad = head_norm_back(
        query_normed_grad, query_raw, query_inv, query_gain
    )
    key_raw_grad, key_gain_grad = head_norm_back(
        key_normed_grad, unnormed_key, key_inv, key_norm_weight
    )
    projected_grad = jnp.concatenate(
        [
            query_raw_grad.reshape(sharded_row_slice, query_total_width),
            key_raw_grad.reshape(sharded_row_slice, key_value_width),
            key_value_gradient[:, key_value_width:],
        ],
        axis=1,
    ).astype(jnp.bfloat16)
    normed_grad = jnp.dot(projected_grad, qkv_weight.T, preferred_element_type=jnp.float32)
    qkv_wgrad = jnp.dot(normed.T, projected_grad, preferred_element_type=jnp.float32)
    input_norm_grad, gain_one_grad = norm_back(normed_grad, inputs, inv_rms_one, gain_one)
    input_grad = residual_grad + input_norm_grad
    device_count = lax.axis_size("rows") * lax.axis_size("seq")
    head_terms = jnp.broadcast_to(
        jnp.concatenate([query_gain_grad, key_gain_grad])[None], (device_count, 2 * HEAD_SIZE)
    )
    reduced = (
        lax.psum_scatter(gain_one_grad, ("rows", "seq"), scatter_dimension=0, tiled=True),
        lax.psum_scatter(qkv_wgrad, ("rows", "seq"), scatter_dimension=0, tiled=True),
        lax.psum_scatter(out_wgrad, ("rows", "seq"), scatter_dimension=1, tiled=True),
        lax.psum_scatter(gain_two_grad, ("rows", "seq"), scatter_dimension=0, tiled=True),
        lax.psum_scatter(head_terms, ("rows", "seq"), scatter_dimension=0, tiled=True),
    )
    head_sums = reduced[4][0]
    return (
        output_rows.astype(jnp.bfloat16)[None],
        input_grad[None],
        reduced[0],
        reduced[1],
        head_sums[:HEAD_SIZE],
        head_sums[HEAD_SIZE:],
        reduced[2],
        reduced[3],
        grad_gate,
        grad_up,
        grad_down,
    )


def solution(mesh):
    return jax.shard_map(
        body,
        mesh=mesh,
        in_specs=(
            P("rows", "seq", None),
            P("rows", "seq"),
            P("rows", "seq"),
            P("rows", "seq", None),
            P(("rows", "seq")),
            P(("rows", "seq"), None),
            P(),
            P(),
            P(None, ("rows", "seq")),
            P(("rows", "seq")),
            P("rows", "seq"),
            P("rows", "seq"),
            P("seq", "rows"),
        ),
        out_specs=(
            P("rows", "seq", None),
            P("rows", "seq", None),
            P(("rows", "seq")),
            P(("rows", "seq"), None),
            P(),
            P(),
            P(None, ("rows", "seq")),
            P(("rows", "seq")),
            P("rows", "seq"),
            P("rows", "seq"),
            P("seq", "rows"),
        ),
        check_vma=False,
    )
```

profile of v0, /device:TPU:0, one launch (start us, length us, event | category | flops | bytes accessed | tf_op | source)
XLA Modules:
  0.0 1568.7 jit_solution(10052581901981620427)
XLA Ops:
  11.8 43.0 %all-reduce.6 = (bf16[2048]{0:T(1024)(128)(2,1)S(1)}, bf16[2048]{0:T(1024)(128)(2,1)S(1)}) all-reduce(bf16[2048]{0:T(1024)(128)(2,1)S(1)} %dynamic-update-slice, bf16[2048]{0:T(1024)(128)(2,1)S(1)} %dynamic-update-slice.1), channel_id=1, replica_groups=mesh['rows'=4,'seq'=8] {'rows','seq'}, use_global_device_ids=true, to_apply=%add | all-reduce | flops 4096 | bytes 16384
  59.0 37.1 %all-gather.10.cloned.1.call-done = bf16[2048,2304]{1,0:T(8,128)(2,1)} async-done(((bf16[64,2304]{1,0:T(8,128)(2,1)}), bf16[2048,2304]{1,0:T(8,128)(2,1)}) %all-gather.10.cloned.1.call-update) | async-done | bytes 9437200 | tf_op jit(solution)/shard_map/all_gather | solution.py:89
  96.1 6.3 fusion.58
  111.9 30.4 %all-gather.16.cloned.1.call-done = bf16[2048,512]{1,0:T(8,128)(2,1)} async-done(((bf16[512,512]{1,0:T(8,128)(2,1)}), bf16[2048,512]{1,0:T(8,128)(2,1)}) %all-gather.16.cloned.1.call-update) | async-done | bytes 2097168 | tf_op jit(solution)/shard_map/all_gather | solution.py:94
  142.3 46.2 %all-gather.20.cloned.1.call-done = bf16[2048,512]{1,0:T(8,128)(2,1)} async-done(((bf16[512,512]{1,0:T(8,128)(2,1)}), bf16[2048,512]{1,0:T(8,128)(2,1)}) %all-gather.20.cloned.1.call-update) | async-done | bytes 2097168 | tf_op jit(solution)/shard_map/all_gather | solution.py:95
  188.6 46.0 %all-gather.24.cloned.1.call-done = bf16[512,2048]{1,0:T(8,128)(2,1)} async-done(((bf16[512,512]{1,0:T(8,128)(2,1)}), bf16[512,2048]{1,0:T(8,128)(2,1)}) %all-gather.24.cloned.1.call-update) | async-done | bytes 2097168 | tf_op jit(solution)/shard_map/all_gather | solution.py:96
  234.8 8.9 all_gather.38
  251.2 16.8 %all-gather.12.cloned.1.call-done = bf16[1,2048,768]{2,1,0:T(8,128)(2,1)} async-done(((bf16[1,256,768]{2,1,0:T(8,128)(2,1)}), bf16[1,2048,768]{2,1,0:T(8,128)(2,1)}) %all-gather.12.cloned.1.call-update) | async-done | bytes 3145744 | tf_op jit(solution)/shard_map/all_gather | solution.py:188
  274.9 99.2 %while.28 = (s32[]{:T(128)}, f32[256,6,4]{0,2,1:T(4,128)S(1)}, f32[256,6,4]{0,2,1:T(4,128)S(1)}, f32[256,6,4,64]{0,3,2,1:T(8,128)S(1)}, s32[8,256]{1,0:T(8,128)S...) while((s32[]{:T(128)}, f32[256,6,4]{0,2,1:T(4,128)S(1)}, ...), condition=%wide.region_6.7_spmd.clone, body=%wide.region_3.6_spmd.clone.sunk | while | flops 419920128 | bytes 49814700 | solution.py:183
  276.1 4.8 fusion.120
  288.5 4.8 fusion.120
  300.9 4.8 fusion.120
  305.7 4.3 fusion.121
  313.2 4.9 fusion.120
  318.2 4.3 fusion.121
  325.7 4.8 fusion.120
  330.6 4.3 fusion.121
  338.1 4.8 fusion.120
  350.7 4.8 fusion.120
  355.5 4.3 fusion.121
  363.0 4.8 fusion.120
  367.8 4.3 fusion.121
  376.1 5.0 multiply_reduce_fusion.2
  381.4 52.4 %all-gather.18.cloned.1.call-done = bf16[2048,4096]{1,0:T(8,128)(2,1)} async-done(((bf16[2048,512]{1,0:T(8,128)(2,1)}), bf16[2048,4096]{1,0:T(8,128)(2,1)}) %all-gather.18.cloned.1.call-update) | async-done | bytes 16777232 | tf_op jit(solution)/shard_map/all_gather | solution.py:201
  433.8 10.4 fusion.69
  444.2 84.7 %all-gather.22.cloned.1.call-done = bf16[2048,4096]{1,0:T(8,128)(2,1)} async-done(((bf16[2048,512]{1,0:T(8,128)(2,1)}), bf16[2048,4096]{1,0:T(8,128)(2,1)}) %all-gather.22.cloned.1.call-update) | async-done | bytes 16777232 | tf_op jit(solution)/shard_map/all_gather | solution.py:202
  528.8 10.9 fusion.70
  539.7 80.9 %all-gather.26.cloned.1.call-done = bf16[4096,2048]{1,0:T(8,128)(2,1)} async-done(((bf16[512,2048]{1,0:T(8,128)(2,1)}), bf16[4096,2048]{1,0:T(8,128)(2,1)}) %all-gather.26.cloned.1.call-update) | async-done | bytes 16777232 | tf_op jit(solution)/shard_map/all_gather | solution.py:203
  620.6 13.8 multiply_convert_fusion
  634.4 9.7 convolution_convert_fusion.2
  644.2 12.1 convolution_convert_fusion.1
  657.2 15.7 fusion.71
  672.9 13.8 multiply_reduce_fusion
  690.4 4.9 convolution_convert_fusion.3
  699.1 10.3 convolution_convert_fusion
  712.5 242.5 %while.29 = (s32[]{:T(128)}, f32[256,6,4,64]{0,3,2,1:T(8,128)}, f32[2048,768]{1,0:T(8,128)}, bf16[8,256,2,6,64]{1,4,3,2,0:T(8,128)(2,1)}, s32[8,256]{1,0:T(8,128...) while((s32[]{:T(128)}, f32[256,6,4,64]{0,3,2,1:T(8,128)}, ...), condition=%wide.region_11.12_spmd.clone, body=%wide.region_10.11_spmd.clone.sunk | while | flops 1023869184 | bytes 48839952 | solution.py:320
  954.9 5.0 convert_bitcast_fusion
  961.2 38.1 %reduce-scatter.24.cloned.1.call-done = bf16[512,2048]{1,0:T(8,128)(2,1)} async-done(((bf16[4096,2048]{1,0:T(8,128)(2,1)}), bf16[512,2048]{1,0:T(8,128)(2,1)}) %reduce-scatter.24.cloned.1.call-update) | async-done | bytes 2097168 | tf_op jit(solution)/shard_map/reduce_scatter | solution.py:237
  999.3 6.4 fusion.52
  1022.8 6.5 multiply_reduce_fusion.3
  1029.4 19.5 %reduce-scatter.10.cloned.1.call-done = bf16[1,256,768]{2,1,0:T(8,128)(2,1)} async-done(((bf16[1,2048,768]{2,1,0:T(8,128)(2,1)}), bf16[1,256,768]{2,1,0:T(8,128)(2,1)}) %reduce-scatter.10.cloned.1.call-update) | async-done | bytes 393232 | tf_op jit(solution)/shard_map/reduce_scatter | solution.py:331
  1054.4 8.2 fusion.55
  1064.5 12.0 fusion.30
  1077.4 8.8 fusion.40
  1086.2 43.0 %all-reduce.5 = (f32[2048]{0:T(1024)S(1)}, f32[32,128]{1,0:T(8,128)S(1)}, f32[2048]{0:T(1024)S(1)}) all-reduce(f32[2048]{0:T(1024)} %get-tuple-element.301, f32[32,128]{1,0:T(8,128)S(1)} %broadcast_in_dim.61, f32[2048]{0:T(1024)} %get-tuple-element.299), channel_id=3, replica_groups=mesh['rows'=4,'seq'=8] {'rows','seq'}, use_global_device_ids=true, to_apply=%region_17.18.clone | all-reduce | flops 8192 | bytes 65536
  1143.2 43.3 %reduce-scatter.26.cloned.1.call-done = bf16[512,512]{1,0:T(8,128)(2,1)} async-done(((bf16[512,2048]{1,0:T(8,128)(2,1)}), bf16[512,512]{1,0:T(8,128)(2,1)}) %reduce-scatter.26.cloned.1.call-update) | async-done | bytes 524304 | tf_op jit(solution)/shard_map/reduce_scatter | solution.py:253
  1188.7 159.0 %reduce-scatter.14.cloned.1.call-done = f32[1536,64]{0,1:T(8,128)} async-done(((f32[1536,2048]{0,1:T(8,128)}), f32[1536,64]{0,1:T(8,128)}) %reduce-scatter.14.cloned.1.call-update) | async-done | bytes 393232 | tf_op jit(solution)/shard_map/reduce_scatter | solution.py:371
  1347.6 214.0 %reduce-scatter.12.cloned.1.call-done = f32[64,2304]{1,0:T(8,128)} async-done(((f32[2048,2304]{1,0:T(8,128)}), f32[64,2304]{1,0:T(8,128)}) %reduce-scatter.12.cloned.1.call-update) | async-done | bytes 589840 | tf_op jit(solution)/shard_map/reduce_scatter | solution.py:370
  (503 shorter events, 353.8 us)
Async XLA Ops:
  7.2 50.8 %copy-start.54 = (bf16[64]{0:T(256)(128)(2,1)S(1)}, bf16[64]{0:T(256)(128)(2,1)}, u32[]{:S(2)}) copy-start(bf16[64]{0:T(256)(128)(2,1)} %param.24) | copy-start | bytes 388
  7.2 50.9 %copy-start.9 = (bf16[1,256,2048]{2,1,0:T(8,128)(2,1)S(1)}, bf16[1,256,2048]{2,1,0:T(8,128)(2,1)}, u32[]{:S(2)}) copy-start(bf16[1,256,2048]{2,1,0:T(8,128)(2,1)} %param.17) | copy-start | bytes 3145732
  7.2 88.9 %all-gather.10.cloned.1.call-start = ((), (), s32[]{:S(2)}) async-start(), calls=%async_computation.9 | async-start | bytes 9732096 | tf_op jit(solution)/shard_map/all_gather | solution.py:89
  7.9 134.3 %all-gather.16.cloned.1.call-start = ((), (), s32[]{:S(2)}) async-start(), calls=%async_computation.12 | async-start | bytes 2621440 | tf_op jit(solution)/shard_map/all_gather | solution.py:94
  8.7 179.8 %all-gather.20.cloned.1.call-start = ((), (), s32[]{:S(2)}) async-start(), calls=%async_computation.14 | async-start | bytes 2621440 | tf_op jit(solution)/shard_map/all_gather | solution.py:95
  9.4 225.2 %all-gather.24.cloned.1.call-start = ((), (), s32[]{:S(2)}) async-start(), calls=%async_computation.16 | async-start | bytes 2621440 | tf_op jit(solution)/shard_map/all_gather | solution.py:96
  10.0 258.0 %all-gather.12.cloned.1.call-start = ((), (), s32[]{:S(2)}) async-start(), calls=%async_computation.10 | async-start | bytes 3538944 | tf_op jit(solution)/shard_map/all_gather | solution.py:188
  54.8 47.6 %copy-start.38 = (f32[2048]{0:T(1024)}, f32[2048]{0:T(1024)S(1)}, u32[]{:S(2)}) copy-start(f32[2048]{0:T(1024)S(1)} %convert_element_type.130) | copy-start | bytes 24580
  55.5 48.1 %copy-start.51 = (f32[64]{0:T(128)}, f32[64]{0:T(128)S(1)}, u32[]{:S(2)}) copy-start(f32[64]{0:T(128)S(1)} %convert_element_type.132) | copy-start | bytes 772
  57.0 192.0 %copy-start.28 = (f32[256,64]{0,1:T(8,128)}, f32[256,64]{0,1:T(8,128)S(1)}, u32[]{:S(2)}) copy-start(f32[256,64]{0,1:T(8,128)S(1)} %get-tuple-element.380) | copy-start | bytes 196612
  58.1 51.1 %copy-start.45 = (f32[384]{0:T(512)}, f32[384]{0:T(512)S(1)}, u32[]{:S(2)}) copy-start(f32[384]{0:T(512)S(1)} %mul.461) | copy-start | bytes 4612
  59.0 43.5 %copy-start.42 = (f32[256]{0:T(256)}, f32[256]{0:T(256)S(1)}, u32[]{:S(2)}) copy-start(f32[256]{0:T(256)S(1)} %get-tuple-element.386) | copy-start | bytes 3076
  102.5 141.3 %copy-start.12 = (f32[256,2304]{1,0:T(8,128)}, f32[256,2304]{1,0:T(8,128)S(1)}, u32[]{:S(2)}) copy-start(f32[256,2304]{1,0:T(8,128)S(1)} %fusion.58) | copy-start | bytes 7077892
  102.7 6.5 copy-start.18
  103.7 5.5 copy-start.24
  111.2 264.0 %all-gather.14.cloned.1.call-start = ((), (), s32[]{:S(2)}) async-start(), calls=%async_computation.11 | async-start | bytes 6488064 | tf_op jit(solution)/shard_map/all_gather | solution.py:90
  111.8 322.0 %all-gather.18.cloned.1.call-start = ((), (), s32[]{:S(2)}) async-start(), calls=%async_computation.13 | async-start | bytes 18874368 | tf_op jit(solution)/shard_map/all_gather | solution.py:201
  142.3 386.6 %all-gather.22.cloned.1.call-start = ((), (), s32[]{:S(2)}) async-start(), calls=%async_computation.15 | async-start | bytes 18874368 | tf_op jit(solution)/shard_map/all_gather | solution.py:202
  188.5 46.2 %copy-start.55 = (bf16[64]{0:T(256)(128)(2,1)S(1)}, bf16[64]{0:T(256)(128)(2,1)}, u32[]{:S(2)}) copy-start(bf16[64]{0:T(256)(128)(2,1)} %param.23) | copy-start | bytes 388
  188.5 46.2 %copy-start.53 = (s32[1,256]{1,0:T(1,128)S(1)}, s32[1,256]{1,0:T(1,128)}, u32[]{:S(2)}) copy-start(s32[1,256]{1,0:T(1,128)} %param.18) | copy-start | bytes 3076
  188.5 432.1 %all-gather.26.cloned.1.call-start = ((), (), s32[]{:S(2)}) async-start(), calls=%async_computation.17 | async-start | bytes 18874368 | tf_op jit(solution)/shard_map/all_gather | solution.py:203
  234.6 725.4 %reduce-scatter.16.cloned.1.call-start = ((), (), s32[]{:S(2)}) async-start(), calls=%async_computation.21 | async-start | bytes 18874368 | tf_op jit(solution)/shard_map/reduce_scatter | solution.py:223
  234.7 14.3 copy-start.48
  381.1 305.6 %copy-start.13 = (f32[256,2048]{1,0:T(8,128)}, f32[256,2048]{1,0:T(8,128)S(1)}, u32[]{:S(2)}) copy-start(f32[256,2048]{1,0:T(8,128)S(1)} %get-tuple-element.392) | copy-start | bytes 6291460
  644.1 316.5 %reduce-scatter.20.cloned.1.call-start = ((), (), s32[]{:S(2)}) async-start(), calls=%async_computation.23 | async-start | bytes 18874368 | tf_op jit(solution)/shard_map/reduce_scatter | solution.py:231
  656.4 342.9 %reduce-scatter.24.cloned.1.call-start = ((), (), s32[]{:S(2)}) async-start(), calls=%async_computation.25 | async-start | bytes 18874368 | tf_op jit(solution)/shard_map/reduce_scatter | solution.py:237
  672.9 13.9 copy-start.21
  709.4 339.5 %reduce-scatter.10.cloned.1.call-start = ((), (), s32[]{:S(2)}) async-start(), calls=%async_computation.18 | async-start | bytes 3538944 | tf_op jit(solution)/shard_map/reduce_scatter | solution.py:331
  733.8 5.7 copy-start.3
  793.8 5.5 copy-start.3
  824.5 5.5 copy-start.3
  884.8 5.5 copy-start.3
  946.2 5.5 copy-start.3
  960.0 175.2 %reduce-scatter.18.cloned.1.call-start = ((), (), s32[]{:S(2)}) async-start(), calls=%async_computation.22 | async-start | bytes 2621440 | tf_op jit(solution)/shard_map/reduce_scatter | solution.py:247
  960.5 180.5 %reduce-scatter.22.cloned.1.call-start = ((), (), s32[]{:S(2)}) async-start(), calls=%async_computation.24 | async-start | bytes 2621440 | tf_op jit(solution)/shard_map/reduce_scatter | solution.py:250
  960.6 38.7 %copy-start.7 = (f32[256,2048]{1,0:T(8,128)S(1)}, f32[256,2048]{1,0:T(8,128)}, u32[]{:S(2)}) copy-start(f32[256,2048]{1,0:T(8,128)} %copy-done.6) | copy-start | bytes 6291460
  960.6 38.7 %copy-start.23 = (bf16[256,6,4,64]{0,3,2,1:T(8,128)(2,1)S(1)}, bf16[256,6,4,64]{0,3,2,1:T(8,128)(2,1)}, u32[]{:S(2)}) copy-start(bf16[256,6,4,64]{0,3,2,1:T(8,128)(2,1)} %fusion.51) | copy-start | bytes 2359300
  961.1 225.4 %reduce-scatter.26.cloned.1.call-start = ((), (), s32[]{:S(2)}) async-start(), calls=%async_computation.26 | async-start | bytes 2621440 | tf_op jit(solution)/shard_map/reduce_scatter | solution.py:253
  999.3 348.4 %reduce-scatter.14.cloned.1.call-start = ((), (), s32[]{:S(2)}) async-start(), calls=%async_computation.20 | async-start | bytes 12976128 | tf_op jit(solution)/shard_map/reduce_scatter | solution.py:371
  1005.8 555.8 %reduce-scatter.12.cloned.1.call-start = ((), (), s32[]{:S(2)}) async-start(), calls=%async_computation.19 | async-start | bytes 19464192 | tf_op jit(solution)/shard_map/reduce_scatter | solution.py:370
  1022.8 27.9 %copy-start.32 = (f32[256,64]{0,1:T(8,128)S(1)}, f32[256,64]{0,1:T(8,128)}, u32[]{:S(2)}) copy-start(f32[256,64]{0,1:T(8,128)} %get-tuple-element.379) | copy-start | bytes 196612
  1029.3 21.6 %copy-start.19 = (f32[256,384]{0,1:T(8,128)S(1)}, f32[256,384]{0,1:T(8,128)}, u32[]{:S(2)}) copy-start(f32[256,384]{0,1:T(8,128)} %copy-done.18) | copy-start | bytes 1179652
  1029.3 21.6 %copy-start.29 = (f32[256,64]{0,1:T(8,128)S(1)}, f32[256,64]{0,1:T(8,128)}, u32[]{:S(2)}) copy-start(f32[256,64]{0,1:T(8,128)} %copy-done.28) | copy-start | bytes 196612
  1029.4 21.6 %copy-start.52 = (f32[64]{0:T(128)S(1)}, f32[64]{0:T(128)}, u32[]{:S(2)}) copy-start(f32[64]{0:T(128)} %copy-done.51) | copy-start | bytes 772
  1064.5 12.0 copy-start.47
  1064.5 12.8 copy-start.44
  1077.4 54.3 %copy-start.8 = (f32[256,2048]{1,0:T(8,128)S(1)}, f32[256,2048]{1,0:T(8,128)}, u32[]{:S(2)}) copy-start(f32[256,2048]{1,0:T(8,128)} %copy-done.6) | copy-start | bytes 6291460
  1077.4 54.3 %copy-start.50 = (f32[256]{0:T(256)S(1)}, f32[256]{0:T(256)}, u32[]{:S(2)}) copy-start(f32[256]{0:T(256)} %get-tuple-element.385) | copy-start | bytes 3076
  (48 other events, 129.4 us)
Sparse Core Ops, SparseCore 0:
  10.9 85.1 all-gather.9
  97.7 44.5 all-gather.15
  143.8 44.6 all-gather.19
  189.9 44.6 all-gather.23
  236.9 31.0 all-gather.11
  270.7 69.4 all-gather.13
  342.1 91.6 all-gather.17
  435.6 93.1 all-gather.21
  530.7 89.8 all-gather.25
  644.3 115.9 reduce-scatter.15
  763.8 115.9 reduce-scatter.19
  883.3 115.9 reduce-scatter.23
  1002.6 46.1 reduce-scatter.9
  1051.1 43.8 reduce-scatter.17
  1097.1 43.8 reduce-scatter.21
  1143.3 43.1 reduce-scatter.25
  1193.0 154.6 reduce-scatter.13
  1355.6 205.9 reduce-scatter.11
where the time goes:
time: 1580 us; the launch traced here: 1570 us
  waiting for transfers between devices  876 us (55%)
  matrix products  315 us (20%)
  local copies, waits for them, and re-layouts  148 us (9%)
  other arithmetic  101 us (6%)
  blocking collectives  94.9 us (6%)
  loops' own time  16.5 us (1%)
    reduce_scatter x1, waiting for transfers between devices, body(): lax.psum_scatter(qkv_wgrad, ('rows', 'seq'), scatter_dimension=0, tiled=T...  214 us
    reduce_scatter x1, waiting for transfers between devices, body(): lax.psum_scatter(out_wgrad, ('rows', 'seq'), scatter_dimension=1, tiled=T...  159 us
    unnamed x2, blocking collectives  86.1 us
    all_gather x1, waiting for transfers between devices, body(): lax.all_gather(up_slab, 'seq', axis=1, tiled=True)  84.7 us
    all_gather x1, waiting for transfers between devices, body(): lax.all_gather(down_slab, 'seq', axis=0, tiled=True)  80.9 us
    all_gather x1, waiting for transfers between devices, body(): lax.all_gather(gate_slab, 'seq', axis=1, tiled=True)  52.4 us
    all_gather x1, waiting for transfers between devices, body(): lax.all_gather(w_up, 'rows', axis=0, tiled=True)  46.2 us
    all_gather x1, waiting for transfers between devices, body(): lax.all_gather(w_down, 'rows', axis=1, tiled=True)  46 us
  transfers between devices with their start and end apart: 18, of which 14 were waited for; matrix products, arithmetic and copies ran while one was open for 34% of the time, Pallas kernels for 0%

commit v1 on v0

v1 whole, which is shorter than its diff:
```python
import functools
import math

import jax
import jax.numpy as jnp
from jax import lax
from jax.experimental import pallas as pl
from jax.experimental.pallas import tpu as pltpu
from jax.sharding import PartitionSpec as P

QUERY_HEADS = 24
KEY_VALUE_HEADS = 6
GROUP = QUERY_HEADS // KEY_VALUE_HEADS
D = 64
HALF = D // 2
EPSILON = 1e-06
THETA = 10000.0
PENALTY = -10000.0
SEGMENT_KINDS = 8
BLOCK = 512
F32 = jnp.float32
BF16 = jnp.bfloat16
VMEM_LIMIT = 56 * 1024 * 1024


def dot(a, b):
    return jnp.dot(a, b, preferred_element_type=F32)


def dot_nt(a, b):
    return lax.dot_general(a, b, (((1,), (1,)), ((), ())), preferred_element_type=F32)


def dot_tn(a, b):
    return lax.dot_general(a, b, (((0,), (0,)), ((), ())), preferred_element_type=F32)


def rotary_table(positions, segments):
    inverse = jnp.exp(-math.log(THETA) * jnp.arange(HALF, dtype=F32) * 2.0 / D)
    angles = inverse[:, None] * positions.astype(F32)[None, :]
    hot = jnp.arange(SEGMENT_KINDS, dtype=jnp.int32)[:, None] == segments[None, :]
    return jnp.concatenate([jnp.cos(angles), jnp.sin(angles), hot.astype(F32)], axis=0)


def split3(x):
    high = x.astype(BF16).astype(F32)
    mid = (x - high).astype(BF16).astype(F32)
    return high, mid, x - high - mid


def attention_forward_kernel(heads, proj_ref, table_ref, gq_ref, gk_ref,
                             merged_ref, o_ref, qa_ref, ka_ref, kt_ref, vt_ref, inv_ref):
    blocks, _, tok = table_ref.shape
    length = blocks * tok
    width = heads * D
    gq = gq_ref[...]
    gk = gk_ref[...]
    ones8 = jnp.ones((8, tok), F32)
    row8 = lax.broadcasted_iota(jnp.int32, (16, tok), 0)
    one_row = jnp.where(row8 == 0, 1.0, 0.0).astype(F32)

    def prepare(b, _):
        lanes = pl.ds(pl.multiple_of(b * tok, tok), tok)
        cos = table_ref[b, 0:HALF, :]
        sin = table_ref[b, HALF:D, :]
        hot = table_ref[b, D:D + 8, :]
        pen = (1.0 - hot) * PENALTY
        for h in range(heads):
            rawq = proj_ref[h * D:(h + 1) * D, lanes]
            rawk = proj_ref[width + h * D:width + (h + 1) * D, lanes]
            rawv = proj_ref[2 * width + h * D:2 * width + (h + 1) * D, lanes]

            def rotated(raw, gain):
                inv = lax.rsqrt(jnp.mean(raw * raw, axis=0, keepdims=True) + EPSILON)
                n = raw * inv * gain
                a, c = n[:HALF], n[HALF:]
                return inv, jnp.concatenate([a * cos - c * sin, c * cos + a * sin], axis=0)

            iq, q = rotated(rawq, gq)
            ik, k = rotated(rawk, gk)
            inv_ref[2 * h:2 * h + 1, lanes] = iq
            inv_ref[2 * h + 1:2 * h + 2, lanes] = ik
            q = (q * (D ** -0.5)).astype(BF16)
            kt_ref[h, :, lanes] = k.astype(BF16)
            extra = jnp.concatenate([pen, jnp.zeros((8, tok), F32)], axis=0).astype(BF16)
            qa_ref[h, :, lanes] = jnp.concatenate([q, extra], axis=0)
            full = jnp.concatenate([k, hot, ones8, jnp.zeros((48, tok), F32)], axis=0)
            ka_ref[h, lanes, :] = jnp.transpose(full).astype(BF16)
            vt_ref[h, :, lanes] = jnp.concatenate([rawv, one_row], axis=0).astype(BF16)
        return 0

    lax.fori_loop(0, blocks, prepare, 0)

    causal = (lax.broadcasted_iota(jnp.int32, (BLOCK, BLOCK), 0)
              <= lax.broadcasted_iota(jnp.int32, (BLOCK, BLOCK), 1))

    def query_block(i, _):
        cols = pl.ds(pl.multiple_of(i * BLOCK, BLOCK), BLOCK)

        def step(j, accs, diagonal):
            rows = pl.ds(pl.multiple_of(j * BLOCK, BLOCK), BLOCK)
            new = []
            for h in range(heads):
                s = dot(ka_ref[h, rows, 0:80], qa_ref[h, :, cols])
                p = jnp.exp(s)
                if diagonal:
                    p = jnp.where(causal, p, 0.0)
                new.append(accs[h] + dot(vt_ref[h, :, rows], p.astype(BF16)))
            return tuple(new)

        accs = tuple(jnp.zeros((80, BLOCK), F32) for _ in range(heads))
        accs = lax.fori_loop(0, i, lambda j, c: step(j, c, False), accs)
        accs = step(i, accs, True)
        outs = []
        for h in range(heads):
            total = accs[h][D:D + 1]
            o = accs[h][:D] * (1.0 / total)
            o_ref[h, :, cols] = o
            outs.append(o)
            pieces = split3(-jnp.log(total))
            old = qa_ref[h, 64:80, cols].astype(F32)
            row = lax.broadcasted_iota(jnp.int32, (16, BLOCK), 0)
            extra = jnp.where(row == 8, pieces[0],
                              jnp.where(row == 9, pieces[1], jnp.where(row == 10, pieces[2], old)))
            qa_ref[h, 64:80, cols] = extra.astype(BF16)
        merged_ref[cols, :] = jnp.transpose(jnp.concatenate(outs, axis=0)).astype(BF16)
        return 0

    lax.fori_loop(0, length // BLOCK, query_block, 0)


def attention_backward_kernel(heads, proj_ref, table_ref, gq_ref, gk_ref, dm_ref,
                              o_ref, qa_ref, ka_ref, kt_ref, vt_ref, inv_ref,
                              pg_ref, gains_ref, doa_ref, q_ref, va_ref, dq_ref, dk_ref, dv_ref):
    blocks, _, tok = table_ref.shape
    length = blocks * tok
    width = heads * D
    gq = gq_ref[...]
    gk = gk_ref[...]

    def prepare(b, _):
        lanes = pl.ds(pl.multiple_of(b * tok, tok), tok)
        dmt = jnp.transpose(dm_ref[lanes, :].astype(F32))
        row = lax.broadcasted_iota(jnp.int32, (16, tok), 0)
        for h in range(heads):
            do = dmt[h * D:(h + 1) * D]
            delta = jnp.sum(do * o_ref[h, :, lanes], axis=0, keepdims=True)
            pieces = split3(-delta)
            extra = jnp.where(row == 0, pieces[0],
                              jnp.where(row == 1, pieces[1], jnp.where(row == 2, pieces[2], 0.0)))
            doa_ref[h, :, lanes] = jnp.concatenate([do, extra], axis=0).astype(BF16)
            qk = jnp.concatenate([qa_ref[h, 0:D, lanes].astype(F32), vt_ref[h, 0:D, lanes].astype(F32)], axis=0)
            back = jnp.transpose(qk)
            q_ref[h, lanes, :] = back[:, :D].astype(BF16)
            va_ref[h, lanes, :] = jnp.concatenate(
                [back[:, D:], jnp.ones((tok, 16), F32)], axis=1).astype(BF16)
            dq_ref[h, :, lanes] = jnp.zeros((D, tok), F32)
        return 0

    lax.fori_loop(0, blocks, prepare, 0)

    causal = (lax.broadcasted_iota(jnp.int32, (BLOCK, BLOCK), 0)
              <= lax.broadcasted_iota(jnp.int32, (BLOCK, BLOCK), 1))
    count = length // BLOCK

    def key_block(j, _):
        rows = pl.ds(pl.multiple_of(j * BLOCK, BLOCK), BLOCK)

        def step(i, accs, diagonal):
            cols = pl.ds(pl.multiple_of(i * BLOCK, BLOCK), BLOCK)
            new = []
            for h in range(heads):
                p = jnp.exp(dot(ka_ref[h, rows, 0:80], qa_ref[h, :, cols]))
                if diagonal:
                    p = jnp.where(causal, p, 0.0)
                dp = dot(va_ref[h, rows, :], doa_ref[h, :, cols])
                ds = (p * dp).astype(BF16)
                do = dm_ref[cols, h * D:(h + 1) * D]
                dv = accs[2 * h] + dot(p.astype(BF16), do)
                dk = accs[2 * h + 1] + dot(ds, q_ref[h, cols, :])
                dq_ref[h, :, cols] += dot(kt_ref[h, :, rows], ds)
                new += [dv, dk]
            return tuple(new)

        accs = tuple(jnp.zeros((BLOCK, D), F32) for _ in range(2 * heads))
        accs = step(j, accs, True)
        accs = lax.fori_loop(j + 1, count, lambda i, c: step(i, c, False), accs)
        for h in range(heads):
            both = jnp.transpose(jnp.concatenate([accs[2 * h], accs[2 * h + 1]], axis=1))
            dv_ref[h, :, rows] = both[:D]
            dk_ref[h, :, rows] = both[D:]
        return 0

    lax.fori_loop(0, count, key_block, 0)

    def finish(b, sums):
        lanes = pl.ds(pl.multiple_of(b * tok, tok), tok)
        cos = table_ref[b, 0:HALF, :]
        sin = table_ref[b, HALF:D, :]

        def back(grad, raw, inv, gain):
            a, c = grad[:HALF], grad[HALF:]
            n = jnp.concatenate([a * cos + c * sin, c * cos - a * sin], axis=0)
            v = n * gain
            out = inv * v - raw * (inv * inv * inv) * jnp.mean(v * raw, axis=0, keepdims=True)
            return out, n * raw * inv

        sum_q, sum_k = sums
        for h in range(heads):
            rawq = proj_ref[h * D:(h + 1) * D, lanes]
            rawk = proj_ref[width + h * D:width + (h + 1) * D, lanes]
            out_q, part_q = back(dq_ref[h, :, lanes] * (D ** -0.5), rawq, inv_ref[2 * h:2 * h + 1, lanes], gq)
            out_k, part_k = back(dk_ref[h, :, lanes], rawk, inv_ref[2 * h + 1:2 * h + 2, lanes], gk)
            pg_ref[h * D:(h + 1) * D, lanes] = out_q.astype(BF16)
            pg_ref[width + h * D:width + (h + 1) * D, lanes] = out_k.astype(BF16)
            pg_ref[2 * width + h * D:2 * width + (h + 1) * D, lanes] = dv_ref[h, :, lanes].astype(BF16)
            sum_q = sum_q + part_q
            sum_k = sum_k + part_k
        return sum_q, sum_k

    zero = jnp.zeros((D, tok), F32)
    sum_q, sum_k = lax.fori_loop(0, blocks, finish, (zero, zero))
    total = jnp.concatenate([jnp.sum(sum_q, axis=1, keepdims=True), jnp.sum(sum_k, axis=1, keepdims=True)], axis=0)
    gains_ref[...] = jnp.broadcast_to(total, gains_ref.shape)


def attention_forward(heads, proj, table, gq, gk):
    length = proj.shape[1]
    return pl.pallas_call(
        functools.partial(attention_forward_kernel, heads),
        out_shape=(
            jax.ShapeDtypeStruct((length, heads * D), BF16),
            jax.ShapeDtypeStruct((heads, D, length), F32),
            jax.ShapeDtypeStruct((heads, 80, length), BF16),
            jax.ShapeDtypeStruct((heads, length, 128), BF16),
            jax.ShapeDtypeStruct((heads, D, length), BF16),
            jax.ShapeDtypeStruct((heads, 80, length), BF16),
            jax.ShapeDtypeStruct((8, length), F32),
        ),
        compiler_params=pltpu.CompilerParams(vmem_limit_bytes=VMEM_LIMIT),
        cost_estimate=pl.CostEstimate(flops=4 * heads * 64 * length * length, bytes_accessed=16 << 20, transcendentals=heads * length * length // 2),
    )(proj, table, gq, gk)


def attention_backward(heads, proj, table, gq, gk, dm, kept):
    length = proj.shape[1]
    return pl.pallas_call(
        functools.partial(attention_backward_kernel, heads),
        out_shape=(
            jax.ShapeDtypeStruct((3 * heads * D, length), BF16),
            jax.ShapeDtypeStruct((2 * D, 128), F32),
        ),
        scratch_shapes=[
            pltpu.VMEM((heads, 80, length), BF16),
            pltpu.VMEM((heads, length, D), BF16),
            pltpu.VMEM((heads, length, 80), BF16),
            pltpu.VMEM((heads, D, length), F32),
            pltpu.VMEM((heads, D, length), F32),
            pltpu.VMEM((heads, D, length), F32),
        ],
        compiler_params=pltpu.CompilerParams(vmem_limit_bytes=VMEM_LIMIT),
        cost_estimate=pl.CostEstimate(flops=10 * heads * 64 * length * length, bytes_accessed=16 << 20, transcendentals=heads * length * length // 2),
    )(proj, table, gq, gk, dm, *kept)


def norm_inverse(x):
    return lax.rsqrt(jnp.mean(x * x, axis=-1, keepdims=True) + EPSILON)


def norm_back(grad_normed, values_in, inv_rms, gain):
    scaled = grad_normed * gain
    gain_grad = jnp.sum(grad_normed * values_in * inv_rms, axis=0)
    input_grad = inv_rms * scaled - values_in * inv_rms**3 * jnp.mean(scaled * values_in, axis=-1, keepdims=True)
    return input_grad, gain_grad


def body(tokens, segments, positions, cotangent, gain_attn, w_qkv, gain_q, gain_k, w_out, gain_ffn, w_gate, w_up, w_down):
    seq = lax.axis_size("seq")
    rows = lax.axis_size("rows")
    heads = -(-QUERY_HEADS // seq)
    padded = seq * heads
    depth = w_qkv.shape[0]
    width = heads * D
    tok = tokens.shape[1]

    def spread(columns):
        return jnp.repeat(columns.reshape(depth, KEY_VALUE_HEADS, D), GROUP, axis=1)

    def slabs(columns):
        columns = columns.reshape(depth, QUERY_HEADS, D)
        columns = jnp.pad(columns, ((0, 0), (0, padded - QUERY_HEADS), (0, 0)))
        return columns.reshape(depth, seq, width)

    qw, kw = QUERY_HEADS * D, KEY_VALUE_HEADS * D
    local = jnp.concatenate([
        slabs(w_qkv[:, :qw]),
        slabs(spread(w_qkv[:, qw:qw + kw])),
        slabs(spread(w_qkv[:, qw + kw:])),
        slabs(w_out.T),
    ], axis=2).transpose(1, 0, 2)
    mine = lax.all_to_all(local, "seq", 0, 0, tiled=False)
    attn_w = lax.all_gather(mine.reshape(seq * depth, 4 * width), "rows", axis=0, tiled=True)
    qkv_slab, out_slab = attn_w[:, :3 * width], attn_w[:, 3 * width:]

    gains = lax.all_gather(jnp.stack([gain_attn, gain_ffn])[:, None], ("rows", "seq"), axis=1, tiled=True)
    gain_one = gains[0].reshape(1, -1).astype(F32)
    gain_two = gains[1].reshape(1, -1).astype(F32)
    gate_slab = lax.all_gather(w_gate, "rows", axis=0, tiled=True)
    up_slab = lax.all_gather(w_up, "rows", axis=0, tiled=True)
    down_slab = lax.all_gather(w_down, "rows", axis=1, tiled=True)
    gq = gain_q.astype(F32)[:, None]
    gk = gain_k.astype(F32)[:, None]

    x = tokens[0].astype(F32)
    inv_one = norm_inverse(x)
    normed = (x * inv_one * gain_one).astype(BF16)
    table = lax.all_gather(rotary_table(positions[0], segments[0]), "seq", axis=0, tiled=False)
    normed_all = lax.all_gather(normed, "seq", axis=0, tiled=True)
    proj = lax.dot_general(qkv_slab, normed_all, (((0,), (1,)), ((), ())), preferred_element_type=F32)
    merged, *kept = attention_forward(heads, proj, table, gq, gk)
    out_part = dot_nt(merged, out_slab).astype(BF16)
    residual = x + lax.psum_scatter(out_part, "seq", scatter_dimension=0, tiled=True).astype(F32)
    inv_two = norm_inverse(residual)
    normed_two = (residual * inv_two * gain_two).astype(BF16)
    two_all = lax.all_gather(normed_two, "seq", axis=0, tiled=True)
    g_all = lax.all_gather(cotangent[0], "seq", axis=0, tiled=True)

    gate_act = dot(two_all, gate_slab)
    up_act = dot(two_all, up_slab)
    s = jax.nn.sigmoid(gate_act)
    hidden = (gate_act * s * up_act).astype(BF16)
    hidden_grad = dot_nt(g_all, down_slab)
    gate_grad = (hidden_grad * up_act * s * (1.0 + gate_act * (1.0 - s))).astype(BF16)
    up_grad = (hidden_grad * gate_act * s).astype(BF16)
    two_grad_part = (dot_nt(gate_grad, gate_slab) + dot_nt(up_grad, up_slab)).astype(BF16)
    two_grad = lax.psum_scatter(two_grad_part, "seq", scatter_dimension=0, tiled=True).astype(F32)
    branch_part = dot(hidden, down_slab).astype(BF16)
    branch = lax.psum_scatter(branch_part, "seq", scatter_dimension=0, tiled=True).astype(F32)
    layer_out = (residual + branch).astype(BF16)
    grad_gate = lax.psum_scatter(dot_tn(two_all, gate_grad).astype(BF16), "rows", scatter_dimension=0, tiled=True).astype(F32)
    grad_up = lax.psum_scatter(dot_tn(two_all, up_grad).astype(BF16), "rows", scatter_dimension=0, tiled=True).astype(F32)
    grad_down = lax.psum_scatter(dot_tn(hidden, g_all).astype(BF16), "rows", scatter_dimension=1, tiled=True).astype(F32)

    norm_grad, gain_two_grad = norm_back(two_grad, residual, inv_two, gain_two)
    residual_grad = cotangent[0].astype(F32) + norm_grad
    branch_all = lax.all_gather(residual_grad.astype(BF16), "seq", axis=0, tiled=True)
    dm = dot(branch_all, out_slab).astype(BF16)
    pg, head_gains = attention_backward(heads, proj, table, gq, gk, dm, kept)
    normed_part = lax.dot_general(pg, qkv_slab, (((0,), (1,)), ((), ())), preferred_element_type=F32).astype(BF16)
    normed_grad = lax.psum_scatter(normed_part, "seq", scatter_dimension=0, tiled=True).astype(F32)
    input_norm_grad, gain_one_grad = norm_back(normed_grad, x, inv_one, gain_one)
    grad_tokens = residual_grad + input_norm_grad

    qkv_wgrad = lax.dot_general(normed_all, pg, (((0,), (1,)), ((), ())), preferred_element_type=F32)
    out_wgrad = dot_tn(branch_all, merged)
    attn_grad = jnp.concatenate([qkv_wgrad, out_wgrad], axis=1).astype(BF16)
    attn_grad = lax.psum_scatter(attn_grad, "rows", scatter_dimension=0, tiled=True)
    attn_grad = lax.all_to_all(attn_grad.reshape(seq, depth, 4 * width), "seq", 0, 0, tiled=False).astype(F32)

    def unslab(part):
        part = attn_grad[:, :, part * width:(part + 1) * width].transpose(1, 0, 2)
        return part.reshape(depth, padded, D)[:, :QUERY_HEADS]

    def unspread(part):
        return jnp.sum(unslab(part).reshape(depth, KEY_VALUE_HEADS, GROUP, D), axis=2).reshape(depth, kw)

    grad_qkv = jnp.concatenate([unslab(0).reshape(depth, qw), unspread(1), unspread(2)], axis=1)
    grad_out = unslab(3).reshape(depth, qw).T

    small = lax.psum(jnp.concatenate([gain_one_grad, gain_two_grad, head_gains[:, 0]]), ("rows", "seq"))
    model = gain_one_grad.shape[0]
    start = (lax.axis_index("rows") * seq + lax.axis_index("seq")) * depth
    return (
        layer_out[None],
        grad_tokens[None],
        lax.dynamic_slice_in_dim(small, start, depth),
        grad_qkv,
        small[2 * model:2 * model + D],
        small[2 * model + D:],
        grad_out,
        lax.dynamic_slice_in_dim(small, model + start, depth),
        grad_gate,
        grad_up,
        grad_down,
    )


def solution(mesh):
    both = ("rows", "seq")
    return jax.shard_map(
        body,
        mesh=mesh,
        in_specs=(
            P("rows", "seq", None), P("rows", "seq"), P("rows", "seq"), P("rows", "seq", None),
            P(both), P(both, None), P(), P(), P(None, both), P(both),
            P("rows", "seq"), P("rows", "seq"), P("seq", "rows"),
        ),
        out_specs=(
            P("rows", "seq", None), P("rows", "seq", None), P(both), P(both, None), P(), P(),
            P(None, both), P(both), P("rows", "seq"), P("rows", "seq"), P("seq", "rows"),
        ),
        check_vma=False,
    )
```

time: 1580 us -> 1100 us (0.70)
  waiting for transfers between devices: 876 us -> 703 us
  matrix products: 315 us -> 146 us
  local copies, waits for them, and re-layouts: 148 us -> 29.5 us
  other arithmetic: 101 us -> 32.4 us
  Pallas kernels: 0 us -> 52.3 us
  loops' own time: 16.5 us -> 0 us
    dot_general x71 -> x15, matrix products: 315 us -> 146 us  [the longest x4 41.6 us: dot_nt(): lax.dot_general(a, b, (((1,), (1,)), ((), ())), preferred_element_type=F32)]
    reduce_scatter x9 -> x8, waiting for transfers between devices: 478 us -> 356 us  [the longest x1 71.4 us: body(): lax.psum_scatter(two_grad_part, 'seq', scatter_dimension=0, tiled=True)]
    unnamed x2 -> x0, blocking collectives: 86.1 us -> none
    pallas_call x0 -> x2, Pallas kernels: none -> 52.3 us  [the longest x1 34.1 us: attention_backward(): pl.pallas_call(functools.partial(attention_backward_kernel, heads), out_s...]
    all_gather x9 -> x8, waiting for transfers between devices: 395 us -> 344 us  [the longest x1 55.6 us: body(): two_all = lax.all_gather(normed_two, 'seq', axis=0, tiled=True)]
    dynamic_update_slice x16 -> x0, local copies, waits for them, and re-layouts: 44 us -> none  [backward_one_block(): lax.dynamic_update_slice_in_dim(key_value_gradient, current + fresh_rows,...]
    all_gather x1 -> x2, blocking collectives: 8.86 us -> 50.3 us  [the longest x1 40.1 us: body(): lax.all_gather(jnp.stack([gain_attn, gain_ffn])[:, None], ('rows', 'seq')...]
    psum x0 -> x1, blocking collectives: none -> 40 us  [body(): lax.psum(jnp.concatenate([gain_one_grad, gain_two_grad, head_gains[:, 0]]...]
  transfers between devices with their start and end apart: 18 -> 17, of which waited for: 14 -> 16; matrix products, arithmetic and copies ran while one was open for 34% -> 11% of each run, Pallas kernels for 0% -> 0%
where the time goes in v1:
time: 1100 us; the launch traced here: 1090 us
  waiting for transfers between devices  703 us (64%)
  matrix products  146 us (13%)
  blocking collectives  108 us (10%)
  Pallas kernels  52.3 us (5%)
  other arithmetic  32.4 us (3%)
  local copies, waits for them, and re-layouts  29.5 us (3%)
  between operations  14.6 us (1%)
    reduce_scatter x1, waiting for transfers between devices, body(): lax.psum_scatter(two_grad_part, 'seq', scatter_dimension=0, tiled=True)  71.4 us
    reduce_scatter x1, waiting for transfers between devices, body(): lax.psum_scatter(out_part, 'seq', scatter_dimension=0, tiled=True)  70.8 us
    all_gather x1, waiting for transfers between devices, body(): two_all = lax.all_gather(normed_two, 'seq', axis=0, tiled=True)  55.6 us
    all_gather x1, waiting for transfers between devices, body(): normed_all = lax.all_gather(normed, 'seq', axis=0, tiled=True)  55.4 us
    all_gather x1, waiting for transfers between devices, body(): g_all = lax.all_gather(cotangent[0], 'seq', axis=0, tiled=True)  55.2 us
    all_gather x1, waiting for transfers between devices, body(): lax.all_gather(residual_grad.astype(BF16), 'seq', axis=0, tiled=True)  54.3 us
    reduce_scatter x1, waiting for transfers between devices, body(): lax.psum_scatter(normed_part, 'seq', scatter_dimension=0, tiled=True)  46.4 us
    reduce_scatter x1, waiting for transfers between devices, body(): lax.psum_scatter(dot_tn(two_all, gate_grad).astype(BF16), 'rows', scatter...  43.8 us
  transfers between devices with their start and end apart: 17, of which 16 were waited for; matrix products, arithmetic and copies ran while one was open for 11% of the time, Pallas kernels for 0%

profile of v1, /device:TPU:0, one launch (start us, length us, event | category | flops | bytes accessed | tf_op | source)
XLA Modules:
  0.0 1091.4 jit_solution(10372790518394728032)
XLA Ops:
  11.3 17.8 %all_to_all.10 = bf16[8,64,768]{2,1,0:T(8,128)(2,1)} all-to-all(bf16[8,64,768]{2,1,0:T(8,128)(2,1)S(1)} %copy.64), channel_id=1, replica_groups=mesh['rows'=4,'seq'=8] {'seq'}, dimensions={0} | all-to-all | bytes 1572864 | tf_op jit(solution)/shard_map/all_to_all | solution.py:301
  29.2 40.1 %all-gather.3 = bf16[32,64,2]{1,2,0:T(2,128)(2,1)S(1)} all-gather(bf16[1,64,2]{1,2,0:T(2,128)(2,1)S(1)} %maximum_bitcast_fusion.1), channel_id=2, replica_groups=mesh['rows'=4,'seq'=8] {'rows','seq'}, dimensions={0}, use_global_device_ids=true | all-gather | bytes 8448 | tf_op jit(solution)/shard_map/all_gather | solution.py:305
  73.3 10.2 all-gather.1
  83.6 8.6 all-gather.13.cloned.1.call-done
  92.2 55.4 %all-gather.15.cloned.1.call-done = bf16[2048,2048]{1,0:T(8,128)(2,1)} async-done(((bf16[256,2048]{1,0:T(8,128)(2,1)}), bf16[2048,2048]{1,0:T(8,128)(2,1)}) %all-gather.15.cloned.1.call-update) | async-done | bytes 8388624 | tf_op jit(solution)/shard_map/all_gather | solution.py:318
  147.6 10.6 fusion.11.proj_ref
  158.2 18.2 %shard_map.212 = (bf16[2048,192]{1,0:T(8,128)(2,1)}, f32[3,64,2048]{2,1,0:T(8,128)}, bf16[3,80,2048]{2,1,0:T(8,128)(2,1)}, bf16[3,2048,128]{2,1,0:T(8,128)(2,1)}...) custom-call(f32[576,2048]{1,0:T(8,128)} %fusion.11.proj_ref, ...), custom_call_target="tpu_custom_call" | custom-call | flops 3221225472 | bytes 16777216 | tf_op jit(solution)/shard_map/pallas_call | solution.py:229
  176.3 7.3 convolution_convert_fusion.2
  184.3 70.8 %reduce-scatter.9.cloned.1.call-done = bf16[256,2048]{1,0:T(8,128)(2,1)} async-done(((bf16[2048,2048]{1,0:T(8,128)(2,1)}), bf16[256,2048]{1,0:T(8,128)(2,1)}) %reduce-scatter.9.cloned.1.call-update) | async-done | bytes 1048592 | tf_op jit(solution)/shard_map/reduce_scatter | solution.py:322
  260.7 41.8 %all-gather.21.cloned.1.call-done = bf16[2048,512]{1,0:T(8,128)(2,1)} async-done(((bf16[512,512]{1,0:T(8,128)(2,1)}), bf16[2048,512]{1,0:T(8,128)(2,1)}) %all-gather.21.cloned.1.call-update) | async-done | bytes 2097168 | tf_op jit(solution)/shard_map/all_gather | solution.py:309
  302.5 55.6 %all-gather.17.cloned.1.call-done = bf16[2048,2048]{1,0:T(8,128)(2,1)} async-done(((bf16[256,2048]{1,0:T(8,128)(2,1)}), bf16[2048,2048]{1,0:T(8,128)(2,1)}) %all-gather.17.cloned.1.call-update) | async-done | bytes 8388624 | tf_op jit(solution)/shard_map/all_gather | solution.py:325
  358.2 10.5 fusion.36
  368.6 37.0 %all-gather.19.cloned.1.call-done = bf16[2048,512]{1,0:T(8,128)(2,1)} async-done(((bf16[512,512]{1,0:T(8,128)(2,1)}), bf16[2048,512]{1,0:T(8,128)(2,1)}) %all-gather.19.cloned.1.call-update) | async-done | bytes 2097168 | tf_op jit(solution)/shard_map/all_gather | solution.py:308
  405.6 10.5 fusion.35
  416.1 35.9 %all-gather.23.cloned.1.call-done = bf16[512,2048]{1,0:T(8,128)(2,1)} async-done(((bf16[512,512]{1,0:T(8,128)(2,1)}), bf16[512,2048]{1,0:T(8,128)(2,1)}) %all-gather.23.cloned.1.call-update) | async-done | bytes 2097168 | tf_op jit(solution)/shard_map/all_gather | solution.py:310
  452.0 55.2 %all-gather.27.cloned.1.call-done = bf16[1,2048,2048]{2,1,0:T(8,128)(2,1)} async-done(((bf16[1,256,2048]{2,1,0:T(8,128)(2,1)}), bf16[1,2048,2048]{2,1,0:T(8,128)(2,1)}) %all-gather.27.cloned.1.call-update) | async-done | bytes 8388624 | tf_op jit(solution)/shard_map/all_gather | solution.py:326
  507.1 15.4 %multiply_convert_fusion = (bf16[2048,512]{1,0:T(8,128)(2,1)}, bf16[2048,512]{1,0:T(8,128)(2,1)S(1)}, bf16[2048,512]{1,0:T(8,128)(2,1)}) fusion(f32[2048,512]{1,0:T(8,128)} %fusion.35, f32[2048,512]{1,0:T(8,128)} %fusion.36, bf16[512,2048]{1,0:T(8,128)(2,1)} %all-gather.23.cloned.1.call-done, bf16[1,2048,2048]{2,1,0:T(8,128)(2,1)} %all-gather.27.cloned.1.call-done), kind=kOutput, calls=%fused_computation.14 | convolution fusion | flops 4311744512 | bytes 25165824 | tf_op jit(solution)/shard_map/dot_general | solution.py:31
  522.6 8.1 fusion.37
  530.7 10.8 add_convert_fusion
  541.6 71.4 %reduce-scatter.13.cloned.1.call-done = bf16[256,2048]{1,0:T(8,128)(2,1)} async-done(((bf16[2048,2048]{1,0:T(8,128)(2,1)}), bf16[256,2048]{1,0:T(8,128)(2,1)}) %reduce-scatter.13.cloned.1.call-update) | async-done | bytes 1048592 | tf_op jit(solution)/shard_map/reduce_scatter | solution.py:336
  613.0 2.6 fusion.20
  617.8 54.3 %all-gather.25.cloned.1.call-done = bf16[2048,2048]{1,0:T(8,128)(2,1)} async-done(((bf16[256,2048]{1,0:T(8,128)(2,1)}), bf16[2048,2048]{1,0:T(8,128)(2,1)}) %all-gather.25.cloned.1.call-update) | async-done | bytes 8388624 | tf_op jit(solution)/shard_map/all_gather | solution.py:346
  672.1 7.5 convolution_convert_fusion.7
  679.6 2.2 copy.70.dm_ref
  681.8 34.1 %shard_map.213 = (bf16[576,2048]{1,0:T(8,128)(2,1)}, f32[128,128]{1,0:T(8,128)}) custom-call(f32[576,2048]{1,0:T(8,128)} %fusion.11.proj_ref, f32[8,72,256]{2,1,0:T(8,128)} %bitcast.98, f32[64,1]{1,0:T(8,128)} %copy.66.gq_ref, f32[64,1]{1,0:T(8,128)} %copy.67.gk_ref, bf16[2048,192]{1,0:T(8,128)(2,1)} %copy.70.dm_ref, ...), custom_call_target="tpu_custom_call" | custom-call | flops 8053063680 | bytes 16777216 | tf_op jit(solution)/shard_map/pallas_call | solution.py:247
  715.9 5.4 convolution_convert_fusion.6
  721.3 8.6 convolution_convert_fusion.3
  732.2 9.9 fusion.4
  742.1 9.9 convolution_convert_fusion.4
  752.5 9.9 convolution_convert_fusion.5
  762.5 11.2 %convolution_convert_fusion = bf16[2048,2048]{1,0:T(8,128)(2,1)} fusion(bf16[576,2048]{1,0:T(8,128)(2,1)} %get-tuple-element.27, bf16[2048,768]{1,0:T(8,128)(2,1)} %all-gather.13.cloned.1.call-done), kind=kOutput, calls=%fused_computation.5 | convolution fusion | flops 4836032512 | bytes 13369344 | tf_op jit(solution)/shard_map/dot_general | solution.py:349
  774.0 10.0 convolution_convert_fusion.1
  784.0 8.3 reduce-scatter.17.cloned.1.call-done
  792.3 2.3 copy.71
  794.6 4.2 all-to-all-start.1
  798.8 39.5 %reduce-scatter.23.cloned.1.call-done = bf16[512,512]{1,0:T(8,128)(2,1)} async-done(((bf16[512,2048]{1,0:T(8,128)(2,1)}), bf16[512,512]{1,0:T(8,128)(2,1)}) %reduce-scatter.23.cloned.1.call-update) | async-done | bytes 524304 | tf_op jit(solution)/shard_map/reduce_scatter | solution.py:342
  840.5 43.5 %reduce-scatter.21.cloned.1.call-done = bf16[512,512]{1,0:T(8,128)(2,1)} async-done(((bf16[2048,512]{1,0:T(8,128)(2,1)}), bf16[512,512]{1,0:T(8,128)(2,1)}) %reduce-scatter.21.cloned.1.call-update) | async-done | bytes 524304 | tf_op jit(solution)/shard_map/reduce_scatter | solution.py:341
  884.0 2.1 convert_element_type.139
  886.1 43.8 %reduce-scatter.19.cloned.1.call-done = bf16[512,512]{1,0:T(8,128)(2,1)} async-done(((bf16[2048,512]{1,0:T(8,128)(2,1)}), bf16[512,512]{1,0:T(8,128)(2,1)}) %reduce-scatter.19.cloned.1.call-update) | async-done | bytes 524304 | tf_op jit(solution)/shard_map/reduce_scatter | solution.py:340
  929.9 2.1 convert_element_type.137
  938.5 2.2 copy.74
  940.7 2.5 reshape_reshape.14
  945.7 2.2 copy.73
  947.9 2.3 reshape_reshape.13
  957.8 46.4 %reduce-scatter.15.cloned.1.call-done = bf16[256,2048]{1,0:T(8,128)(2,1)} async-done(((bf16[2048,2048]{1,0:T(8,128)(2,1)}), bf16[256,2048]{1,0:T(8,128)(2,1)}) %reduce-scatter.15.cloned.1.call-update) | async-done | bytes 1048592 | tf_op jit(solution)/shard_map/reduce_scatter | solution.py:350
  1006.2 40.0 %psum.7 = f32[4224]{0:T(1024)S(1)} all-reduce(f32[4224]{0:T(1024)S(1)} %pad_maximum_fusion.3), channel_id=1, replica_groups=mesh['rows'=4,'seq'=8] {'rows','seq'}, use_global_device_ids=true, to_apply=%region_10.11 | all-reduce | flops 4224 | bytes 33792 | tf_op jit(solution)/shard_map/psum | solution.py:370
  1046.8 32.7 %reduce-scatter.11.cloned.1.call-done = bf16[256,2048]{1,0:T(8,128)(2,1)} async-done(((bf16[2048,2048]{1,0:T(8,128)(2,1)}), bf16[256,2048]{1,0:T(8,128)(2,1)}) %reduce-scatter.11.cloned.1.call-update) | async-done | bytes 1048592 | tf_op jit(solution)/shard_map/reduce_scatter | solution.py:338
  1079.5 5.1 fusion.15
  (144 shorter events, 40.6 us)
Async XLA Ops:
  7.2 3.4 copy-start.5
  7.2 85.0 %all-gather.13.cloned.1.call-start = ((), (), s32[]{:S(2)}) async-start(), calls=%async_computation.10 | async-start | bytes 3932160 | tf_op jit(solution)/shard_map/all_gather | solution.py:302
  11.1 18.0 %copy-start.24 = (bf16[64]{0:T(256)(128)(2,1)S(1)}, bf16[64]{0:T(256)(128)(2,1)}, u32[]{:S(2)}) copy-start(bf16[64]{0:T(256)(128)(2,1)} %param.22) | copy-start | bytes 388
  11.1 18.0 %copy-start.25 = (bf16[64]{0:T(256)(128)(2,1)S(1)}, bf16[64]{0:T(256)(128)(2,1)}, u32[]{:S(2)}) copy-start(bf16[64]{0:T(256)(128)(2,1)} %param.17) | copy-start | bytes 388
  11.1 58.2 %copy-start = (bf16[1,256,2048]{2,1,0:T(8,128)(2,1)S(1)}, bf16[1,256,2048]{2,1,0:T(8,128)(2,1)}, u32[]{:S(2)}) copy-start(bf16[1,256,2048]{2,1,0:T(8,128)(2,1)} %param.13) | copy-start | bytes 3145732
  29.1 118.5 %all-gather.15.cloned.1.call-start = ((), (), s32[]{:S(2)}) async-start(), calls=%async_computation.11 | async-start | bytes 9437184 | tf_op jit(solution)/shard_map/all_gather | solution.py:318
  69.3 2.3 copy-start.21
  69.3 2.3 copy-start.26
  69.3 3.0 copy-start.27
  69.3 3.7 copy-start.20
  70.2 3.0 copy-start.12
  70.3 3.0 copy-start.6
  71.6 183.5 %reduce-scatter.9.cloned.1.call-start = ((), (), s32[]{:S(2)}) async-start(), calls=%async_computation.12 | async-start | bytes 9437184 | tf_op jit(solution)/shard_map/reduce_scatter | solution.py:322
  183.6 118.9 %all-gather.21.cloned.1.call-start = ((), (), s32[]{:S(2)}) async-start(), calls=%async_computation.15 | async-start | bytes 2621440 | tf_op jit(solution)/shard_map/all_gather | solution.py:309
  184.2 173.9 %all-gather.17.cloned.1.call-start = ((), (), s32[]{:S(2)}) async-start(), calls=%async_computation.13 | async-start | bytes 9437184 | tf_op jit(solution)/shard_map/all_gather | solution.py:325
  255.1 1.8 copy-start.1
  256.8 358.8 %copy-start.10 = (f32[256]{0:T(256)}, f32[256]{0:T(256)S(1)}, u32[]{:S(2)}) copy-start(f32[256]{0:T(256)S(1)} %get-tuple-element.55) | copy-start | bytes 3076
  256.8 358.8 %copy-start.14 = (f32[256]{0:T(256)}, f32[256]{0:T(256)S(1)}, u32[]{:S(2)}) copy-start(f32[256]{0:T(256)S(1)} %get-tuple-element.54) | copy-start | bytes 3076
  258.4 147.2 %all-gather.19.cloned.1.call-start = ((), (), s32[]{:S(2)}) async-start(), calls=%async_computation.14 | async-start | bytes 2621440 | tf_op jit(solution)/shard_map/all_gather | solution.py:308
  259.0 193.0 %all-gather.23.cloned.1.call-start = ((), (), s32[]{:S(2)}) async-start(), calls=%async_computation.16 | async-start | bytes 2621440 | tf_op jit(solution)/shard_map/all_gather | solution.py:310
  259.7 247.4 %all-gather.27.cloned.1.call-start = ((), (), s32[]{:S(2)}) async-start(), calls=%async_computation.25 | async-start | bytes 9437184 | tf_op jit(solution)/shard_map/all_gather | solution.py:326
  260.5 352.5 %reduce-scatter.13.cloned.1.call-start = ((), (), s32[]{:S(2)}) async-start(), calls=%async_computation.18 | async-start | bytes 9437184 | tf_op jit(solution)/shard_map/reduce_scatter | solution.py:336
  507.1 15.4 %copy-start.23 = (bf16[2048,512]{1,0:T(8,128)(2,1)S(1)}, bf16[2048,512]{1,0:T(8,128)(2,1)}, u32[]{:S(2)}) copy-start(bf16[2048,512]{1,0:T(8,128)(2,1)} %all-gather.19.cloned.1.call-done) | copy-start | bytes 6291460
  522.6 8.1 copy-start.28
  522.6 8.1 copy-start.22
  541.5 74.1 %copy-start.2 = (bf16[1,256,2048]{2,1,0:T(8,128)(2,1)S(1)}, bf16[1,256,2048]{2,1,0:T(8,128)(2,1)}, u32[]{:S(2)}) copy-start(bf16[1,256,2048]{2,1,0:T(8,128)(2,1)} %param.16) | copy-start | bytes 3145732
  541.6 130.5 %all-gather.25.cloned.1.call-start = ((), (), s32[]{:S(2)}) async-start(), calls=%async_computation.19 | async-start | bytes 9437184 | tf_op jit(solution)/shard_map/all_gather | solution.py:346
  613.0 2.7 copy-start.3
  615.6 1.9 copy-start.16
  617.5 174.8 %reduce-scatter.17.cloned.1.call-start = ((), (), s32[]{:S(2)}) async-start(), calls=%async_computation.21 | async-start | bytes 3932160 | tf_op jit(solution)/shard_map/reduce_scatter | solution.py:357
  681.8 34.1 %copy-start.4 = (bf16[2048,192]{1,0:T(8,128)(2,1)S(1)}, bf16[2048,192]{1,0:T(8,128)(2,1)}, u32[]{:S(2)}) copy-start(bf16[2048,192]{1,0:T(8,128)(2,1)} %get-tuple-element.20) | copy-start | bytes 2359300
  715.9 5.4 copy-start.29
  731.9 106.5 %reduce-scatter.23.cloned.1.call-start = ((), (), s32[]{:S(2)}) async-start(), calls=%async_computation.24 | async-start | bytes 2621440 | tf_op jit(solution)/shard_map/reduce_scatter | solution.py:342
  742.1 141.9 %reduce-scatter.21.cloned.1.call-start = ((), (), s32[]{:S(2)}) async-start(), calls=%async_computation.23 | async-start | bytes 2621440 | tf_op jit(solution)/shard_map/reduce_scatter | solution.py:341
  752.0 177.9 %reduce-scatter.19.cloned.1.call-start = ((), (), s32[]{:S(2)}) async-start(), calls=%async_computation.22 | async-start | bytes 2621440 | tf_op jit(solution)/shard_map/reduce_scatter | solution.py:340
  762.4 241.8 %reduce-scatter.15.cloned.1.call-start = ((), (), s32[]{:S(2)}) async-start(), calls=%async_computation.20 | async-start | bytes 9437184 | tf_op jit(solution)/shard_map/reduce_scatter | solution.py:350
  773.8 305.7 %reduce-scatter.11.cloned.1.call-start = ((), (), s32[]{:S(2)}) async-start(), calls=%async_computation.17 | async-start | bytes 9437184 | tf_op jit(solution)/shard_map/reduce_scatter | solution.py:338
  794.6 138.1 %all-to-all-start.1 = ((bf16[8,64,768]{2,1,0:T(8,128)(2,1)}), bf16[8,64,768]{2,1,0:T(8,128)(2,1)}, u32[]{:S(2)}, u32[]{:S(2)}) async-start(bf16[8,64,768]{2,1,0:T(8,128)(2,1)} %bitcast.95), calls=%async_computation.6 | async-start | bytes 1572864 | tf_op jit(solution)/shard_map/all_to_all | solution.py:358
  798.8 133.3 %copy-start.8 = (f32[128,128]{1,0:T(8,128)S(1)}, f32[128,128]{1,0:T(8,128)}, u32[]{:S(2)}) copy-start(f32[128,128]{1,0:T(8,128)} %get-tuple-element.28) | copy-start | bytes 196612
  950.3 54.0 %copy-start.7 = (f32[1,2048]{1,0:T(1,128)S(1)}, f32[1,2048]{1,0:T(1,128)}, u32[]{:S(2)}) copy-start(f32[1,2048]{1,0:T(1,128)} %copy-done.6) | copy-start | bytes 24580
  957.8 48.3 %copy-start.9 = (f32[2048]{0:T(1024)S(1)}, f32[2048]{0:T(1024)}, u32[]{:S(2)}) copy-start(f32[2048]{0:T(1024)} %get-tuple-element.29) | copy-start | bytes 24580
  957.8 48.4 %copy-start.19 = (f32[128]{0:T(128)S(1)}, f32[128]{0:T(128)}, u32[]{:S(2)}) copy-start(f32[128]{0:T(128)} %slice_reduce_fusion) | copy-start | bytes 1540
  957.8 121.7 %copy-start.11 = (f32[256]{0:T(256)S(1)}, f32[256]{0:T(256)}, u32[]{:S(2)}) copy-start(f32[256]{0:T(256)} %copy-done.10) | copy-start | bytes 3076
  957.8 121.7 %copy-start.13 = (f32[256]{0:T(256)S(1)}, f32[256]{0:T(256)}, u32[]{:S(2)}) copy-start(f32[256]{0:T(256)} %copy-done.12) | copy-start | bytes 3076
  957.8 121.7 %copy-start.15 = (f32[256]{0:T(256)S(1)}, f32[256]{0:T(256)}, u32[]{:S(2)}) copy-start(f32[256]{0:T(256)} %copy-done.14) | copy-start | bytes 3076
  957.8 121.7 %copy-start.17 = (f32[256]{0:T(256)S(1)}, f32[256]{0:T(256)}, u32[]{:S(2)}) copy-start(f32[256]{0:T(256)} %copy-done.16) | copy-start | bytes 3076
  957.8 121.7 %copy-start.18 = (f32[256]{0:T(256)S(1)}, f32[256]{0:T(256)}, u32[]{:S(2)}) copy-start(f32[256]{0:T(256)} %get-tuple-element.52) | copy-start | bytes 3076
Sparse Core Ops, SparseCore 0:
  29.2 62.9 all-gather.12
  94.6 52.9 all-gather.14
  183.8 71.2 reduce-scatter.8
  256.6 45.9 all-gather.20
  305.0 53.0 all-gather.16
  359.7 45.9 all-gather.18
  407.3 44.6 all-gather.22
  454.0 53.0 all-gather.26
  541.7 71.3 reduce-scatter.12
  617.7 54.3 all-gather.24
  732.0 60.2 reduce-scatter.16
  794.4 43.8 reduce-scatter.22
  840.8 43.1 reduce-scatter.20
  886.7 43.1 reduce-scatter.18
  933.6 70.5 reduce-scatter.14
  1007.6 71.8 reduce-scatter.10

commit v2 on v1

--- a/solution.py
+++ b/solution.py
@@ -263,6 +263,366 @@
     )(proj, table, gq, gk, dm, *kept)
 
 
+MESH = pl.DeviceIdType.MESH
+
+
+class Place:
+    def __init__(self):
+        self.row = lax.axis_index("rows")
+        self.me = lax.axis_index("seq")
+        self.core = lax.rem(self.me, 2)
+        self.chip = self.me // 2
+        self.sib = self.me + 1 - 2 * self.core
+        chip = self.chip
+        self.chips = (chip, chip + 1 - 2 * lax.rem(chip, 2), lax.rem(chip + 2, 4), 3 - chip)
+        self.same = tuple(2 * q + self.core for q in self.chips)
+
+    def greet(self):
+        barrier = pltpu.get_barrier_semaphore()
+        for other in (self.sib, self.same[1], self.same[2]):
+            pl.semaphore_signal(barrier, inc=1, device_id=(self.row, other), device_id_type=MESH)
+        pl.semaphore_wait(barrier, 3)
+
+    def send(self, src, dst, send_sem, recv_sem, slot, target):
+        return pltpu.make_async_remote_copy(
+            src_ref=src, dst_ref=dst, send_sem=send_sem.at[slot], recv_sem=recv_sem.at[slot],
+            device_id=(self.row, target), device_id_type=MESH)
+
+
+GATHER_SLOTS = 10
+
+
+class Gather:
+    def __init__(self, place, every, send_sem, recv_sem):
+        half = every.shape[1] // 2
+        low = lambda b: every.at[b, 0:half]
+        high = lambda b: every.at[b, half:2 * half]
+        whole = lambda b: every.at[b]
+        send = lambda part, b, slot, target: place.send(part(b), part(b), send_sem, recv_sem, slot, target)
+        me, (_, s1, s2, s3), sib = place.me, place.same, place.sib
+        self.copies = (
+            send(whole, me, 0, sib),
+            send(low, me, 1, s1), send(high, me, 2, s1),
+            send(high, me, 3, s2), send(low, me, 4, s2),
+            send(low, s1, 5, s2), send(high, s2, 6, s1),
+            send(whole, s1, 7, sib), send(whole, s2, 8, sib), send(whole, s3, 9, sib),
+        )
+
+    def start(self):
+        for slot in (1, 3, 2, 4, 0):
+            self.copies[slot].start()
+
+    def own_chip(self):
+        self.copies[0].wait_recv()
+
+    def neighbours(self):
+        c = self.copies
+        c[1].wait_recv()
+        c[5].start()
+        c[3].wait_recv()
+        c[6].start()
+        c[2].wait_recv()
+        c[7].start()
+        c[4].wait_recv()
+        c[8].start()
+
+    def chip1(self):
+        self.copies[7].wait_recv()
+
+    def chip2(self):
+        self.copies[8].wait_recv()
+
+    def diagonal(self):
+        c = self.copies
+        c[5].wait_recv()
+        c[6].wait_recv()
+        c[9].start()
+
+    def chip3(self):
+        self.copies[9].wait_recv()
+
+    def close(self):
+        for copy in self.copies:
+            copy.wait_send()
+
+
+SCATTER_SLOTS = 10
+
+
+class Scatter:
+    def __init__(self, place, part, sibling, passing, final, send_sem, recv_sem):
+        self.place, self.part, self.sibling, self.passing, self.final = place, part, sibling, passing, final
+        half = part.shape[2] // 2
+        self.half = half
+        core, other = place.core, 1 - place.core
+        _, s1, s2, _ = place.same
+        send = lambda src, dst, slot, target: place.send(src, dst, send_sem, recv_sem, slot, target)
+        low, high = slice(0, half), slice(half, 2 * half)
+        self.exchange = tuple(send(part.at[k, other], sibling.at[k], k, place.sib) for k in range(4))
+        self.pass1 = send(part.at[3, core, low], passing.at[0], 4, s1)
+        self.pass2 = send(part.at[3, core, high], passing.at[1], 5, s2)
+        self.first1 = send(part.at[1, core, low], final.at[0, low], 6, s1)
+        self.second1 = send(part.at[1, core, high], final.at[0, high], 7, s1)
+        self.first2 = send(part.at[2, core, high], final.at[1, high], 8, s2)
+        self.second2 = send(part.at[2, core, low], final.at[1, low], 9, s2)
+
+    def add(self, k, start, size, term, offset):
+        core, step = self.place.core, 64
+
+        def one(i, _):
+            rows = pl.ds(pl.multiple_of(start + i * step, step), step)
+            from_rows = pl.ds(pl.multiple_of(offset + i * step, step), step)
+            total = self.part[k, core, rows, :].astype(F32) + term[from_rows, :].astype(F32)
+            self.part[k, core, rows, :] = total.astype(BF16)
+            return 0
+
+        lax.fori_loop(0, size // step, one, 0)
+
+    def combine(self, k):
+        self.exchange[k].wait_recv()
+        self.add(k, 0, 2 * self.half, self.sibling.at[k], 0)
+
+    def finish_two(self):
+        self.pass1.wait_recv()
+        self.add(2, 0, self.half, self.passing.at[0], 0)
+        self.second2.start()
+        self.pass2.wait_recv()
+        self.add(1, self.half, self.half, self.passing.at[1], 0)
+        self.second1.start()
+
+    def arrive(self):
+        for copy in (self.first1, self.second1, self.first2, self.second2):
+            copy.wait_recv()
+
+    def total(self, rows):
+        return (self.part[0, self.place.core, rows, :].astype(F32) + self.final[0, rows, :].astype(F32)
+                + self.final[1, rows, :].astype(F32))
+
+    def close(self):
+        for copy in self.exchange + (self.pass1, self.pass2, self.first1, self.second1, self.first2, self.second2):
+            copy.wait_send()
+
+
+def scatter_scratch(tok, width):
+    return [
+        pltpu.VMEM((4, 2, tok, width), BF16),
+        pltpu.VMEM((4, tok, width), BF16),
+        pltpu.VMEM((2, tok // 2, width), BF16),
+        pltpu.VMEM((2, tok, width), BF16),
+        pltpu.SemaphoreType.DMA((SCATTER_SLOTS,)),
+        pltpu.SemaphoreType.DMA((SCATTER_SLOTS,)),
+    ]
+
+
+def ffn_kernel(res_ref, gain_ref, g_hbm, gate_hbm, up_hbm, down_hbm,
+               out_hbm, rgrad_ref, branch_ref, gain_grad_ref, gate_grad_hbm, up_grad_hbm, down_grad_hbm,
+               two_ref, g_ref, gate_ref, up_ref, down_ref, hid_ref, gu_ref, stage_ref, wstage_ref,
+               part_ref, sibling_ref, passing_ref, final_ref, rs_send, rs_recv,
+               ag_send, ag_recv, load_sem, stage_sem, wstage_sem):
+    place = Place()
+    _, tok, model = g_ref.shape
+    ff = gate_ref.shape[1]
+    tile = 256
+    loads = [pltpu.make_async_copy(src, dst, load_sem.at[i]) for i, (src, dst) in enumerate(
+        ((gate_hbm, gate_ref), (up_hbm, up_ref), (g_hbm, g_ref), (down_hbm, down_ref)))]
+    for copy in loads:
+        copy.start()
+
+    def norm_rows(i, _):
+        rows = pl.ds(pl.multiple_of(i * 32, 32), 32)
+        res = res_ref[rows, :]
+        inv = lax.rsqrt(jnp.mean(res * res, axis=-1, keepdims=True) + EPSILON)
+        two_ref[place.me, rows, :] = (res * inv * gain_ref[...]).astype(BF16)
+        return 0
+
+    lax.fori_loop(0, tok // 32, norm_rows, 0)
+    place.greet()
+    gather = Gather(place, two_ref, ag_send, ag_recv)
+    scatter = Scatter(place, part_ref, sibling_ref, passing_ref, final_ref, rs_send, rs_recv)
+    gather.start()
+    for copy in loads:
+        copy.wait()
+
+    def stage_copy(k):
+        m = place.chips[k]
+        return pltpu.make_async_copy(stage_ref.at[k % 2], out_hbm.at[pl.ds(2 * m, 2)], stage_sem.at[k % 2])
+
+    def compute(k):
+        m = place.chips[k]
+        pair = pl.ds(2 * m, 2)
+
+        def hidden_tile(h, _):
+            cols = pl.ds(pl.multiple_of(h * tile, tile), tile)
+            cols2 = pl.ds(pl.multiple_of(ff + h * tile, tile), tile)
+            x = two_ref[pair].reshape(2 * tok, model)
+            gate = dot(x, gate_ref[:, cols])
+            up = dot(x, up_ref[:, cols])
+            back = dot_nt(g_ref[pair].reshape(2 * tok, model), down_ref[cols, :])
+            s = 1.0 / (1.0 + jnp.exp(-gate))
+            act = gate * s
+            hid_ref[pair, :, cols] = (act * up).astype(BF16).reshape(2, tok, tile)
+            gu_ref[pair, :, cols] = (back * up * s * (1.0 + gate * (1.0 - s))).astype(BF16).reshape(2, tok, tile)
+            gu_ref[pair, :, cols2] = (back * act).astype(BF16).reshape(2, tok, tile)
+            return 0
+
+        lax.fori_loop(0, ff // tile, hidden_tile, 0)
+        if k >= 2:
+            stage_copy(k - 2).wait()
+
+        def model_tile(n, _):
+            cols = pl.ds(pl.multiple_of(n * tile, tile), tile)
+            gg = gu_ref[pair, :, 0:ff].reshape(2 * tok, ff)
+            ug = gu_ref[pair, :, ff:2 * ff].reshape(2 * tok, ff)
+            back = dot_nt(gg, gate_ref[cols, :]) + dot_nt(ug, up_ref[cols, :])
+            part_ref[k, :, :, cols] = back.astype(BF16).reshape(2, tok, tile)
+            return 0
+
+        lax.fori_loop(0, model // tile, model_tile, 0)
+        scatter.exchange[k].start()
+
+        def out_tile(n, _):
+            cols = pl.ds(pl.multiple_of(n * tile, tile), tile)
+            hid = hid_ref[pair].reshape(2 * tok, ff)
+            out = dot(hid, down_ref[:, cols])
+            stage_ref[k % 2, :, :, cols] = out.astype(BF16).reshape(2, tok, tile)
+            return 0
+
+        lax.fori_loop(0, model // tile, out_tile, 0)
+        stage_copy(k).start()
+
+    gather.own_chip()
+    compute(0)
+    gather.neighbours()
+    gather.chip1()
+    compute(1)
+    gather.chip2()
+    scatter.combine(1)
+    scatter.first1.start()
+    compute(2)
+    gather.diagonal()
+    scatter.combine(2)
+    scatter.first2.start()
+    gather.chip3()
+    compute(3)
+    scatter.combine(3)
+    scatter.pass1.start()
+    scatter.pass2.start()
+    scatter.combine(0)
+
+    blocks = two_ref.shape[0]
+
+    def wstage_copies(i, slot):
+        rows = pl.ds(pl.multiple_of(i * tile, tile), tile)
+        return (pltpu.make_async_copy(wstage_ref.at[slot, :, 0:ff], gate_grad_hbm.at[rows], wstage_sem.at[slot, 0]),
+                pltpu.make_async_copy(wstage_ref.at[slot, :, ff:2 * ff], up_grad_hbm.at[rows], wstage_sem.at[slot, 1]))
+
+    def gate_up_rows(i, _):
+        cols = pl.ds(pl.multiple_of(i * tile, tile), tile)
+        slot = lax.rem(i, 2)
+
+        @pl.when(i >= 2)
+        def _():
+            for copy in wstage_copies(i - 2, slot):
+                copy.wait()
+
+        x = two_ref[:, :, cols].reshape(blocks * tok, tile)
+        wstage_ref[slot] = dot_tn(x, gu_ref[...].reshape(blocks * tok, 2 * ff)).astype(BF16)
+        for copy in wstage_copies(i, slot):
+            copy.start()
+        return 0
+
+    count = model // tile
+    lax.fori_loop(0, count // 2, gate_up_rows, 0)
+    scatter.finish_two()
+    lax.fori_loop(count // 2, count, gate_up_rows, 0)
+    for i in (count - 2, count - 1):
+        for copy in wstage_copies(i, i % 2):
+            copy.wait()
+
+    stage_copy(2).wait()
+    stage_copy(3).wait()
+
+    def down_rows(i, _):
+        rows = pl.ds(pl.multiple_of(i * tile, tile), tile)
+        h = hid_ref[:, :, rows].reshape(blocks * tok, tile)
+
+        def down_cols(n, _):
+            cols = pl.ds(pl.multiple_of(n * 512, 512), 512)
+            g = g_ref[:, :, cols].reshape(blocks * tok, 512)
+            stage_ref[0, i, :, cols] = dot_tn(h, g).astype(BF16)
+            return 0
+
+        lax.fori_loop(0, model // 512, down_cols, 0)
+        return 0
+
+    lax.fori_loop(0, ff // tile, down_rows, 0)
+    down_out = [pltpu.make_async_copy(stage_ref.at[0, i], down_grad_hbm.at[pl.ds(i * tile, tile)], stage_sem.at[i])
+                for i in range(ff // tile)]
+    for copy in down_out:
+        copy.start()
+
+    scatter.arrive()
+
+    def finish(i, sums):
+        rows = pl.ds(pl.multiple_of(i * 32, 32), 32)
+        res = res_ref[rows, :]
+        inv = lax.rsqrt(jnp.mean(res * res, axis=-1, keepdims=True) + EPSILON)
+        grad = scatter.total(rows)
+        v = grad * gain_ref[...]
+        mean = jnp.mean(v * res, axis=-1, keepdims=True)
+        out = g_ref[place.me, rows, :].astype(F32) + inv * v - res * (inv * inv * inv * mean)
+        rgrad_ref[rows, :] = out
+        branch_ref[rows, :] = out.astype(BF16)
+        return sums + jnp.sum(grad * res * inv, axis=0, keepdims=True)
+
+    gain_grad_ref[...] = lax.fori_loop(0, tok // 32, finish, jnp.zeros((1, model), F32))
+    for copy in down_out:
+        copy.wait()
+    gather.close()
+    scatter.close()
+
+
+def feed_forward(res, gain, g_all, gate, up, down):
+    tok, model = res.shape
+    ff = gate.shape[1]
+    blocks = g_all.shape[0]
+    any_spec = pl.BlockSpec(memory_space=pl.ANY)
+    vmem = pl.BlockSpec(memory_space=pltpu.VMEM)
+    return pl.pallas_call(
+        ffn_kernel,
+        out_shape=(
+            jax.ShapeDtypeStruct((blocks, tok, model), BF16),
+            jax.ShapeDtypeStruct((tok, model), F32),
+            jax.ShapeDtypeStruct((tok, model), BF16),
+            jax.ShapeDtypeStruct((1, model), F32),
+            jax.ShapeDtypeStruct((model, ff), BF16),
+            jax.ShapeDtypeStruct((model, ff), BF16),
+            jax.ShapeDtypeStruct((ff, model), BF16),
+        ),
+        in_specs=[vmem, vmem] + [any_spec] * 4,
+        out_specs=(any_spec, vmem, vmem, vmem, any_spec, any_spec, any_spec),
+        scratch_shapes=[
+            pltpu.VMEM((blocks, tok, model), BF16),
+            pltpu.VMEM((blocks, tok, model), BF16),
+            pltpu.VMEM((model, ff), BF16),
+            pltpu.VMEM((model, ff), BF16),
+            pltpu.VMEM((ff, model), BF16),
+            pltpu.VMEM((blocks, tok, ff), BF16),
+            pltpu.VMEM((blocks, tok, 2 * ff), BF16),
+            pltpu.VMEM((2, 2, tok, model), BF16),
+            pltpu.VMEM((2, 256, 2 * ff), BF16),
+            *scatter_scratch(tok, model),
+            pltpu.SemaphoreType.DMA((GATHER_SLOTS,)),
+            pltpu.SemaphoreType.DMA((GATHER_SLOTS,)),
+            pltpu.SemaphoreType.DMA((4,)),
+            pltpu.SemaphoreType.DMA((2,)),
+            pltpu.SemaphoreType.DMA((2, 2)),
+        ],
+        compiler_params=pltpu.CompilerParams(collective_id=3, has_side_effects=True, vmem_limit_bytes=60 * 1024 * 1024),
+        cost_estimate=pl.CostEstimate(flops=18 * blocks * tok * model * ff, bytes_accessed=64 << 20, transcendentals=0),
+    )(res, gain, g_all, gate, up, down)
+
+
 def norm_inverse(x):
     return lax.rsqrt(jnp.mean(x * x, axis=-1, keepdims=True) + EPSILON)
 
@@ -272,6 +632,29 @@
     gain_grad = jnp.sum(grad_normed * values_in * inv_rms, axis=0)
     input_grad = inv_rms * scaled - values_in * inv_rms**3 * jnp.mean(scaled * values_in, axis=-1, keepdims=True)
     return input_grad, gain_grad
+
+
+def feed_forward_wide(res, gain, g_blocks, gate_slab, up_slab, down_slab):
+    blocks, tok, model = g_blocks.shape
+    inv = norm_inverse(res)
+    two_all = lax.all_gather((res * inv * gain).astype(BF16), "seq", axis=0, tiled=True)
+    g_all = g_blocks.reshape(blocks * tok, model)
+    gate_act = dot(two_all, gate_slab)
+    up_act = dot(two_all, up_slab)
+    s = jax.nn.sigmoid(gate_act)
+    hidden = (gate_act * s * up_act).astype(BF16)
+    hidden_grad = dot_nt(g_all, down_slab)
+    gate_grad = (hidden_grad * up_act * s * (1.0 + gate_act * (1.0 - s))).astype(BF16)
+    up_grad = (hidden_grad * gate_act * s).astype(BF16)
+    part = (dot_nt(gate_grad, gate_slab) + dot_nt(up_grad, up_slab)).astype(BF16)
+    two_grad = lax.psum_scatter(part, "seq", scatter_dimension=0, tiled=True).astype(F32)
+    branch_part = dot(hidden, down_slab).astype(BF16).reshape(blocks, tok, model)
+    norm_grad, gain_grad = norm_back(two_grad, res, inv, gain)
+    g = lax.dynamic_index_in_dim(g_blocks, lax.axis_index("seq"), 0, keepdims=False)
+    residual_grad = g.astype(F32) + norm_grad
+    return (branch_part, residual_grad, residual_grad.astype(BF16), gain_grad[None],
+            dot_tn(two_all, gate_grad).astype(BF16), dot_tn(two_all, up_grad).astype(BF16),
+            dot_tn(hidden, g_all).astype(BF16))
 
 
 def body(tokens, segments, positions, cotangent, gain_attn, w_qkv, gain_q, gain_k, w_out, gain_ffn, w_gate, w_up, w_down):
@@ -320,30 +703,17 @@
     merged, *kept = attention_forward(heads, proj, table, gq, gk)
     out_part = dot_nt(merged, out_slab).astype(BF16)
     residual = x + lax.psum_scatter(out_part, "seq", scatter_dimension=0, tiled=True).astype(F32)
-    inv_two = norm_inverse(residual)
-    normed_two = (residual * inv_two * gain_two).astype(BF16)
-    two_all = lax.all_gather(normed_two, "seq", axis=0, tiled=True)
-    g_all = lax.all_gather(cotangent[0], "seq", axis=0, tiled=True)
-
-    gate_act = dot(two_all, gate_slab)
-    up_act = dot(two_all, up_slab)
-    s = jax.nn.sigmoid(gate_act)
-    hidden = (gate_act * s * up_act).astype(BF16)
-    hidden_grad = dot_nt(g_all, down_slab)
-    gate_grad = (hidden_grad * up_act * s * (1.0 + gate_act * (1.0 - s))).astype(BF16)
-    up_grad = (hidden_grad * gate_act * s).astype(BF16)
-    two_grad_part = (dot_nt(gate_grad, gate_slab) + dot_nt(up_grad, up_slab)).astype(BF16)
-    two_grad = lax.psum_scatter(two_grad_part, "seq", scatter_dimension=0, tiled=True).astype(F32)
-    branch_part = dot(hidden, down_slab).astype(BF16)
-    branch = lax.psum_scatter(branch_part, "seq", scatter_dimension=0, tiled=True).astype(F32)
+    g_all = lax.all_gather(cotangent[0], "seq", axis=0, tiled=False)
+    phase = feed_forward if seq == 8 else feed_forward_wide
+    branch_part, residual_grad, branch_grad, gain_two_grad, gate_wgrad, up_wgrad, down_wgrad = phase(
+        residual, gain_two, g_all, gate_slab, up_slab, down_slab)
+    gain_two_grad = gain_two_grad[0]
+    branch = lax.psum_scatter(branch_part.reshape(seq * tok, -1), "seq", scatter_dimension=0, tiled=True).astype(F32)
     layer_out = (residual + branch).astype(BF16)
-    grad_gate = lax.psum_scatter(dot_tn(two_all, gate_grad).astype(BF16), "rows", scatter_dimension=0, tiled=True).astype(F32)
-    grad_up = lax.psum_scatter(dot_tn(two_all, up_grad).astype(BF16), "rows", scatter_dimension=0, tiled=True).astype(F32)
-    grad_down = lax.psum_scatter(dot_tn(hidden, g_all).astype(BF16), "rows", scatter_dimension=1, tiled=True).astype(F32)
-
-    norm_grad, gain_two_grad = norm_back(two_grad, residual, inv_two, gain_two)
-    residual_grad = cotangent[0].astype(F32) + norm_grad
-    branch_all = lax.all_gather(residual_grad.astype(BF16), "seq", axis=0, tiled=True)
+    grad_gate = lax.psum_scatter(gate_wgrad, "rows", scatter_dimension=0, tiled=True).astype(F32)
+    grad_up = lax.psum_scatter(up_wgrad, "rows", scatter_dimension=0, tiled=True).astype(F32)
+    grad_down = lax.psum_scatter(down_wgrad, "rows", scatter_dimension=1, tiled=True).astype(F32)
+    branch_all = lax.all_gather(branch_grad, "seq", axis=0, tiled=True)
     dm = dot(branch_all, out_slab).astype(BF16)
     pg, head_gains = attention_backward(heads, proj, table, gq, gk, dm, kept)
     normed_part = lax.dot_general(pg, qkv_slab, (((0,), (1,)), ((), ())), preferred_element_type=F32).astype(BF16)

time: 1100 us -> 1020 us (0.927)
  matrix products: 146 us -> 49.1 us
  Pallas kernels: 52.3 us -> 147 us
  waiting for transfers between devices: 703 us -> 655 us
  local copies, waits for them, and re-layouts: 29.5 us -> 14.7 us
    pallas_call x0 -> x1, Pallas kernels: none -> 94.3 us  [feed_forward(): pl.pallas_call(ffn_kernel, out_shape=(jax.ShapeDtypeStruct((blocks, tok,...]
    reduce_scatter x5 -> x4, waiting for transfers between devices: 231 us -> 160 us  [the longest x1 43.4 us: body(): lax.psum_scatter(up_wgrad, 'rows', scatter_dimension=0, tiled=True)]
    all_gather x3 -> x2, waiting for transfers between devices: 165 us -> 109 us  [the longest x1 55.2 us: body(): g_all = lax.all_gather(cotangent[0], 'seq', axis=0, tiled=False)]
    reduce_scatter x1, waiting for transfers between devices: 8.3 us -> 46.8 us  [body(): lax.psum_scatter(attn_grad, 'rows', scatter_dimension=0, tiled=True)]
    dot_general x4 -> x1, matrix products: 41.6 us -> 7.25 us  [dot_nt(): lax.dot_general(a, b, (((1,), (1,)), ((), ())), preferred_element_type=F32)]
    dot_general x4 -> x1, matrix products: 38.4 us -> 6.58 us  [dot(): return jnp.dot(a, b, preferred_element_type=F32)]
    dot_general x4 -> x1, matrix products: 35.1 us -> 5.36 us  [dot_tn(): lax.dot_general(a, b, (((0,), (0,)), ((), ())), preferred_element_type=F32)]
    reduce_scatter x1, waiting for transfers between devices: 46.4 us -> 63.7 us  [body(): lax.psum_scatter(normed_part, 'seq', scatter_dimension=0, tiled=True)]
  transfers between devices with their start and end apart: 17 -> 15, of which waited for: 16 -> 14; matrix products, arithmetic and copies ran while one was open for 11% -> 4% of each run, Pallas kernels for 0% -> 0%
where the time goes in v2:
time: 1020 us; the launch traced here: 1010 us
  waiting for transfers between devices  655 us (64%)
  Pallas kernels  147 us (14%)
  blocking collectives  108 us (11%)
  matrix products  49.1 us (5%)
  other arithmetic  22.3 us (2%)
  local copies, waits for them, and re-layouts  14.7 us (1%)
  between operations  14.7 us (1%)
    pallas_call x1, Pallas kernels, feed_forward(): pl.pallas_call(ffn_kernel, out_shape=(jax.ShapeDtypeStruct((blocks, tok,...  94.3 us
    reduce_scatter x1, waiting for transfers between devices, body(): lax.psum_scatter(out_part, 'seq', scatter_dimension=0, tiled=True)  68.9 us
    reduce_scatter x1, waiting for transfers between devices, body(): lax.psum_scatter(normed_part, 'seq', scatter_dimension=0, tiled=True)  63.7 us
    all_gather x1, waiting for transfers between devices, body(): normed_all = lax.all_gather(normed, 'seq', axis=0, tiled=True)  55.4 us
    all_gather x1, waiting for transfers between devices, body(): g_all = lax.all_gather(cotangent[0], 'seq', axis=0, tiled=False)  55.2 us
    all_gather x1, waiting for transfers between devices, body(): branch_all = lax.all_gather(branch_grad, 'seq', axis=0, tiled=True)  54.3 us
    reduce_scatter x1, waiting for transfers between devices, body(): lax.psum_scatter(attn_grad, 'rows', scatter_dimension=0, tiled=True)  46.8 us
    all_gather x1, waiting for transfers between devices, body(): down_slab = lax.all_gather(w_down, 'rows', axis=1, tiled=True)  46.2 us
  transfers between devices with their start and end apart: 15, of which 14 were waited for; matrix products, arithmetic and copies ran while one was open for 4% of the time, Pallas kernels for 0%

profile of v2, /device:TPU:0, one launch (start us, length us, event | category | flops | bytes accessed | tf_op | source)
XLA Modules:
  0.0 1014.6 jit_solution(5160129010003546581)
XLA Ops:
  7.2 0.9 fusion.18
  10.4 17.8 %all_to_all.10 = bf16[8,64,768]{2,1,0:T(8,128)(2,1)} all-to-all(bf16[8,64,768]{2,1,0:T(8,128)(2,1)S(1)} %copy.65), channel_id=1, replica_groups=mesh['rows'=4,'seq'=8] {'seq'}, dimensions={0} | all-to-all | bytes 1572864 | tf_op jit(solution)/shard_map/all_to_all | solution.py:684
  28.3 40.1 %all-gather.2 = bf16[32,64,2]{1,2,0:T(2,128)(2,1)S(1)} all-gather(bf16[1,64,2]{1,2,0:T(2,128)(2,1)S(1)} %maximum_bitcast_fusion.1), channel_id=2, replica_groups=mesh['rows'=4,'seq'=8] {'rows','seq'}, dimensions={0}, use_global_device_ids=true | all-gather | bytes 8448 | tf_op jit(solution)/shard_map/all_gather | solution.py:688
  69.4 1.3 fusion.9
  70.8 0.7 copy.67.gq_ref
  71.5 0.7 copy.68.gk_ref
  72.5 10.1 all-gather.1
  82.5 8.7 all-gather.11.cloned.1.call-done
  91.3 55.4 %all-gather.13.cloned.1.call-done = bf16[2048,2048]{1,0:T(8,128)(2,1)} async-done(((bf16[256,2048]{1,0:T(8,128)(2,1)}), bf16[2048,2048]{1,0:T(8,128)(2,1)}) %all-gather.13.cloned.1.call-update) | async-done | bytes 8388624 | tf_op jit(solution)/shard_map/all_gather | solution.py:701
  146.7 10.5 %fusion.2.proj_ref = f32[576,2048]{1,0:T(8,128)} fusion(bf16[2048,2048]{1,0:T(8,128)(2,1)} %all-gather.13.cloned.1.call-done, bf16[2048,768]{1,0:T(8,128)(2,1)} %all-gather.11.cloned.1.call-done), kind=kOutput, calls=%fused_computation.15 | convolution fusion | flops 4831838208 | bytes 15728640 | tf_op jit(solution)/shard_map/dot_general | solution.py:702
  157.2 18.2 %shard_map.212 = (bf16[2048,192]{1,0:T(8,128)(2,1)}, f32[3,64,2048]{2,1,0:T(8,128)}, bf16[3,80,2048]{2,1,0:T(8,128)(2,1)}, bf16[3,2048,128]{2,1,0:T(8,128)(2,1)}...) custom-call(f32[576,2048]{1,0:T(8,128)} %fusion.2.proj_ref, ...), custom_call_target="tpu_custom_call" | custom-call | flops 3221225472 | bytes 16777216 | tf_op jit(solution)/shard_map/pallas_call | solution.py:229
  175.4 7.2 convolution_convert_fusion.1
  184.5 0.7 all-gather.15.cloned.1.call-update
  185.2 68.9 %reduce-scatter.8.cloned.1.call-done = bf16[256,2048]{1,0:T(8,128)(2,1)} async-done(((bf16[2048,2048]{1,0:T(8,128)(2,1)}), bf16[256,2048]{1,0:T(8,128)(2,1)}) %reduce-scatter.8.cloned.1.call-update) | async-done | bytes 1048592 | tf_op jit(solution)/shard_map/reduce_scatter | solution.py:705
  254.1 2.9 convert_add_fusion.res_ref
  257.0 44.6 %all-gather.17.cloned.1.call-done.gate_hbm = bf16[2048,512]{1,0:T(8,128)(2,1)} async-done(((bf16[512,512]{1,0:T(8,128)(2,1)}), bf16[2048,512]{1,0:T(8,128)(2,1)}) %all-gather.17.cloned.1.call-update) | async-done | bytes 2097168 | tf_op jit(solution)/shard_map/all_gather | solution.py:691
  301.6 46.2 %all-gather.19.cloned.1.call-done.up_hbm = bf16[2048,512]{1,0:T(8,128)(2,1)} async-done(((bf16[512,512]{1,0:T(8,128)(2,1)}), bf16[2048,512]{1,0:T(8,128)(2,1)}) %all-gather.19.cloned.1.call-update) | async-done | bytes 2097168 | tf_op jit(solution)/shard_map/all_gather | solution.py:692
  347.8 46.2 %all-gather.21.cloned.1.call-done.down_hbm = bf16[512,2048]{1,0:T(8,128)(2,1)} async-done(((bf16[512,512]{1,0:T(8,128)(2,1)}), bf16[512,2048]{1,0:T(8,128)(2,1)}) %all-gather.21.cloned.1.call-update) | async-done | bytes 2097168 | tf_op jit(solution)/shard_map/all_gather | solution.py:693
  393.9 55.2 %all-gather.15.cloned.1.call-done.g_hbm = bf16[8,256,2048]{2,1,0:T(8,128)(2,1)} async-done(((bf16[1,256,2048]{2,1,0:T(8,128)(2,1)}), bf16[8,256,2048]{2,1,0:T(8,128)(2,1)}) %all-gather.15.cloned.1.call-update) | async-done | bytes 8388624 | tf_op jit(solution)/shard_map/all_gather | solution.py:706
  449.1 94.3 %shard_map.213 = (bf16[8,256,2048]{2,1,0:T(8,128)(2,1)}, f32[256,2048]{1,0:T(8,128)}, bf16[256,2048]{1,0:T(8,128)(2,1)}, f32[1,2048]{1,0:T(1,128)}, bf16[2048,51...) custom-call(f32[256,2048]{1,0:T(8,128)} %convert_add_fusion.res_ref, ...), custom_call_target="tpu_custom_call" | custom-call | flops 38654705664 | bytes 67108864 | tf_op jit(solution)/shard_map/pallas_call | solution.py:591
  543.7 54.3 %all-gather.23.cloned.1.call-done = bf16[2048,2048]{1,0:T(8,128)(2,1)} async-done(((bf16[256,2048]{1,0:T(8,128)(2,1)}), bf16[2048,2048]{1,0:T(8,128)(2,1)}) %all-gather.23.cloned.1.call-update) | async-done | bytes 8388624 | tf_op jit(solution)/shard_map/all_gather | solution.py:716
  598.0 6.6 convolution_convert_fusion.4
  604.6 1.3 copy.71.dm_ref
  605.9 34.1 %shard_map.214 = (bf16[576,2048]{1,0:T(8,128)(2,1)}, f32[128,128]{1,0:T(8,128)}) custom-call(f32[576,2048]{1,0:T(8,128)} %fusion.2.proj_ref, f32[8,72,256]{2,1,0:T(8,128)} %bitcast.60, f32[64,1]{1,0:T(8,128)} %copy.67.gq_ref, f32[64,1]{1,0:T(8,128)} %copy.68.gk_ref, bf16[2048,192]{1,0:T(8,128)(2,1)} %copy.71.dm_ref, f32[3,64,2048]{2,1,0:T(8,128)} %get-tuple-element.31.o_ref, ...), custom_call_target="tpu_custom_call" | custom-call | flops 8053063680 | bytes 16777216 | tf_op jit(solution)/shard_map/pallas_call | solution.py:247
  640.0 5.4 convolution_convert_fusion.3
  645.4 8.6 convolution_convert_fusion.2
  654.0 1.9 pad_maximum_fusion
  656.5 0.7 reduce-scatter.18.cloned.1.call-update
  658.1 10.8 %convolution_convert_fusion = bf16[2048,2048]{1,0:T(8,128)(2,1)} fusion(bf16[576,2048]{1,0:T(8,128)(2,1)S(1)} %copy-done.14, bf16[2048,768]{1,0:T(8,128)(2,1)} %all-gather.11.cloned.1.call-done), kind=kOutput, calls=%fused_computation | convolution fusion | flops 4836032512 | bytes 13369344 | tf_op jit(solution)/shard_map/dot_general | solution.py:719
  669.5 46.8 %reduce-scatter.14.cloned.1.call-done = bf16[512,768]{0,1:T(8,128)(2,1)} async-done(((bf16[2048,768]{0,1:T(8,128)(2,1)}), bf16[512,768]{0,1:T(8,128)(2,1)}) %reduce-scatter.14.cloned.1.call-update) | async-done | bytes 786448 | tf_op jit(solution)/shard_map/reduce_scatter | solution.py:727
  716.3 2.3 copy.72
  718.6 3.6 all-to-all-start.1
  722.2 40.2 %reduce-scatter.16.cloned.1.call-done = bf16[512,512]{1,0:T(8,128)(2,1)} async-done(((bf16[2048,512]{1,0:T(8,128)(2,1)}), bf16[512,512]{1,0:T(8,128)(2,1)}) %reduce-scatter.16.cloned.1.call-update) | async-done | bytes 524304 | tf_op jit(solution)/shard_map/reduce_scatter | solution.py:713
  762.4 2.1 convert_element_type.85
  764.6 43.4 %reduce-scatter.18.cloned.1.call-done = bf16[512,512]{1,0:T(8,128)(2,1)} async-done(((bf16[2048,512]{1,0:T(8,128)(2,1)}), bf16[512,512]{1,0:T(8,128)(2,1)}) %reduce-scatter.18.cloned.1.call-update) | async-done | bytes 524304 | tf_op jit(solution)/shard_map/reduce_scatter | solution.py:714
  808.0 2.1 convert_element_type.86
  810.1 43.3 %reduce-scatter.20.cloned.1.call-done = bf16[512,512]{1,0:T(8,128)(2,1)} async-done(((bf16[512,2048]{1,0:T(8,128)(2,1)}), bf16[512,512]{1,0:T(8,128)(2,1)}) %reduce-scatter.20.cloned.1.call-update) | async-done | bytes 524304 | tf_op jit(solution)/shard_map/reduce_scatter | solution.py:715
  853.4 2.1 convert_element_type.87
  855.8 1.1 slice_bitcast_fusion
  858.3 1.3 copy.75
  860.5 0.7 reshape.121
  862.1 0.9 reshape_reshape.15
  863.0 0.9 pad_maximum_fusion.1
  863.9 63.7 %reduce-scatter.12.cloned.1.call-done = bf16[256,2048]{1,0:T(8,128)(2,1)} async-done(((bf16[2048,2048]{1,0:T(8,128)(2,1)}), bf16[256,2048]{1,0:T(8,128)(2,1)}) %reduce-scatter.12.cloned.1.call-update) | async-done | bytes 1048592 | tf_op jit(solution)/shard_map/reduce_scatter | solution.py:720
  927.6 2.0 fusion.13
  929.5 39.8 %psum.7 = f32[4224]{0:T(1024)S(1)} all-reduce(f32[4224]{0:T(1024)S(1)} %pad_maximum_fusion.3), channel_id=1, replica_groups=mesh['rows'=4,'seq'=8] {'rows','seq'}, use_global_device_ids=true, to_apply=%region_6.7 | all-reduce | flops 4224 | bytes 33792 | tf_op jit(solution)/shard_map/psum | solution.py:740
  969.9 33.3 %reduce-scatter.10.cloned.1.call-done = bf16[256,2048]{1,0:T(8,128)(2,1)} async-done(((bf16[2048,2048]{1,0:T(8,128)(2,1)}), bf16[256,2048]{1,0:T(8,128)(2,1)}) %reduce-scatter.10.cloned.1.call-update) | async-done | bytes 1048592 | tf_op jit(solution)/shard_map/reduce_scatter | solution.py:711
  1003.2 4.4 fusion.6
  (96 shorter events, 11.5 us)
Async XLA Ops:
  7.2 2.3 slice-start
  7.2 2.5 copy-start.5
  7.2 84.1 %all-gather.11.cloned.1.call-start = ((), (), s32[]{:S(2)}) async-start(), calls=%async_computation.9 | async-start | bytes 3932160 | tf_op jit(solution)/shard_map/all_gather | solution.py:685
  10.2 18.0 %copy-start.10 = (bf16[64]{0:T(256)(128)(2,1)S(1)}, bf16[64]{0:T(256)(128)(2,1)}, u32[]{:S(2)}) copy-start(bf16[64]{0:T(256)(128)(2,1)} %param.22) | copy-start | bytes 388
  10.2 18.0 %copy-start.11 = (bf16[64]{0:T(256)(128)(2,1)S(1)}, bf16[64]{0:T(256)(128)(2,1)}, u32[]{:S(2)}) copy-start(bf16[64]{0:T(256)(128)(2,1)} %param.17) | copy-start | bytes 388
  10.3 58.2 %copy-start = (bf16[1,256,2048]{2,1,0:T(8,128)(2,1)S(1)}, bf16[1,256,2048]{2,1,0:T(8,128)(2,1)}, u32[]{:S(2)}) copy-start(bf16[1,256,2048]{2,1,0:T(8,128)(2,1)} %param.13) | copy-start | bytes 3145732
  28.2 118.5 %all-gather.13.cloned.1.call-start = ((), (), s32[]{:S(2)}) async-start(), calls=%async_computation.10 | async-start | bytes 9437184 | tf_op jit(solution)/shard_map/all_gather | solution.py:701
  68.5 2.3 copy-start.9
  68.5 2.3 copy-start.12
  68.5 3.0 copy-start.13
  68.5 3.7 copy-start.8
  70.7 183.4 %reduce-scatter.8.cloned.1.call-start = ((), (), s32[]{:S(2)}) async-start(), calls=%async_computation.11 | async-start | bytes 9437184 | tf_op jit(solution)/shard_map/reduce_scatter | solution.py:705
  182.7 118.9 %all-gather.17.cloned.1.call-start = ((), (), s32[]{:S(2)}) async-start(), calls=%async_computation.13 | async-start | bytes 2621440 | tf_op jit(solution)/shard_map/all_gather | solution.py:691
  183.3 164.5 %all-gather.19.cloned.1.call-start = ((), (), s32[]{:S(2)}) async-start(), calls=%async_computation.14 | async-start | bytes 2621440 | tf_op jit(solution)/shard_map/all_gather | solution.py:692
  183.8 210.1 %all-gather.21.cloned.1.call-start = ((), (), s32[]{:S(2)}) async-start(), calls=%async_computation.15 | async-start | bytes 2621440 | tf_op jit(solution)/shard_map/all_gather | solution.py:693
  184.4 264.7 %all-gather.15.cloned.1.call-start = ((), (), s32[]{:S(2)}) async-start(), calls=%async_computation.12 | async-start | bytes 9437184 | tf_op jit(solution)/shard_map/all_gather | solution.py:706
  185.2 412.9 %all-gather.23.cloned.1.call-start = ((), (), s32[]{:S(2)}) async-start(), calls=%async_computation.17 | async-start | bytes 9437184 | tf_op jit(solution)/shard_map/all_gather | solution.py:716
  543.5 172.8 %reduce-scatter.14.cloned.1.call-start = ((), (), s32[]{:S(2)}) async-start(), calls=%async_computation.19 | async-start | bytes 3932160 | tf_op jit(solution)/shard_map/reduce_scatter | solution.py:727
  605.9 34.1 %copy-start.3 = (bf16[2048,192]{1,0:T(8,128)(2,1)S(1)}, bf16[2048,192]{1,0:T(8,128)(2,1)}, u32[]{:S(2)}) copy-start(bf16[2048,192]{1,0:T(8,128)(2,1)} %get-tuple-element.27) | copy-start | bytes 2359300
  640.0 5.4 copy-start.14
  655.9 106.6 %reduce-scatter.16.cloned.1.call-start = ((), (), s32[]{:S(2)}) async-start(), calls=%async_computation.20 | async-start | bytes 2621440 | tf_op jit(solution)/shard_map/reduce_scatter | solution.py:713
  656.5 151.5 %reduce-scatter.18.cloned.1.call-start = ((), (), s32[]{:S(2)}) async-start(), calls=%async_computation.21 | async-start | bytes 2621440 | tf_op jit(solution)/shard_map/reduce_scatter | solution.py:714
  657.2 196.2 %reduce-scatter.20.cloned.1.call-start = ((), (), s32[]{:S(2)}) async-start(), calls=%async_computation.22 | async-start | bytes 2621440 | tf_op jit(solution)/shard_map/reduce_scatter | solution.py:715
  657.8 269.8 %reduce-scatter.12.cloned.1.call-start = ((), (), s32[]{:S(2)}) async-start(), calls=%async_computation.18 | async-start | bytes 9437184 | tf_op jit(solution)/shard_map/reduce_scatter | solution.py:720
  668.9 334.3 %reduce-scatter.10.cloned.1.call-start = ((), (), s32[]{:S(2)}) async-start(), calls=%async_computation.16 | async-start | bytes 9437184 | tf_op jit(solution)/shard_map/reduce_scatter | solution.py:711
  718.6 137.1 %all-to-all-start.1 = ((bf16[8,64,768]{2,1,0:T(8,128)(2,1)}), bf16[8,64,768]{2,1,0:T(8,128)(2,1)S(1)}, u32[]{:S(2)}, u32[]{:S(2)}) async-start(bf16[8,64,768]{2,1,0:T(8,128)(2,1)} %bitcast.22), calls=%async_computation.5 | async-start | bytes 1572864 | tf_op jit(solution)/shard_map/all_to_all | solution.py:728
  722.2 133.4 %copy-start.6 = (f32[128,128]{1,0:T(8,128)S(1)}, f32[128,128]{1,0:T(8,128)}, u32[]{:S(2)}) copy-start(f32[128,128]{1,0:T(8,128)} %get-tuple-element.39) | copy-start | bytes 196612
  861.6 1.5 copy-start.4
  862.1 67.4 %copy-start.7 = (f32[1,2048]{1,0:T(1,128)S(1)}, f32[1,2048]{1,0:T(1,128)}, u32[]{:S(2)}) copy-start(f32[1,2048]{1,0:T(1,128)} %get-tuple-element.38) | copy-start | bytes 24580
  862.1 141.1 %copy-start.2 = (bf16[256,2048]{1,0:T(8,128)(2,1)S(1)}, bf16[256,2048]{1,0:T(8,128)(2,1)}, u32[]{:S(2)}) copy-start(bf16[256,2048]{1,0:T(8,128)(2,1)} %reduce-scatter.8.cloned.1.call-done) | copy-start | bytes 3145732
  927.6 75.6 %copy-start.1 = (bf16[256,2048]{1,0:T(8,128)(2,1)S(1)}, bf16[256,2048]{1,0:T(8,128)(2,1)}, u32[]{:S(2)}) copy-start(bf16[256,2048]{1,0:T(8,128)(2,1)} %reduce-scatter.12.cloned.1.call-done) | copy-start | bytes 3145732
Sparse Core Ops, SparseCore 0:
  28.3 62.9 all-gather.10
  93.7 52.9 all-gather.12
  182.8 71.2 reduce-scatter.7
  255.6 45.9 all-gather.16
  303.1 44.6 all-gather.18
  349.3 44.6 all-gather.20
  396.0 53.0 all-gather.14
  543.6 54.3 all-gather.22
  656.0 60.2 reduce-scatter.13
  718.5 43.8 reduce-scatter.15
  764.7 43.1 reduce-scatter.17
  810.2 43.1 reduce-scatter.19
  856.9 70.6 reduce-scatter.11
  931.3 71.8 reduce-scatter.9

commit v3 on v2

v3 whole, which is shorter than its diff:
```python
import functools
import math

import jax
import jax.numpy as jnp
from jax import lax
from jax.experimental import pallas as pl
from jax.experimental.pallas import tpu as pltpu
from jax.sharding import PartitionSpec as P

QUERY_HEADS = 24
KEY_VALUE_HEADS = 6
GROUP = QUERY_HEADS // KEY_VALUE_HEADS
D = 64
HALF = D // 2
EPSILON = 1e-06
THETA = 10000.0
PENALTY = -10000.0
SEGMENT_KINDS = 8
TABLE_ROWS = 80
BLOCK = 512
PLANE = 8
F32 = jnp.float32
BF16 = jnp.bfloat16
VMEM_LIMIT = 60 * 1024 * 1024
MESH = pl.DeviceIdType.MESH
ANY_SPEC = pl.BlockSpec(memory_space=pl.ANY)
VMEM_SPEC = pl.BlockSpec(memory_space=pltpu.VMEM)


def dot(a, b):
    return jnp.dot(a, b, preferred_element_type=F32)


def dot_nt(a, b):
    return lax.dot_general(a, b, (((1,), (1,)), ((), ())), preferred_element_type=F32)


def dot_tn(a, b):
    return lax.dot_general(a, b, (((0,), (0,)), ((), ())), preferred_element_type=F32)


def norm_inverse(x):
    return lax.rsqrt(jnp.mean(x * x, axis=-1, keepdims=True) + EPSILON)


def split3(x):
    high = x.astype(BF16).astype(F32)
    mid = (x - high).astype(BF16).astype(F32)
    return high, mid, x - high - mid


def span(start, size):
    return pl.ds(pl.multiple_of(start, size), size)


class Heads:
    def __init__(self, seq):
        self.seq = seq
        self.queries = -(-QUERY_HEADS // seq)
        last = [min((s + 1) * self.queries, QUERY_HEADS) - 1 for s in range(seq)]
        self.pairs = max(last[s] // GROUP - self.first(s) + 1 for s in range(seq) if last[s] >= s * self.queries)
        self.wide = self.queries * D
        self.narrow = self.pairs * D
        self.qkv = self.wide + 2 * self.narrow
        self.columns = self.qkv + self.wide

    def first(self, s):
        return (s * self.queries) // GROUP

    def slot(self, s, h):
        return (s * self.queries + h) // GROUP - (s * self.queries) // GROUP


class Place:
    def __init__(self):
        self.row = lax.axis_index("rows")
        self.me = lax.axis_index("seq")
        self.core = lax.rem(self.me, 2)
        self.chip = self.me // 2
        self.sib = self.me + 1 - 2 * self.core
        chip = self.chip
        self.chips = (chip, chip + 1 - 2 * lax.rem(chip, 2), lax.rem(chip + 2, 4), 3 - chip)
        self.same = tuple(2 * q + self.core for q in self.chips)

    def greet(self):
        barrier = pltpu.get_barrier_semaphore()
        for other in (self.sib, self.same[1], self.same[2]):
            pl.semaphore_signal(barrier, inc=1, device_id=(self.row, other), device_id_type=MESH)
        pl.semaphore_wait(barrier, 3)

    def greet_all(self, rows):
        barrier = pltpu.get_barrier_semaphore()
        for j in range(1, PLANE):
            other = lax.rem(self.me + j, PLANE)
            pl.semaphore_signal(barrier, inc=1, device_id=(self.row, other), device_id_type=MESH)
        for j in range(1, rows):
            other = lax.rem(self.row + j, rows)
            pl.semaphore_signal(barrier, inc=1, device_id=(other, self.me), device_id_type=MESH)
        pl.semaphore_wait(barrier, PLANE - 1 + rows - 1)

    def send(self, src, dst, send_sem, recv_sem, slot, target):
        return pltpu.make_async_remote_copy(
            src_ref=src, dst_ref=dst, send_sem=send_sem.at[slot], recv_sem=recv_sem.at[slot],
            device_id=(self.row, target), device_id_type=MESH)


GATHER_SLOTS = 10


class Gather:
    def __init__(self, place, own, every, send_sem, recv_sem):
        half = every.shape[1] // 2
        low, high, whole = slice(0, half), slice(half, 2 * half), slice(0, 2 * half)

        def send(part, b, slot, target, src=None):
            src = every.at[b, part] if src is None else src.at[part]
            return place.send(src, every.at[b, part], send_sem, recv_sem, slot, target)

        me, (_, s1, s2, s3), sib = place.me, place.same, place.sib
        self.copies = (
            send(whole, me, 0, sib, own),
            send(low, me, 1, s1, own), send(high, me, 2, s1, own),
            send(high, me, 3, s2, own), send(low, me, 4, s2, own),
            send(low, s1, 5, s2), send(high, s2, 6, s1),
            send(whole, s1, 7, sib), send(whole, s2, 8, sib), send(whole, s3, 9, sib),
        )

    def start(self):
        for slot in (1, 3, 2, 4, 0):
            self.copies[slot].start()

    def own_chip(self):
        self.copies[0].wait_recv()

    def neighbours(self):
        c = self.copies
        c[1].wait_recv()
        c[5].start()
        c[3].wait_recv()
        c[6].start()
        c[2].wait_recv()
        c[7].start()
        c[4].wait_recv()
        c[8].start()

    def chip1(self):
        self.copies[7].wait_recv()

    def chip2(self):
        self.copies[8].wait_recv()

    def diagonal(self):
        c = self.copies
        c[5].wait_recv()
        c[6].wait_recv()
        c[9].start()

    def chip3(self):
        self.copies[9].wait_recv()

    def close(self):
        for copy in self.copies:
            copy.wait_send()


SCATTER_SLOTS = 10


class Scatter:
    def __init__(self, place, part, sibling, passing, final, send_sem, recv_sem):
        self.place, self.part, self.sibling, self.passing, self.final = place, part, sibling, passing, final
        half = part.shape[2] // 2
        self.half = half
        core, other = place.core, 1 - place.core
        _, s1, s2, _ = place.same
        send = lambda src, dst, slot, target: place.send(src, dst, send_sem, recv_sem, slot, target)
        low, high = slice(0, half), slice(half, 2 * half)
        self.exchange = tuple(send(part.at[k, other], sibling.at[k], k, place.sib) for k in range(4))
        self.pass1 = send(part.at[3, core, low], passing.at[0], 4, s1)
        self.pass2 = send(part.at[3, core, high], passing.at[1], 5, s2)
        self.first1 = send(part.at[1, core, low], final.at[0, low], 6, s1)
        self.second1 = send(part.at[1, core, high], final.at[0, high], 7, s1)
        self.first2 = send(part.at[2, core, high], final.at[1, high], 8, s2)
        self.second2 = send(part.at[2, core, low], final.at[1, low], 9, s2)

    def add(self, k, start, size, term, offset):
        core, step = self.place.core, 64

        def one(i, _):
            rows = pl.ds(pl.multiple_of(start + i * step, step), step)
            from_rows = pl.ds(pl.multiple_of(offset + i * step, step), step)
            total = self.part[k, core, rows, :].astype(F32) + term[from_rows, :].astype(F32)
            self.part[k, core, rows, :] = total.astype(BF16)
            return 0

        lax.fori_loop(0, size // step, one, 0)

    def combine(self, k):
        self.exchange[k].wait_recv()
        self.add(k, 0, 2 * self.half, self.sibling.at[k], 0)

    def finish_two(self):
        self.pass1.wait_recv()
        self.add(2, 0, self.half, self.passing.at[0], 0)
        self.second2.start()
        self.pass2.wait_recv()
        self.add(1, self.half, self.half, self.passing.at[1], 0)
        self.second1.start()

    def arrive(self):
        for copy in (self.first1, self.second1, self.first2, self.second2):
            copy.wait_recv()

    def total(self, rows):
        return (self.part[0, self.place.core, rows, :].astype(F32) + self.final[0, rows, :].astype(F32)
                + self.final[1, rows, :].astype(F32))

    def close(self):
        for copy in self.exchange + (self.pass1, self.pass2, self.first1, self.second1, self.first2, self.second2):
            copy.wait_send()


def scatter_scratch(tok, width):
    return [
        pltpu.VMEM((4, 2, tok, width), BF16),
        pltpu.VMEM((4, tok, width), BF16),
        pltpu.VMEM((2, tok // 2, width), BF16),
        pltpu.VMEM((2, tok, width), BF16),
        pltpu.SemaphoreType.DMA((SCATTER_SLOTS,)),
        pltpu.SemaphoreType.DMA((SCATTER_SLOTS,)),
    ]


def start_kernel(x_hbm, table_hbm, pieces_hbm, gain_hbm, x_all, table_all, w_all, gain_all,
                 x_send, x_recv, t_send, t_recv, p_send, p_recv, g_send, g_recv, z_send, z_recv, local_sem):
    place = Place()
    rows = w_all.shape[0]
    me, row = place.me, place.row
    local = [pltpu.make_async_copy(src, dst, local_sem.at[i]) for i, (src, dst) in enumerate((
        (pieces_hbm.at[me], w_all.at[row, me]), (gain_hbm, gain_all.at[row, me]),
        (x_hbm, x_all.at[me]), (table_hbm, table_all.at[me])))]
    for copy in local:
        copy.start()
    place.greet_all(rows)
    exchange = []
    for j in range(1, PLANE):
        other = lax.rem(me + j, PLANE)
        exchange.append(place.send(pieces_hbm.at[other], w_all.at[row, me], p_send, p_recv, j, other))
        exchange.append(place.send(gain_hbm, gain_all.at[row, me], g_send, g_recv, j, other))
    for copy in exchange:
        copy.start()
    gathers = (Gather(place, x_hbm, x_all, x_send, x_recv), Gather(place, table_hbm, table_all, t_send, t_recv))
    gathers[1].start()
    gathers[0].start()
    for copy in local[:2]:
        copy.wait()
    for copy in exchange:
        copy.wait_recv()
    along = []
    for j in range(1, rows):
        other = lax.rem(row + j, rows)
        for i, every in enumerate((w_all, gain_all)):
            along.append(pltpu.make_async_remote_copy(
                src_ref=every.at[row], dst_ref=every.at[row], send_sem=z_send.at[2 * j + i], recv_sem=z_recv.at[2 * j + i],
                device_id=(other, me), device_id_type=MESH))
    for copy in along:
        copy.start()
    for name in ("own_chip", "neighbours", "chip1", "chip2", "diagonal", "chip3"):
        for gather in gathers[::-1]:
            getattr(gather, name)()
    for copy in local[2:]:
        copy.wait()
    for copy in along:
        copy.wait_recv()
    for copy in exchange + along:
        copy.wait_send()
    for gather in gathers:
        gather.close()


def start_phase(rows, x, table, pieces, gain):
    tok, model = x.shape
    dma = pltpu.SemaphoreType.DMA
    return pl.pallas_call(
        start_kernel,
        out_shape=(
            jax.ShapeDtypeStruct((PLANE, tok, model), BF16),
            jax.ShapeDtypeStruct((PLANE,) + table.shape, F32),
            jax.ShapeDtypeStruct((rows,) + pieces.shape, BF16),
            jax.ShapeDtypeStruct((rows, PLANE) + gain.shape, F32),
        ),
        in_specs=[ANY_SPEC] * 4,
        out_specs=(ANY_SPEC,) * 4,
        scratch_shapes=[dma((GATHER_SLOTS,))] * 4 + [dma((PLANE,))] * 4 + [dma((2 * rows,))] * 2 + [dma((4,))],
        compiler_params=pltpu.CompilerParams(collective_id=0, has_side_effects=True),
        cost_estimate=pl.CostEstimate(flops=0, bytes_accessed=160 << 20, transcendentals=0),
    )(x, table, pieces, gain)


class Forward:
    def __init__(self, heads, me, table, gq, gk, raw, merged, o, qa, ka, kt, vt, inv):
        self.heads, self.table, self.gq, self.gk = heads, table, gq[...], gk[...]
        self.raw, self.merged, self.o, self.qa, self.ka, self.kt, self.vt, self.inv = raw, merged, o, qa, ka, kt, vt, inv
        self.slots = [heads.slot(me, h) for h in range(heads.queries)]

    def prepare(self, b, projected):
        heads = self.heads
        tok = self.table.shape[2]
        lanes = span(b * tok, tok)
        cos = self.table[b, 0:HALF, :]
        sin = self.table[b, HALF:D, :]
        hot = self.table[b, D:D + 8, :]
        row = lax.broadcasted_iota(jnp.int32, (16, tok), 0)
        one_row = jnp.where(row == 0, 1.0, 0.0).astype(F32)
        penalty = jnp.concatenate([(1.0 - hot) * PENALTY, jnp.zeros((8, tok), F32)], axis=0).astype(BF16)
        self.raw[:, lanes] = projected[:heads.wide + heads.narrow]

        def rotated(raw, gain):
            inv = lax.rsqrt(jnp.mean(raw * raw, axis=0, keepdims=True) + EPSILON)
            n = raw * inv * gain
            a, c = n[:HALF], n[HALF:]
            return inv, jnp.concatenate([a * cos - c * sin, c * cos + a * sin], axis=0)

        for h in range(heads.queries):
            inv, q = rotated(projected[h * D:(h + 1) * D], self.gq)
            self.inv[h:h + 1, lanes] = inv
            self.qa[h, :, lanes] = jnp.concatenate([(q * (D ** -0.5)).astype(BF16), penalty], axis=0)
        for g in range(heads.pairs):
            start = heads.wide + g * D
            inv, k = rotated(projected[start:start + D], self.gk)
            self.inv[heads.queries + g:heads.queries + g + 1, lanes] = inv
            self.kt[g, :, lanes] = k.astype(BF16)
            full = jnp.concatenate([k, hot, jnp.ones((8, tok), F32), jnp.zeros((48, tok), F32)], axis=0)
            self.ka[g, lanes, :] = jnp.transpose(full).astype(BF16)
            start += heads.narrow
            self.vt[g, :, lanes] = jnp.concatenate([projected[start:start + D], one_row], axis=0).astype(BF16)

    def query_block(self, i):
        heads = self.heads
        cols = span(i * BLOCK, BLOCK)
        causal = (lax.broadcasted_iota(jnp.int32, (BLOCK, BLOCK), 0)
                  <= lax.broadcasted_iota(jnp.int32, (BLOCK, BLOCK), 1))

        def step(j, accs, diagonal):
            rows = span(j * BLOCK, BLOCK)
            new = []
            for h in range(heads.queries):
                slot = self.slots[h]
                p = jnp.exp(dot(self.ka[slot, rows, 0:80], self.qa[h, :, cols]))
                if diagonal:
                    p = jnp.where(causal, p, 0.0)
                new.append(accs[h] + dot(self.vt[slot, :, rows], p.astype(BF16)))
            return tuple(new)

        accs = tuple(jnp.zeros((80, BLOCK), F32) for _ in range(heads.queries))
        accs = lax.fori_loop(0, i, lambda j, c: step(j, c, False), accs)
        accs = step(i, accs, True)
        row = lax.broadcasted_iota(jnp.int32, (16, BLOCK), 0)
        lead = self.merged.shape[1] - heads.wide
        outs = [jnp.zeros((lead, BLOCK), F32)] if lead else []
        for h in range(heads.queries):
            total = accs[h][D:D + 1]
            o = accs[h][:D] * (1.0 / total)
            self.o[h, :, cols] = o
            outs.append(o)
            pieces = split3(-jnp.log(total))
            old = self.qa[h, 64:80, cols].astype(F32)
            extra = jnp.where(row == 8, pieces[0],
                              jnp.where(row == 9, pieces[1], jnp.where(row == 10, pieces[2], old)))
            self.qa[h, 64:80, cols] = extra.astype(BF16)
        merged = jnp.transpose(jnp.concatenate(outs, axis=0)).astype(BF16)
        self.merged[cols, :] = merged
        return merged


class Backward:
    def __init__(self, heads, me, table, gq, gk, raw, o, qa, ka, kt, vt, inv, doa, dopad, qpad, va, dq, acc):
        self.heads, self.table, self.gq, self.gk = heads, table, gq[...], gk[...]
        self.raw, self.o, self.qa, self.ka, self.kt, self.vt, self.inv = raw, o, qa, ka, kt, vt, inv
        self.doa, self.dopad, self.qpad, self.va, self.dq, self.acc = doa, dopad, qpad, va, dq, acc
        self.slots = [heads.slot(me, h) for h in range(heads.queries)]

    def prepare(self, b):
        heads = self.heads
        tok = self.table.shape[2]
        lanes = span(b * tok, tok)
        for h in range(heads.queries):
            q = jnp.concatenate([jnp.zeros((D, tok), F32), self.qa[h, 0:D, lanes].astype(F32)], axis=0)
            self.qpad[h, lanes, :] = jnp.transpose(q).astype(BF16)
            self.acc[h, lanes, :] = jnp.zeros((tok, 2 * D), F32)
        for g in range(heads.pairs):
            v = jnp.concatenate([self.vt[g, 0:D, lanes].astype(F32), jnp.ones((D, tok), F32)], axis=0)
            self.va[g, lanes, :] = jnp.transpose(v).astype(BF16)

    def gradient(self, b, dm):
        heads = self.heads
        tok = self.table.shape[2]
        lanes = span(b * tok, tok)
        row = lax.broadcasted_iota(jnp.int32, (16, tok), 0)
        dmt = jnp.transpose(dm.astype(BF16).astype(F32))
        for h in range(heads.queries):
            do = dmt[h * D:(h + 1) * D]
            delta = jnp.sum(do * self.o[h, :, lanes], axis=0, keepdims=True)
            pieces = split3(-delta)
            extra = jnp.where(row == 0, pieces[0],
                              jnp.where(row == 1, pieces[1], jnp.where(row == 2, pieces[2], 0.0)))
            self.doa[h, :, lanes] = jnp.concatenate([do, extra], axis=0).astype(BF16)
            both = jnp.concatenate([do, jnp.zeros((D, tok), F32)], axis=0)
            self.dopad[h, lanes, :] = jnp.transpose(both).astype(BF16)

    def query_block(self, i):
        heads = self.heads
        cols = span(i * BLOCK, BLOCK)
        causal = (lax.broadcasted_iota(jnp.int32, (BLOCK, BLOCK), 0)
                  <= lax.broadcasted_iota(jnp.int32, (BLOCK, BLOCK), 1))

        def step(j, accs, diagonal):
            rows = span(j * BLOCK, BLOCK)
            new = []
            for h in range(heads.queries):
                slot = self.slots[h]
                p = jnp.exp(dot(self.ka[slot, rows, 0:80], self.qa[h, :, cols]))
                if diagonal:
                    p = jnp.where(causal, p, 0.0)
                dp = dot(self.va[slot, rows, 0:80], self.doa[h, :, cols])
                ds = (p * dp).astype(BF16)
                self.acc[h, rows, :] += dot(p.astype(BF16), self.dopad[h, cols, :]) + dot(ds, self.qpad[h, cols, :])
                new.append(accs[h] + dot(self.kt[slot, :, rows], ds))
            return tuple(new)

        accs = tuple(jnp.zeros((D, BLOCK), F32) for _ in range(heads.queries))
        accs = lax.fori_loop(0, i, lambda j, c: step(j, c, False), accs)
        accs = step(i, accs, True)
        for h in range(heads.queries):
            self.dq[h, :, cols] = accs[h]

    def finish(self, b, sums):
        heads = self.heads
        tok = self.table.shape[2]
        lanes = span(b * tok, tok)
        cos = self.table[b, 0:HALF, :]
        sin = self.table[b, HALF:D, :]
        scale = self.table[b, 72:73, :]

        def back(grad, raw, inv, gain):
            a, c = grad[:HALF], grad[HALF:]
            n = jnp.concatenate([a * cos + c * sin, c * cos - a * sin], axis=0)
            v = n * gain
            out = inv * v - raw * (inv * inv * inv) * jnp.mean(v * raw, axis=0, keepdims=True)
            return out * scale, n * raw * inv

        sum_q, sum_k = sums
        pairs = [jnp.zeros((2 * D, tok), F32) for _ in range(heads.pairs)]
        out = []
        for h in range(heads.queries):
            raw = self.raw[h * D:(h + 1) * D, lanes]
            grad, part = back(self.dq[h, :, lanes] * (D ** -0.5), raw, self.inv[h:h + 1, lanes], self.gq)
            out.append(grad)
            sum_q = sum_q + part
            both = jnp.transpose(self.acc[h, lanes, :])
            for g in range(heads.pairs):
                pairs[g] = pairs[g] + jnp.where(self.slots[h] == g, both, 0.0)
        for g in range(heads.pairs):
            start = heads.wide + g * D
            raw = self.raw[start:start + D, lanes]
            inv = self.inv[heads.queries + g:heads.queries + g + 1, lanes]
            grad, part = back(pairs[g][D:], raw, inv, self.gk)
            out.append(grad)
            sum_k = sum_k + part
        for g in range(heads.pairs):
            out.append(pairs[g][:D] * scale)
        return jnp.concatenate(out, axis=0), (sum_q, sum_k)


def kept_shapes(heads, length, lead):
    return (
        jax.ShapeDtypeStruct((heads.wide + heads.narrow, length), F32),
        jax.ShapeDtypeStruct((length, lead + heads.wide), BF16),
        jax.ShapeDtypeStruct((heads.queries, D, length), F32),
        jax.ShapeDtypeStruct((heads.queries, 80, length), BF16),
        jax.ShapeDtypeStruct((heads.pairs, length, 128), BF16),
        jax.ShapeDtypeStruct((heads.pairs, D, length), BF16),
        jax.ShapeDtypeStruct((heads.pairs, 80, length), BF16),
        jax.ShapeDtypeStruct((8, length), F32),
    )


def backward_scratch(heads, length):
    return [
        pltpu.VMEM((heads.queries, 80, length), BF16),
        pltpu.VMEM((heads.queries, length, 2 * D), BF16),
        pltpu.VMEM((heads.queries, length, 2 * D), BF16),
        pltpu.VMEM((heads.pairs, length, 2 * D), BF16),
        pltpu.VMEM((heads.queries, D, length), F32),
        pltpu.VMEM((heads.queries, length, 2 * D), F32),
    ]


def local_forward_kernel(heads, proj_ref, table_ref, gq_ref, gk_ref, *kept):
    forward = Forward(heads, lax.axis_index("seq"), table_ref, gq_ref, gk_ref, *kept)
    blocks, _, tok = table_ref.shape

    def prepare(b, _):
        rows = span(b * tok, tok)
        forward.prepare(b, jnp.transpose(proj_ref[rows, :]) * table_ref[b, 72:73, :])
        return 0

    def query_block(i, _):
        forward.query_block(i)
        return 0

    lax.fori_loop(0, blocks, prepare, 0)
    lax.fori_loop(0, blocks * tok // BLOCK, query_block, 0)


def local_backward_kernel(heads, dm_ref, table_ref, gq_ref, gk_ref, raw_ref, o_ref, qa_ref, ka_ref, kt_ref, vt_ref, inv_ref,
                          pg_ref, gains_ref, *scratch):
    backward = Backward(heads, lax.axis_index("seq"), table_ref, gq_ref, gk_ref, raw_ref, o_ref, qa_ref, ka_ref, kt_ref,
                        vt_ref, inv_ref, *scratch)
    blocks, _, tok = table_ref.shape

    def prepare(b, _):
        backward.prepare(b)
        backward.gradient(b, dm_ref[span(b * tok, tok), :])
        return 0

    def query_block(i, _):
        backward.query_block(i)
        return 0

    def finish(b, sums):
        grad, sums = backward.finish(b, sums)
        pg_ref[span(b * tok, tok), :] = jnp.transpose(grad).astype(BF16)
        return sums

    lax.fori_loop(0, blocks, prepare, 0)
    lax.fori_loop(0, blocks * tok // BLOCK, query_block, 0)
    zero = jnp.zeros((D, tok), F32)
    sum_q, sum_k = lax.fori_loop(0, blocks, finish, (zero, zero))
    gains_ref[0:D, :] = jnp.broadcast_to(jnp.sum(sum_q, axis=1, keepdims=True), (D, 128))
    gains_ref[D:2 * D, :] = jnp.broadcast_to(jnp.sum(sum_k, axis=1, keepdims=True), (D, 128))


def attention_kernel(heads, x_hbm, g_hbm, w_hbm, table_ref, gq_ref, gk_ref,
                     res_ref, g_all, raw_ref, merged_ref, o_ref, qa_ref, ka_ref, kt_ref, vt_ref, inv_ref,
                     x_ref, w_ref, part_ref, sibling_ref, passing_ref, final_ref, rs_send, rs_recv,
                     ag_send, ag_recv, load_sem):
    place = Place()
    blocks, tok, model = x_ref.shape
    load_w = pltpu.make_async_copy(w_hbm, w_ref, load_sem.at[blocks])
    load_w.start()
    loads = [pltpu.make_async_copy(x_hbm.at[b], x_ref.at[b], load_sem.at[b]) for b in range(blocks)]
    for copy in loads:
        copy.start()
    keep_own = pltpu.make_async_copy(g_hbm, g_all.at[place.me], load_sem.at[blocks + 1])
    keep_own.start()
    place.greet()
    gather = Gather(place, g_hbm, g_all, ag_send, ag_recv)
    scatter = Scatter(place, part_ref, sibling_ref, passing_ref, final_ref, rs_send, rs_recv)
    gather.start()
    forward = Forward(heads, place.me, table_ref, gq_ref, gk_ref, raw_ref, merged_ref, o_ref, qa_ref, ka_ref, kt_ref,
                      vt_ref, inv_ref)
    load_w.wait()
    for copy in loads:
        copy.wait()

    def prepare(b, _):
        proj = dot(x_ref[b], w_ref[:, 0:512])
        forward.prepare(b, jnp.transpose(proj) * table_ref[b, 72:73, :])
        return 0

    lax.fori_loop(0, blocks, prepare, 0)
    tile = 512

    def compute(k):
        merged = forward.query_block(place.chips[k])

        def model_tile(n, _):
            cols = span(n * tile, tile)
            out = dot_nt(merged_ref[span(place.chips[k] * BLOCK, BLOCK), :], w_ref[cols, 384:640])
            part_ref[k, :, :, cols] = out.astype(BF16).reshape(2, tok, tile)
            return 0

        lax.fori_loop(0, model // tile, model_tile, 0)
        scatter.exchange[k].start()

    compute(3)
    gather.own_chip()
    gather.neighbours()
    scatter.combine(3)
    scatter.pass1.start()
    scatter.pass2.start()
    compute(1)
    scatter.combine(1)
    scatter.first1.start()
    gather.chip1()
    gather.chip2()
    compute(2)
    scatter.combine(2)
    scatter.first2.start()
    gather.diagonal()
    compute(0)
    scatter.combine(0)
    scatter.finish_two()
    gather.chip3()
    scatter.arrive()

    def finish(i, _):
        rows = span(i * 32, 32)
        res_ref[rows, :] = x_ref[place.me, rows, :].astype(F32) + scatter.total(rows)
        return 0

    lax.fori_loop(0, tok // 32, finish, 0)
    keep_own.wait()
    gather.close()
    scatter.close()


def attention_phase(heads, x_all, g, w, table, gq, gk):
    blocks, tok, model = x_all.shape
    dma = pltpu.SemaphoreType.DMA
    lead = 256 - heads.wide
    kept = kept_shapes(heads, blocks * tok, lead)
    return pl.pallas_call(
        functools.partial(attention_kernel, heads),
        out_shape=(jax.ShapeDtypeStruct((tok, model), F32), jax.ShapeDtypeStruct((blocks, tok, model), BF16)) + kept,
        in_specs=[ANY_SPEC] * 3 + [VMEM_SPEC] * 3,
        out_specs=(VMEM_SPEC, ANY_SPEC) + (VMEM_SPEC,) * len(kept),
        scratch_shapes=[
            pltpu.VMEM((blocks, tok, model), BF16),
            pltpu.VMEM((model, heads.columns), BF16),
            *scatter_scratch(tok, model),
            dma((GATHER_SLOTS,)), dma((GATHER_SLOTS,)), dma((blocks + 2,)),
        ],
        compiler_params=pltpu.CompilerParams(collective_id=1, has_side_effects=True, vmem_limit_bytes=VMEM_LIMIT),
        cost_estimate=pl.CostEstimate(flops=40 << 30, bytes_accessed=64 << 20, transcendentals=0),
    )(x_all, g, w, table, gq, gk)


def ffn_kernel(res_ref, gain_ref, g_hbm, gate_hbm, up_hbm, down_hbm,
               out_hbm, rgrad_ref, branch_ref, gain_grad_ref, gate_grad_hbm, up_grad_hbm, down_grad_hbm,
               two_ref, g_ref, gate_ref, up_ref, down_ref, hid_ref, gu_ref, stage_ref, wstage_ref,
               part_ref, sibling_ref, passing_ref, final_ref, rs_send, rs_recv,
               ag_send, ag_recv, load_sem, stage_sem, wstage_sem):
    place = Place()
    _, tok, model = g_ref.shape
    ff = gate_ref.shape[1]
    tile = 256
    loads = [pltpu.make_async_copy(src, dst, load_sem.at[i]) for i, (src, dst) in enumerate(
        ((gate_hbm, gate_ref), (up_hbm, up_ref), (g_hbm, g_ref), (down_hbm, down_ref)))]
    for copy in loads:
        copy.start()

    def norm_rows(i, _):
        rows = pl.ds(pl.multiple_of(i * 32, 32), 32)
        res = res_ref[rows, :]
        inv = lax.rsqrt(jnp.mean(res * res, axis=-1, keepdims=True) + EPSILON)
        two_ref[place.me, rows, :] = (res * inv * gain_ref[...]).astype(BF16)
        return 0

    lax.fori_loop(0, tok // 32, norm_rows, 0)
    place.greet()
    gather = Gather(place, two_ref.at[place.me], two_ref, ag_send, ag_recv)
    scatter = Scatter(place, part_ref, sibling_ref, passing_ref, final_ref, rs_send, rs_recv)
    gather.start()
    for copy in loads:
        copy.wait()

    def stage_copy(k):
        return pltpu.make_async_copy(stage_ref.at[k % 2], out_hbm.at[k], stage_sem.at[k % 2])

    def compute(k):
        m = place.chips[k]
        pair = pl.ds(2 * m, 2)

        def hidden_tile(h, _):
            cols = pl.ds(pl.multiple_of(h * tile, tile), tile)
            cols2 = pl.ds(pl.multiple_of(ff + h * tile, tile), tile)
            x = two_ref[pair].reshape(2 * tok, model)
            gate = dot(x, gate_ref[:, cols])
            up = dot(x, up_ref[:, cols])
            back = dot_nt(g_ref[pair].reshape(2 * tok, model), down_ref[cols, :])
            s = 1.0 / (1.0 + jnp.exp(-gate))
            act = gate * s
            hid_ref[pair, :, cols] = (act * up).astype(BF16).reshape(2, tok, tile)
            gu_ref[pair, :, cols] = (back * up * s * (1.0 + gate * (1.0 - s))).astype(BF16).reshape(2, tok, tile)
            gu_ref[pair, :, cols2] = (back * act).astype(BF16).reshape(2, tok, tile)
            return 0

        lax.fori_loop(0, ff // tile, hidden_tile, 0)
        if k >= 2:
            stage_copy(k - 2).wait()

        def model_tile(n, _):
            cols = pl.ds(pl.multiple_of(n * tile, tile), tile)
            gg = gu_ref[pair, :, 0:ff].reshape(2 * tok, ff)
            ug = gu_ref[pair, :, ff:2 * ff].reshape(2 * tok, ff)
            back = dot_nt(gg, gate_ref[cols, :]) + dot_nt(ug, up_ref[cols, :])
            part_ref[k, :, :, cols] = back.astype(BF16).reshape(2, tok, tile)
            return 0

        lax.fori_loop(0, model // tile, model_tile, 0)
        scatter.exchange[k].start()

        def out_tile(n, _):
            cols = pl.ds(pl.multiple_of(n * tile, tile), tile)
            hid = hid_ref[pair].reshape(2 * tok, ff)
            out = dot(hid, down_ref[:, cols])
            stage_ref[k % 2, :, :, cols] = out.astype(BF16).reshape(2, tok, tile)
            return 0

        lax.fori_loop(0, model // tile, out_tile, 0)
        stage_copy(k).start()

    gather.own_chip()
    compute(0)
    gather.neighbours()
    gather.chip1()
    compute(1)
    gather.chip2()
    scatter.combine(1)
    scatter.first1.start()
    compute(2)
    gather.diagonal()
    scatter.combine(2)
    scatter.first2.start()
    gather.chip3()
    compute(3)
    scatter.combine(3)
    scatter.pass1.start()
    scatter.pass2.start()
    scatter.combine(0)

    blocks = two_ref.shape[0]

    def wstage_copies(i, slot):
        rows = pl.ds(pl.multiple_of(i * tile, tile), tile)
        return (pltpu.make_async_copy(wstage_ref.at[slot, :, 0:ff], gate_grad_hbm.at[rows], wstage_sem.at[slot, 0]),
                pltpu.make_async_copy(wstage_ref.at[slot, :, ff:2 * ff], up_grad_hbm.at[rows], wstage_sem.at[slot, 1]))

    def gate_up_rows(i, _):
        cols = pl.ds(pl.multiple_of(i * tile, tile), tile)
        slot = lax.rem(i, 2)

        @pl.when(i >= 2)
        def _():
            for copy in wstage_copies(i - 2, slot):
                copy.wait()

        x = two_ref[:, :, cols].reshape(blocks * tok, tile)
        wstage_ref[slot] = dot_tn(x, gu_ref[...].reshape(blocks * tok, 2 * ff)).astype(BF16)
        for copy in wstage_copies(i, slot):
            copy.start()
        return 0

    count = model // tile
    lax.fori_loop(0, count // 2, gate_up_rows, 0)
    scatter.finish_two()
    lax.fori_loop(count // 2, count, gate_up_rows, 0)
    for i in (count - 2, count - 1):
        for copy in wstage_copies(i, i % 2):
            copy.wait()

    stage_copy(2).wait()
    stage_copy(3).wait()

    def down_rows(i, _):
        rows = pl.ds(pl.multiple_of(i * tile, tile), tile)
        h = hid_ref[:, :, rows].reshape(blocks * tok, tile)

        def down_cols(n, _):
            cols = pl.ds(pl.multiple_of(n * 512, 512), 512)
            g = g_ref[:, :, cols].reshape(blocks * tok, 512)
            stage_ref[0, i, :, cols] = dot_tn(h, g).astype(BF16)
            return 0

        lax.fori_loop(0, model // 512, down_cols, 0)
        return 0

    lax.fori_loop(0, ff // tile, down_rows, 0)
    down_out = [pltpu.make_async_copy(stage_ref.at[0, i], down_grad_hbm.at[pl.ds(i * tile, tile)], stage_sem.at[i])
                for i in range(ff // tile)]
    for copy in down_out:
        copy.start()

    scatter.arrive()

    def finish(i, sums):
        rows = pl.ds(pl.multiple_of(i * 32, 32), 32)
        res = res_ref[rows, :]
        inv = lax.rsqrt(jnp.mean(res * res, axis=-1, keepdims=True) + EPSILON)
        grad = scatter.total(rows)
        v = grad * gain_ref[...]
        mean = jnp.mean(v * res, axis=-1, keepdims=True)
        out = g_ref[place.me, rows, :].astype(F32) + inv * v - res * (inv * inv * inv * mean)
        rgrad_ref[rows, :] = out
        branch_ref[rows, :] = out.astype(BF16)
        return sums + jnp.sum(grad * res * inv, axis=0, keepdims=True)

    gain_grad_ref[...] = lax.fori_loop(0, tok // 32, finish, jnp.zeros((1, model), F32))
    for copy in down_out:
        copy.wait()
    gather.close()
    scatter.close()


def feed_forward(res, gain, g_all, gate, up, down):
    tok, model = res.shape
    ff = gate.shape[1]
    blocks = g_all.shape[0]
    any_spec = pl.BlockSpec(memory_space=pl.ANY)
    vmem = pl.BlockSpec(memory_space=pltpu.VMEM)
    return pl.pallas_call(
        ffn_kernel,
        out_shape=(
            jax.ShapeDtypeStruct((4, 2, tok, model), BF16),
            jax.ShapeDtypeStruct((tok, model), F32),
            jax.ShapeDtypeStruct((tok, model), BF16),
            jax.ShapeDtypeStruct((1, model), F32),
            jax.ShapeDtypeStruct((model, ff), BF16),
            jax.ShapeDtypeStruct((model, ff), BF16),
            jax.ShapeDtypeStruct((ff, model), BF16),
        ),
        in_specs=[vmem, vmem] + [any_spec] * 4,
        out_specs=(any_spec, vmem, vmem, vmem, any_spec, any_spec, any_spec),
        scratch_shapes=[
            pltpu.VMEM((blocks, tok, model), BF16),
            pltpu.VMEM((blocks, tok, model), BF16),
            pltpu.VMEM((model, ff), BF16),
            pltpu.VMEM((model, ff), BF16),
            pltpu.VMEM((ff, model), BF16),
            pltpu.VMEM((blocks, tok, ff), BF16),
            pltpu.VMEM((blocks, tok, 2 * ff), BF16),
            pltpu.VMEM((2, 2, tok, model), BF16),
            pltpu.VMEM((2, 256, 2 * ff), BF16),
            *scatter_scratch(tok, model),
            pltpu.SemaphoreType.DMA((GATHER_SLOTS,)),
            pltpu.SemaphoreType.DMA((GATHER_SLOTS,)),
            pltpu.SemaphoreType.DMA((4,)),
            pltpu.SemaphoreType.DMA((2,)),
            pltpu.SemaphoreType.DMA((2, 2)),
        ],
        compiler_params=pltpu.CompilerParams(collective_id=2, has_side_effects=True, vmem_limit_bytes=60 * 1024 * 1024),
        cost_estimate=pl.CostEstimate(flops=18 * blocks * tok * model * ff, bytes_accessed=64 << 20, transcendentals=0),
    )(res, gain, g_all, gate, up, down)


def backward_kernel(heads, branch_hbm, out_hbm, x_hbm, w_hbm, table_ref, gq_ref, gk_ref, merged_hbm,
                    raw_ref, o_ref, qa_ref, ka_ref, kt_ref, vt_ref, inv_ref,
                    ysum_ref, outsum_ref, grad_hbm, gains_ref,
                    every_ref, w_ref, pg_ref, merged_ref, xt_ref, wstage_ref,
                    doa_ref, dopad_ref, qpad_ref, va_ref, dq_ref, acc_ref,
                    part_ref, sibling_ref, passing_ref, final_ref, rs_send, rs_recv, rs2_send, rs2_recv,
                    ag_send, ag_recv, load_sem, xt_sem, wstage_sem, ready_sem):
    place = Place()
    blocks, tok, model = every_ref.shape
    load_w = pltpu.make_async_copy(w_hbm, w_ref, load_sem.at[0])
    load_out = pltpu.make_async_copy(out_hbm, part_ref, load_sem.at[1])
    load_own = pltpu.make_async_copy(branch_hbm, every_ref.at[place.me], load_sem.at[2])
    load_merged = pltpu.make_async_copy(merged_hbm, merged_ref, load_sem.at[3])
    load_own.start()
    load_w.start()
    load_out.start()
    load_merged.start()
    place.greet()
    gather = Gather(place, branch_hbm, every_ref, ag_send, ag_recv)
    gather.start()
    first = Scatter(place, part_ref, sibling_ref, passing_ref, final_ref, rs_send, rs_recv)
    second = Scatter(place, part_ref, sibling_ref, passing_ref, final_ref, rs2_send, rs2_recv)
    back = Backward(heads, place.me, table_ref, gq_ref, gk_ref, raw_ref, o_ref, qa_ref, ka_ref, kt_ref, vt_ref, inv_ref,
                    doa_ref, dopad_ref, qpad_ref, va_ref, dq_ref, acc_ref)
    lead = 256 - heads.wide

    def prepare(b, _):
        back.prepare(b)
        return 0

    lax.fori_loop(0, blocks, prepare, 0)
    load_out.wait()
    for copy in first.exchange:
        copy.start()
    load_w.wait()
    load_own.wait()

    def compute(k):
        m = place.chips[k]

        def gradient(j, _):
            b = 2 * m + j
            dm = dot(every_ref[b], w_ref[:, 384:640])
            back.gradient(b, dm[:, lead:])
            return 0

        lax.fori_loop(0, 2, gradient, 0)
        back.query_block(m)

    gather.own_chip()
    compute(0)
    gather.neighbours()
    first.combine(3)
    first.pass1.start()
    first.pass2.start()
    gather.chip1()
    compute(1)
    first.combine(1)
    first.first1.start()
    gather.chip2()
    compute(2)
    first.combine(2)
    first.first2.start()
    gather.diagonal()
    first.combine(0)
    gather.chip3()
    compute(3)
    first.finish_two()

    pad = 512 - heads.qkv

    def finish(b, sums):
        grad, sums = back.finish(b, sums)
        grad = jnp.concatenate([grad, jnp.zeros((pad, tok), F32)], axis=0)
        pg_ref[b] = jnp.transpose(grad).astype(BF16)
        return sums

    zero = jnp.zeros((D, tok), F32)
    sum_q, sum_k = lax.fori_loop(0, blocks, finish, (zero, zero))
    gains_ref[0:D, :] = jnp.broadcast_to(jnp.sum(sum_q, axis=1, keepdims=True), (D, 128))
    gains_ref[D:2 * D, :] = jnp.broadcast_to(jnp.sum(sum_k, axis=1, keepdims=True), (D, 128))
    load_merged.wait()

    tile = 256
    count = model // tile

    def x_copy(i, slot):
        return pltpu.make_async_copy(x_hbm.at[:, :, span(i * tile, tile)], xt_ref.at[slot], xt_sem.at[slot])

    def grad_copy(i, slot):
        return pltpu.make_async_copy(wstage_ref.at[slot], grad_hbm.at[span(i * tile, tile)], wstage_sem.at[slot])

    x_copy(0, 0).start()

    def weight_rows(i, _):
        slot = lax.rem(i, 2)
        cols = span(i * tile, tile)

        @pl.when(i + 1 < count)
        def _():
            x_copy(i + 1, 1 - slot).start()

        @pl.when(i >= 2)
        def _():
            grad_copy(i - 2, slot).wait()

        out = dot_tn(every_ref[:, :, cols].reshape(blocks * tok, tile), merged_ref[...])
        x_copy(i, slot).wait()
        x = xt_ref[slot].reshape(blocks * tok, tile)
        qkv = dot_tn(x, pg_ref[...].reshape(blocks * tok, 512))
        wstage_ref[slot, :, 0:heads.qkv] = qkv[:, 0:heads.qkv].astype(BF16)
        wstage_ref[slot, :, heads.qkv:heads.columns] = out[:, lead:].astype(BF16)
        grad_copy(i, slot).start()
        return 0

    lax.fori_loop(0, count, weight_rows, 0)
    first.arrive()

    def take(out_ref, scatter):
        def one(i, _):
            rows = span(i * 32, 32)
            out_ref[rows, :] = scatter.total(rows)
            return 0

        lax.fori_loop(0, tok // 32, one, 0)

    take(outsum_ref, first)
    first.close()
    for other in (place.sib, place.same[1], place.same[2]):
        pl.semaphore_signal(ready_sem, inc=1, device_id=(place.row, other), device_id_type=MESH)
    pl.semaphore_wait(ready_sem, 3)

    def project(k):
        m = place.chips[k]

        def model_tile(n, _):
            cols = span(n * 512, 512)
            out = dot_nt(pg_ref[pl.ds(2 * m, 2)].reshape(2 * tok, 512), w_ref[cols, 0:512])
            part_ref[k, :, :, cols] = out.astype(BF16).reshape(2, tok, 512)
            return 0

        lax.fori_loop(0, model // 512, model_tile, 0)
        second.exchange[k].start()

    project(3)
    project(1)
    second.combine(3)
    second.pass1.start()
    second.pass2.start()
    project(2)
    second.combine(1)
    second.first1.start()
    project(0)
    second.combine(2)
    second.first2.start()
    second.combine(0)
    for i in (count - 2, count - 1):
        grad_copy(i, i % 2).wait()
    second.finish_two()
    second.arrive()
    take(ysum_ref, second)
    gather.close()
    second.close()


def backward_phase(heads, branch, out_part, x_all, w, table, gq, gk, kept):
    blocks, tok, model = x_all.shape
    length = blocks * tok
    dma = pltpu.SemaphoreType.DMA
    raw, merged, *rest = kept
    return pl.pallas_call(
        functools.partial(backward_kernel, heads),
        out_shape=(
            jax.ShapeDtypeStruct((tok, model), F32),
            jax.ShapeDtypeStruct((tok, model), F32),
            jax.ShapeDtypeStruct((model, heads.columns), BF16),
            jax.ShapeDtypeStruct((2 * D, 128), F32),
        ),
        in_specs=[ANY_SPEC] * 4 + [VMEM_SPEC] * 3 + [ANY_SPEC] + [VMEM_SPEC] * (1 + len(rest)),
        out_specs=(VMEM_SPEC, VMEM_SPEC, ANY_SPEC, VMEM_SPEC),
        scratch_shapes=[
            pltpu.VMEM((blocks, tok, model), BF16),
            pltpu.VMEM((model, heads.columns), BF16),
            pltpu.VMEM((blocks, tok, 512), BF16),
            pltpu.VMEM(merged.shape, BF16),
            pltpu.VMEM((2, blocks, tok, 256), BF16),
            pltpu.VMEM((2, 256, heads.columns), BF16),
            *backward_scratch(heads, length),
            *scatter_scratch(tok, model),
            dma((SCATTER_SLOTS,)), dma((SCATTER_SLOTS,)),
            dma((GATHER_SLOTS,)), dma((GATHER_SLOTS,)), dma((4,)), dma((2,)), dma((2,)),
            pltpu.SemaphoreType.REGULAR,
        ],
        compiler_params=pltpu.CompilerParams(collective_id=3, has_side_effects=True, vmem_limit_bytes=62 * 1024 * 1024),
        cost_estimate=pl.CostEstimate(flops=60 << 30, bytes_accessed=64 << 20, transcendentals=0),
    )(branch, out_part, x_all, w, table, gq, gk, merged, raw, *rest)


def norm_back(grad_normed, values_in, inv_rms, gain):
    scaled = grad_normed * gain
    gain_grad = jnp.sum(grad_normed * values_in * inv_rms, axis=0)
    input_grad = inv_rms * scaled - values_in * inv_rms**3 * jnp.mean(scaled * values_in, axis=-1, keepdims=True)
    return input_grad, gain_grad


def start_wide(rows, x, table, pieces, gain):
    return (
        lax.all_gather(x, "seq", axis=0, tiled=False),
        lax.all_gather(table, "seq", axis=0, tiled=False),
        lax.all_gather(lax.all_to_all(pieces, "seq", 0, 0, tiled=False), "rows", axis=0, tiled=False),
        lax.all_gather(lax.all_gather(gain, "seq", axis=0, tiled=False), "rows", axis=0, tiled=False),
    )


def scatter_rows(part, tok):
    return lax.psum_scatter(part.reshape(-1, part.shape[-1]), "seq", scatter_dimension=0, tiled=True).astype(F32)


def attention_wide(heads, x_all, g, w, table, gq, gk):
    blocks, tok, model = x_all.shape
    proj = dot(x_all.reshape(blocks * tok, model), w[:, :heads.qkv])
    kept = pl.pallas_call(
        functools.partial(local_forward_kernel, heads),
        out_shape=kept_shapes(heads, blocks * tok, 0),
        compiler_params=pltpu.CompilerParams(vmem_limit_bytes=VMEM_LIMIT),
    )(proj, table, gq, gk)
    total = scatter_rows(dot_nt(kept[1], w[:, heads.qkv:]).astype(BF16), tok)
    own = lax.dynamic_index_in_dim(x_all, lax.axis_index("seq"), 0, keepdims=False)
    return (own.astype(F32) + total, lax.all_gather(g, "seq", axis=0, tiled=False)) + tuple(kept)


def feed_forward_wide(res, gain, g_blocks, gate_slab, up_slab, down_slab):
    blocks, tok, model = g_blocks.shape
    inv = norm_inverse(res)
    two_all = lax.all_gather((res * inv * gain).astype(BF16), "seq", axis=0, tiled=True)
    g_all = g_blocks.reshape(blocks * tok, model)
    gate_act = dot(two_all, gate_slab)
    up_act = dot(two_all, up_slab)
    s = jax.nn.sigmoid(gate_act)
    hidden = (gate_act * s * up_act).astype(BF16)
    hidden_grad = dot_nt(g_all, down_slab)
    gate_grad = (hidden_grad * up_act * s * (1.0 + gate_act * (1.0 - s))).astype(BF16)
    up_grad = (hidden_grad * gate_act * s).astype(BF16)
    two_grad = scatter_rows((dot_nt(gate_grad, gate_slab) + dot_nt(up_grad, up_slab)).astype(BF16), tok)
    branch_part = dot(hidden, down_slab).astype(BF16).reshape(blocks, tok, model)
    norm_grad, gain_grad = norm_back(two_grad, res, inv, gain)
    g = lax.dynamic_index_in_dim(g_blocks, lax.axis_index("seq"), 0, keepdims=False)
    residual_grad = g.astype(F32) + norm_grad
    return (branch_part, residual_grad, residual_grad.astype(BF16), gain_grad[None],
            dot_tn(two_all, gate_grad).astype(BF16), dot_tn(two_all, up_grad).astype(BF16),
            dot_tn(hidden, g_all).astype(BF16))


def backward_wide(heads, branch, out_part, x_all, w, table, gq, gk, kept):
    blocks, tok, model = x_all.shape
    length = blocks * tok
    raw, merged, *rest = kept
    out_sum = scatter_rows(out_part, tok)
    branch_all = lax.all_gather(branch, "seq", axis=0, tiled=True)
    pg, gains = pl.pallas_call(
        functools.partial(local_backward_kernel, heads),
        out_shape=(jax.ShapeDtypeStruct((length, heads.qkv), BF16), jax.ShapeDtypeStruct((2 * D, 128), F32)),
        scratch_shapes=backward_scratch(heads, length),
        compiler_params=pltpu.CompilerParams(vmem_limit_bytes=VMEM_LIMIT),
    )(dot(branch_all, w[:, heads.qkv:]), table, gq, gk, raw, *rest)
    y_sum = scatter_rows(dot_nt(pg, w[:, :heads.qkv]).astype(BF16), tok)
    grad = jnp.concatenate([dot_tn(x_all.reshape(length, model), pg), dot_tn(branch_all, merged)], axis=1)
    return y_sum, out_sum, grad.astype(BF16), gains


def rotary_table(x, positions, segments):
    inverse = jnp.exp(-math.log(THETA) * jnp.arange(HALF, dtype=F32) * 2.0 / D)
    angles = inverse[:, None] * positions.astype(F32)[None, :]
    hot = jnp.arange(SEGMENT_KINDS, dtype=jnp.int32)[:, None] == segments[None, :]
    root = jnp.pad(norm_inverse(x).T, ((0, 7), (0, 0)))
    return jnp.concatenate([jnp.cos(angles), jnp.sin(angles), hot.astype(F32), root], axis=0)


def attention_pieces(heads, w_qkv, w_out):
    depth = w_qkv.shape[0]
    qw, kw = QUERY_HEADS * D, KEY_VALUE_HEADS * D
    out_t = w_out.T

    def columns(array, start, first, count, most):
        parts = []
        for i in range(count):
            n = first + i
            parts.append(array[:, start + n * D:start + (n + 1) * D] if n < most else jnp.zeros((depth, D), BF16))
        return parts

    pieces = []
    for s in range(heads.seq):
        q, k = s * heads.queries, heads.first(s)
        parts = (columns(w_qkv, 0, q, heads.queries, QUERY_HEADS)
                 + columns(w_qkv, qw, k, heads.pairs, KEY_VALUE_HEADS)
                 + columns(w_qkv, qw + kw, k, heads.pairs, KEY_VALUE_HEADS)
                 + columns(out_t, 0, q, heads.queries, QUERY_HEADS))
        pieces.append(jnp.concatenate(parts, axis=1))
    return jnp.stack(pieces)


def attention_sums(heads, pieces):
    depth = pieces.shape[1]
    cut = lambda s, start, n: pieces[s, :, start + n * D:start + (n + 1) * D]
    queries = [cut(n // heads.queries, 0, n % heads.queries) for n in range(QUERY_HEADS)]
    outs = [cut(n // heads.queries, heads.qkv, n % heads.queries) for n in range(QUERY_HEADS)]

    def pairs(start):
        found = []
        for n in range(KEY_VALUE_HEADS):
            terms = [cut(s, start, n - heads.first(s)) for s in range(heads.seq)
                     if s * heads.queries < QUERY_HEADS and 0 <= n - heads.first(s) < heads.pairs]
            found.append(functools.reduce(jnp.add, terms))
        return found

    qkv = jnp.concatenate(queries + pairs(heads.wide) + pairs(heads.wide + heads.narrow), axis=1)
    return qkv, jnp.concatenate(outs, axis=1)


def body(tokens, segments, positions, cotangent, gain_attn, w_qkv, gain_q, gain_k, w_out, gain_ffn, w_gate, w_up, w_down):
    seq = lax.axis_size("seq")
    rows = lax.axis_size("rows")
    heads = Heads(seq)
    depth = w_qkv.shape[0]
    tok, model = tokens.shape[1:]
    plane = seq == PLANE

    gate_slab = lax.all_gather(w_gate, "rows", axis=0, tiled=True)
    up_slab = lax.all_gather(w_up, "rows", axis=0, tiled=True)
    down_slab = lax.all_gather(w_down, "rows", axis=1, tiled=True)
    gq = gain_q.astype(F32)[:, None]
    gk = gain_k.astype(F32)[:, None]
    x = tokens[0].astype(F32)

    scaled = (w_qkv.astype(F32) * gain_attn.astype(F32)[:, None]).astype(BF16)
    pieces = attention_pieces(heads, scaled, w_out)
    gain = jnp.pad(gain_ffn.astype(F32)[None], ((0, 7), (0, 128 - depth)))
    x_all, table, w, gains = (start_phase if plane else start_wide)(
        rows, tokens[0], rotary_table(x, positions[0], segments[0]), pieces, gain)
    w = w.reshape(model, heads.columns)
    gain_two = gains[:, :, 0, :depth].reshape(1, model)

    residual, g_all, *kept = (attention_phase if plane else attention_wide)(heads, x_all, cotangent[0], w, table, gq, gk)
    out_part, residual_grad, branch, gain_two_grad, gate_wgrad, up_wgrad, down_wgrad = (
        feed_forward if plane else feed_forward_wide)(residual, gain_two, g_all, gate_slab, up_slab, down_slab)
    grad_gate = lax.psum_scatter(gate_wgrad, "rows", scatter_dimension=0, tiled=True).astype(F32)
    grad_up = lax.psum_scatter(up_wgrad, "rows", scatter_dimension=0, tiled=True).astype(F32)
    grad_down = lax.psum_scatter(down_wgrad, "rows", scatter_dimension=1, tiled=True).astype(F32)
    y_sum, out_sum, attn_grad, head_gains = (backward_phase if plane else backward_wide)(
        heads, branch, out_part, x_all, w, table, gq, gk, kept)

    layer_out = (residual + out_sum).astype(BF16)
    inv = norm_inverse(x)
    grad_tokens = residual_grad + y_sum - x * (inv * inv * jnp.mean(y_sum * x, axis=-1, keepdims=True))

    attn_grad = lax.psum_scatter(attn_grad, "rows", scatter_dimension=0, tiled=True)
    attn_grad = lax.all_to_all(attn_grad.reshape(seq, depth, heads.columns), "seq", 0, 0, tiled=False).astype(F32)
    unscaled, grad_out = attention_sums(heads, attn_grad)
    grad_gain_attn = jnp.sum(unscaled * w_qkv.astype(F32), axis=1)
    grad_qkv = unscaled * gain_attn.astype(F32)[:, None]

    small = lax.psum(jnp.concatenate([gain_two_grad[0], head_gains[:, 0]]), ("rows", "seq"))
    start = (lax.axis_index("rows") * seq + lax.axis_index("seq")) * depth
    return (
        layer_out[None],
        grad_tokens[None],
        grad_gain_attn,
        grad_qkv,
        small[model:model + D],
        small[model + D:],
        grad_out.T,
        lax.dynamic_slice_in_dim(small, start, depth),
        grad_gate,
        grad_up,
        grad_down,
    )


def solution(mesh):
    both = ("rows", "seq")
    return jax.shard_map(
        body,
        mesh=mesh,
        in_specs=(
            P("rows", "seq", None), P("rows", "seq"), P("rows", "seq"), P("rows", "seq", None),
            P(both), P(both, None), P(), P(), P(None, both), P(both),
            P("rows", "seq"), P("rows", "seq"), P("seq", "rows"),
        ),
        out_specs=(
            P("rows", "seq", None), P("rows", "seq", None), P(both), P(both, None), P(), P(),
            P(None, both), P(both), P("rows", "seq"), P("rows", "seq"), P("seq", "rows"),
        ),
        check_vma=False,
    )
```

time: 1020 us -> 633 us (0.62)
  waiting for transfers between devices: 655 us -> 149 us
  Pallas kernels: 147 us -> 378 us
  blocking collectives: 108 us -> 53.7 us
  matrix products: 49.1 us -> 0 us
    pallas_call x3 -> x4, Pallas kernels: 147 us -> 378 us  [the longest x1 118 us: backward_phase(): pl.pallas_call(functools.partial(backward_kernel, heads), out_shape=(jax....]
    all_gather x4 -> x0, waiting for transfers between devices: 174 us -> none  [the longest x1 55.4 us: body(): normed_all = lax.all_gather(normed, 'seq', axis=0, tiled=True)]
    reduce_scatter x3 -> x0, waiting for transfers between devices: 166 us -> none  [the longest x1 68.9 us: body(): lax.psum_scatter(out_part, 'seq', scatter_dimension=0, tiled=True)]
    all_gather x2 -> x0, blocking collectives: 50.1 us -> none  [the longest x1 40.1 us: body(): lax.all_gather(jnp.stack([gain_attn, gain_ffn])[:, None], ('rows', 'seq')...]
    dot_general x6 -> x0, matrix products: 49.1 us -> none  [the longest x1 10.8 us: body(): lax.dot_general(pg, qkv_slab, (((0,), (1,)), ((), ())), preferred_element...]
    all_gather x1, waiting for transfers between devices: 46.2 us -> 0.02 us  [body(): up_slab = lax.all_gather(w_up, 'rows', axis=0, tiled=True)]
    all_gather x1, waiting for transfers between devices: 44.6 us -> 0.02 us  [body(): gate_slab = lax.all_gather(w_gate, 'rows', axis=0, tiled=True)]
    reduce_scatter x1, waiting for transfers between devices: 46.8 us -> 4.94 us  [body(): lax.psum_scatter(attn_grad, 'rows', scatter_dimension=0, tiled=True)]
  transfers between devices with their start and end apart: 15 -> 8, of which waited for: 14 -> 5; matrix products, arithmetic and copies ran while one was open for 4% -> 3% of each run, Pallas kernels for 0% -> 26%
where the time goes in v3:
time: 633 us; the launch traced here: 625 us
  Pallas kernels  378 us (60%)
  waiting for transfers between devices  149 us (24%)
  blocking collectives  53.7 us (8%)
  other arithmetic  18.4 us (3%)
  between operations  14.7 us (2%)
  local copies, waits for them, and re-layouts  6.67 us (1%)
    pallas_call x1, Pallas kernels, backward_phase(): pl.pallas_call(functools.partial(backward_kernel, heads), out_shape=(jax....  118 us
    pallas_call x1, Pallas kernels, feed_forward(): pl.pallas_call(ffn_kernel, out_shape=(jax.ShapeDtypeStruct((4, 2, tok, mo...  95.6 us
    pallas_call x1, Pallas kernels, start_phase(): pl.pallas_call(start_kernel, out_shape=(jax.ShapeDtypeStruct((PLANE, tok,...  86.9 us
    pallas_call x1, Pallas kernels, attention_phase(): pl.pallas_call(functools.partial(attention_kernel, heads), out_shape=(jax...  77.6 us
    psum x1, blocking collectives, body(): lax.psum(jnp.concatenate([gain_two_grad[0], head_gains[:, 0]]), ('rows',...  53.7 us
    reduce_scatter x1, waiting for transfers between devices, body(): lax.psum_scatter(down_wgrad, 'rows', scatter_dimension=1, tiled=True)  43.4 us
    reduce_scatter x1, waiting for transfers between devices, body(): lax.psum_scatter(up_wgrad, 'rows', scatter_dimension=0, tiled=True)  43.3 us
    reduce_scatter x1, waiting for transfers between devices, body(): lax.psum_scatter(gate_wgrad, 'rows', scatter_dimension=0, tiled=True)  38.6 us
  transfers between devices with their start and end apart: 8, of which 5 were waited for; matrix products, arithmetic and copies ran while one was open for 3% of the time, Pallas kernels for 26%

profile of v3, /device:TPU:0, one launch (start us, length us, event | category | flops | bytes accessed | tf_op | source)
XLA Modules:
  0.0 624.7 jit_solution(15576307381874117825)
XLA Ops:
  7.3 0.7 all-gather.4.cloned.1.call-update
  8.0 0.7 all-gather.6.cloned.1.call-update
  8.8 0.7 all-gather.8.cloned.1.call-update
  9.5 0.7 convert_element_type.47
  10.2 1.1 fusion.5
  11.5 0.2 fusion.36
  11.7 0.3 fusion
  12.0 0.6 pad_convert_fusion.gain_hbm
  12.6 0.7 copy.28.gq_ref
  13.3 0.7 copy.29.gk_ref
  14.1 0.1 fusion.18
  14.5 0.1 fusion.9
  14.6 0.1 fusion.12
  14.8 0.1 concatenate.52
  14.9 0.2 multiply_cosine_fusion
  15.1 0.7 select_maximum_fusion.table_hbm
  15.8 86.9 %shard_map.212 = (bf16[8,256,2048]{2,1,0:T(8,128)(2,1)}, f32[8,80,256]{2,1,0:T(8,128)}, bf16[4,8,64,640]{3,2,1,0:T(8,128)(2,1)}, f32[4,8,8,128]{3,2,1,0:T(8,128)}) custom-call(bf16[256,2048]{1,0:T(8,128)(2,1)} %bitcast.174, f32[80,256]{1,0:T(8,128)} %select_maximum_fusion.table_hbm, bf16[8,64,640]{2,1,0:T(8,128)(2,1)} %copy-done.5, ...), custom_call_target="tpu_custom_call" | custom-call | bytes 167772160 | tf_op jit(solution)/shard_map/pallas_call | solution.py:285
  102.7 0.9 slice_reduce_fusion.1
  103.6 0.7 reshape_squeeze.3.gain_ref
  104.3 77.6 %shard_map.213 = (f32[256,2048]{1,0:T(8,128)}, bf16[8,256,2048]{2,1,0:T(8,128)(2,1)}, f32[320,2048]{1,0:T(8,128)}, bf16[2048,256]{1,0:T(8,128)(2,1)}, f32[3,64,2...) custom-call(bf16[8,256,2048]{2,1,0:T(8,128)(2,1)} %get-tuple-element, ...), custom_call_target="tpu_custom_call" | custom-call | flops 42949672960 | bytes 67108864 | tf_op jit(solution)/shard_map/pallas_call | solution.py:625
  182.0 15.2 %all-gather.8.cloned.1.call-done.down_hbm = bf16[512,2048]{1,0:T(8,128)(2,1)} async-done(((bf16[512,512]{1,0:T(8,128)(2,1)}), bf16[512,2048]{1,0:T(8,128)(2,1)}) %all-gather.8.cloned.1.call-update) | async-done | bytes 2097168 | tf_op jit(solution)/shard_map/all_gather | solution.py:1178
  197.2 95.6 %shard_map.214 = (bf16[4,2,256,2048]{3,2,1,0:T(8,128)(2,1)}, f32[256,2048]{1,0:T(8,128)}, bf16[256,2048]{1,0:T(8,128)(2,1)}, f32[1,2048]{1,0:T(1,128)}, bf16[204...) custom-call(f32[256,2048]{1,0:T(8,128)} %get-tuple-element.39.res_ref, ...), custom_call_target="tpu_custom_call" | custom-call | flops 38654705664 | bytes 67108864 | tf_op jit(solution)/shard_map/pallas_call | solution.py:814
  292.9 117.7 %shard_map.215 = (f32[256,2048]{1,0:T(8,128)}, f32[256,2048]{1,0:T(8,128)}, bf16[2048,640]{1,0:T(8,128)(2,1)}, f32[128,128]{1,0:T(8,128)}) custom-call(bf16[256,2048]{1,0:T(8,128)(2,1)} %get-tuple-element.42.branch_hbm, bf16[4,2,256,2048]{3,2,1,0:T(8,128)(2,1)} %get-tuple-element.43.out_hbm, bf16[8,256,2048]{2,1,0:T(8,128)(2,1)} %get-tuple-element.36.x_hbm, ...), custom_call_target="tpu_custom_call" | custom-call | flops 64424509440 | bytes 67108864 | tf_op jit(solution)/shard_map/pallas_call | solution.py:1019
  410.7 0.5 reduce-scatter.7.cloned.1.call-update
  411.3 0.5 reduce-scatter.9.cloned.1.call-update
  411.9 0.7 reduce-scatter.11.cloned.1.call-update
  412.7 53.7 %psum.7 = f32[2176]{0:T(1024)S(1)} all-reduce(f32[2176]{0:T(1024)S(1)} %pad_maximum_fusion.8), channel_id=1, replica_groups=mesh['rows'=4,'seq'=8] {'rows','seq'}, use_global_device_ids=true, to_apply=%region_4.5 | all-reduce | flops 2176 | bytes 17408 | tf_op jit(solution)/shard_map/psum | solution.py:1210
  466.4 0.3 fusion.1
  466.7 0.6 fusion.39
  467.3 0.7 copy-done.3
  468.0 1.9 fusion.3
  469.9 4.9 reduce-scatter.5.cloned.1.call-done
  474.9 3.7 all-to-all-start
  478.6 3.5 fusion.4
  482.1 38.6 %reduce-scatter.7.cloned.1.call-done = bf16[512,512]{1,0:T(8,128)(2,1)} async-done(((bf16[2048,512]{1,0:T(8,128)(2,1)}), bf16[512,512]{1,0:T(8,128)(2,1)}) %reduce-scatter.7.cloned.1.call-update) | async-done | bytes 524304 | tf_op jit(solution)/shard_map/reduce_scatter | solution.py:1194
  520.7 2.1 convert_element_type.51
  522.8 43.3 %reduce-scatter.9.cloned.1.call-done = bf16[512,512]{1,0:T(8,128)(2,1)} async-done(((bf16[2048,512]{1,0:T(8,128)(2,1)}), bf16[512,512]{1,0:T(8,128)(2,1)}) %reduce-scatter.9.cloned.1.call-update) | async-done | bytes 524304 | tf_op jit(solution)/shard_map/reduce_scatter | solution.py:1195
  566.2 2.1 convert_element_type.52
  568.3 43.4 %reduce-scatter.11.cloned.1.call-done = bf16[512,512]{1,0:T(8,128)(2,1)} async-done(((bf16[512,2048]{1,0:T(8,128)(2,1)}), bf16[512,512]{1,0:T(8,128)(2,1)}) %reduce-scatter.11.cloned.1.call-update) | async-done | bytes 524304 | tf_op jit(solution)/shard_map/reduce_scatter | solution.py:1196
  611.7 2.1 convert_element_type.53
  613.9 0.2 slice_bitcast_fusion
  614.1 0.2 slice_bitcast_fusion.12
  614.3 0.2 slice_bitcast_fusion.5
  614.4 0.1 slice_bitcast_fusion.27
  614.6 0.3 concatenate.53
  614.9 0.3 copy-done.4
  615.2 1.5 broadcast_multiply_fusion
  616.8 0.9 concatenate.55
  (64 shorter events, 1.3 us)
Async XLA Ops:
  7.2 4.3 copy-start.6
  7.2 4.4 copy-start.14
  7.2 4.5 copy-start
  7.2 174.8 %all-gather.4.cloned.1.call-start = ((), (), s32[]{:S(2)}) async-start(), calls=%async_computation.5 | async-start | bytes 2621440 | tf_op jit(solution)/shard_map/all_gather | solution.py:1176
  7.9 4.0 copy-start.13
  8.0 4.0 copy-start.15
  8.0 4.6 copy-start.16
  8.0 5.3 copy-start.17
  8.0 174.0 %all-gather.6.cloned.1.call-start = ((), (), s32[]{:S(2)}) async-start(), calls=%async_computation.6 | async-start | bytes 2621440 | tf_op jit(solution)/shard_map/all_gather | solution.py:1177
  8.7 188.5 %all-gather.8.cloned.1.call-start = ((), (), s32[]{:S(2)}) async-start(), calls=%async_computation.7 | async-start | bytes 2621440 | tf_op jit(solution)/shard_map/all_gather | solution.py:1178
  9.5 465.4 %reduce-scatter.5.cloned.1.call-start = ((), (), s32[]{:S(2)}) async-start(), calls=%async_computation.8 | async-start | bytes 3276800 | tf_op jit(solution)/shard_map/reduce_scatter | solution.py:1204
  10.2 1.4 copy-start.11
  11.9 170.0 %copy-start.8 = (f32[256]{0:T(256)}, f32[256]{0:T(256)S(1)}, u32[]{:S(2)}) copy-start(f32[256]{0:T(256)S(1)} %fusion) | copy-start | bytes 3076
  14.9 0.9 copy-start.5
  410.7 110.0 %reduce-scatter.7.cloned.1.call-start = ((), (), s32[]{:S(2)}) async-start(), calls=%async_computation.9 | async-start | bytes 2621440 | tf_op jit(solution)/shard_map/reduce_scatter | solution.py:1194
  411.2 154.9 %reduce-scatter.9.cloned.1.call-start = ((), (), s32[]{:S(2)}) async-start(), calls=%async_computation.10 | async-start | bytes 2621440 | tf_op jit(solution)/shard_map/reduce_scatter | solution.py:1195
  411.3 1.3 copy-start.7
  411.3 1.4 copy-start.10
  411.3 55.1 %copy-start.1 = (bf16[1,256,2048]{2,1,0:T(8,128)(2,1)S(1)}, bf16[1,256,2048]{2,1,0:T(8,128)(2,1)}, u32[]{:S(2)}) copy-start(bf16[1,256,2048]{2,1,0:T(8,128)(2,1)} %param.13) | copy-start | bytes 3145732
  411.3 55.1 %copy-start.2 = (f32[256,2048]{1,0:T(8,128)S(1)}, f32[256,2048]{1,0:T(8,128)}, u32[]{:S(2)}) copy-start(f32[256,2048]{1,0:T(8,128)} %get-tuple-element.54) | copy-start | bytes 6291460
  411.8 199.8 %reduce-scatter.11.cloned.1.call-start = ((), (), s32[]{:S(2)}) async-start(), calls=%async_computation.11 | async-start | bytes 2621440 | tf_op jit(solution)/shard_map/reduce_scatter | solution.py:1196
  412.6 54.2 %copy-start.9 = (f32[256]{0:T(256)S(1)}, f32[256]{0:T(256)}, u32[]{:S(2)}) copy-start(f32[256]{0:T(256)} %copy-done.8) | copy-start | bytes 3076
  466.4 1.6 copy-start.3
  474.9 138.9 %all-to-all-start = ((bf16[8,64,640]{2,1,0:T(8,128)(2,1)}), bf16[8,64,640]{2,1,0:T(8,128)(2,1)S(1)}, u32[]{:S(2)}, u32[]{:S(2)}) async-start(bf16[8,64,640]{2,1,0:T(8,128)(2,1)} %bitcast.175), calls=%async_computation.1 | async-start | bytes 1310720 | tf_op jit(solution)/shard_map/all_to_all | solution.py:1205
  614.2 1.0 copy-start.4
  614.3 1.0 copy-start.12
Sparse Core Ops, SparseCore 0:
  9.6 90.8 all-gather.3
  102.1 48.6 all-gather.5
  152.4 44.7 all-gather.7
  410.8 64.0 reduce-scatter.4
  477.0 43.6 reduce-scatter.6
  522.9 43.1 reduce-scatter.8
  568.5 43.1 reduce-scatter.10

commit v4 on v3

--- a/solution.py
+++ b/solution.py
@@ -83,11 +83,14 @@
         self.chips = (chip, chip + 1 - 2 * lax.rem(chip, 2), lax.rem(chip + 2, 4), 3 - chip)
         self.same = tuple(2 * q + self.core for q in self.chips)
 
-    def greet(self):
+    def greet(self, rows=1):
         barrier = pltpu.get_barrier_semaphore()
         for other in (self.sib, self.same[1], self.same[2]):
             pl.semaphore_signal(barrier, inc=1, device_id=(self.row, other), device_id_type=MESH)
-        pl.semaphore_wait(barrier, 3)
+        for j in range(1, rows):
+            other = lax.rem(self.row + j, rows)
+            pl.semaphore_signal(barrier, inc=1, device_id=(other, self.me), device_id_type=MESH)
+        pl.semaphore_wait(barrier, 3 + rows - 1)
 
     def greet_all(self, rows):
         barrier = pltpu.get_barrier_semaphore()
@@ -103,6 +106,116 @@
         return pltpu.make_async_remote_copy(
             src_ref=src, dst_ref=dst, send_sem=send_sem.at[slot], recv_sem=recv_sem.at[slot],
             device_id=(self.row, target), device_id_type=MESH)
+
+
+class Line:
+    def __init__(self, place):
+        self.place = place
+        row = place.row
+        self.a = row + 1 - 2 * lax.rem(row, 2)
+        self.b = 3 - row
+        self.c = lax.rem(row + 2, 4)
+        self.middle = (row + 1) // 2 == 1
+
+    def send(self, src, dst, send_sem, send_slot, recv_sem, recv_slot, target):
+        return pltpu.make_async_remote_copy(
+            src_ref=src, dst_ref=dst, send_sem=send_sem.at[send_slot], recv_sem=recv_sem.at[recv_slot],
+            device_id=(target, self.place.me), device_id_type=MESH)
+
+
+ROW_SLOTS = 4
+
+
+class RowGather:
+    def __init__(self, line, own, every, send_sem, recv_sem):
+        self.line = line
+        mine = every.at[line.place.row]
+        passed = every.at[line.c]
+        self.to_a = line.send(own, mine, send_sem, 0, recv_sem, 0, line.a)
+        self.to_c = line.send(own, mine, send_sem, 1, recv_sem, 1, line.c)
+        self.to_b = line.send(own, mine, send_sem, 2, recv_sem, 2, line.b)
+        self.on = line.send(passed, passed, send_sem, 3, recv_sem, 2, line.a)
+
+    def start(self):
+        self.to_c.start()
+        self.to_a.start()
+
+        @pl.when(self.line.middle)
+        def _():
+            self.to_b.start()
+
+    def forward(self):
+        self.to_c.wait_recv()
+
+        @pl.when(self.line.middle)
+        def _():
+            self.on.start()
+
+    def finish(self):
+        self.to_a.wait_recv()
+        self.to_b.wait_recv()
+
+    def close(self):
+        self.to_a.wait_send()
+        self.to_c.wait_send()
+
+        @pl.when(self.line.middle)
+        def _():
+            self.to_b.wait_send()
+            self.on.wait_send()
+
+
+class RowScatter:
+    def __init__(self, line, part, recv, merge, total, send_sem, recv_sem):
+        self.line, self.total = line, total
+        self.to_a = line.send(part.at[line.a], recv.at[0], send_sem, 0, recv_sem, 0, line.a)
+        self.to_b = line.send(part.at[line.b], recv.at[1], send_sem, 1, recv_sem, 1, line.b)
+        self.to_c = line.send(part.at[line.c], recv.at[2], send_sem, 2, recv_sem, 2, line.c)
+        self.added = line.send(total, recv.at[2], send_sem, 2, recv_sem, 2, line.c)
+        self.over = line.send(part.at[line.b], merge, send_sem, 3, recv_sem, 3, line.a)
+
+    def start_over(self):
+        @pl.when(jnp.logical_not(self.line.middle))
+        def _():
+            self.over.start()
+
+    def start(self):
+        @pl.when(jnp.logical_not(self.line.middle))
+        def _():
+            self.to_c.start()
+
+        @pl.when(self.line.middle)
+        def _():
+            self.to_b.start()
+
+        self.to_a.start()
+
+    def add(self, work):
+        @pl.when(self.line.middle)
+        def _():
+            self.over.wait_recv()
+            work()
+            self.added.start()
+
+    def finish(self):
+        self.to_a.wait_recv()
+        self.to_c.wait_recv()
+
+        @pl.when(self.line.middle)
+        def _():
+            self.to_b.wait_recv()
+
+    def close(self):
+        self.to_a.wait_send()
+        self.to_c.wait_send()
+
+        @pl.when(self.line.middle)
+        def _():
+            self.to_b.wait_send()
+
+        @pl.when(jnp.logical_not(self.line.middle))
+        def _():
+            self.over.wait_send()
 
 
 GATHER_SLOTS = 10
@@ -233,7 +346,7 @@
 
 
 def start_kernel(x_hbm, table_hbm, pieces_hbm, gain_hbm, x_all, table_all, w_all, gain_all,
-                 x_send, x_recv, t_send, t_recv, p_send, p_recv, g_send, g_recv, z_send, z_recv, local_sem):
+                 x_send, x_recv, t_send, t_recv, p_send, p_recv, g_send, g_recv, z_send, z_recv, w_send, w_recv, local_sem):
     place = Place()
     rows = w_all.shape[0]
     me, row = place.me, place.row
@@ -257,18 +370,24 @@
         copy.wait()
     for copy in exchange:
         copy.wait_recv()
+    line = Line(place)
+    weights = RowGather(line, w_all.at[row], w_all, w_send, w_recv)
+    weights.start()
     along = []
     for j in range(1, rows):
         other = lax.rem(row + j, rows)
-        for i, every in enumerate((w_all, gain_all)):
-            along.append(pltpu.make_async_remote_copy(
-                src_ref=every.at[row], dst_ref=every.at[row], send_sem=z_send.at[2 * j + i], recv_sem=z_recv.at[2 * j + i],
-                device_id=(other, me), device_id_type=MESH))
+        along.append(line.send(gain_all.at[row], gain_all.at[row], z_send, j, z_recv, j, other))
     for copy in along:
         copy.start()
-    for name in ("own_chip", "neighbours", "chip1", "chip2", "diagonal", "chip3"):
+    for name in ("own_chip", "neighbours"):
         for gather in gathers[::-1]:
             getattr(gather, name)()
+    weights.forward()
+    for name in ("chip1", "chip2", "diagonal", "chip3"):
+        for gather in gathers[::-1]:
+            getattr(gather, name)()
+    weights.finish()
+    weights.close()
     for copy in local[2:]:
         copy.wait()
     for copy in along:
@@ -292,7 +411,7 @@
         ),
         in_specs=[ANY_SPEC] * 4,
         out_specs=(ANY_SPEC,) * 4,
-        scratch_shapes=[dma((GATHER_SLOTS,))] * 4 + [dma((PLANE,))] * 4 + [dma((2 * rows,))] * 2 + [dma((4,))],
+        scratch_shapes=[dma((GATHER_SLOTS,))] * 4 + [dma((PLANE,))] * 4 + [dma((rows,))] * 2 + [dma((ROW_SLOTS,))] * 2 + [dma((4,))],
         compiler_params=pltpu.CompilerParams(collective_id=0, has_side_effects=True),
         cost_estimate=pl.CostEstimate(flops=0, bytes_accessed=160 << 20, transcendentals=0),
     )(x, table, pieces, gain)
@@ -542,12 +661,16 @@
     gains_ref[D:2 * D, :] = jnp.broadcast_to(jnp.sum(sum_k, axis=1, keepdims=True), (D, 128))
 
 
-def attention_kernel(heads, x_hbm, g_hbm, w_hbm, table_ref, gq_ref, gk_ref,
-                     res_ref, g_all, raw_ref, merged_ref, o_ref, qa_ref, ka_ref, kt_ref, vt_ref, inv_ref,
+def attention_kernel(heads, x_hbm, g_hbm, w_hbm, gate_hbm, up_hbm, down_hbm, table_ref, gq_ref, gk_ref,
+                     res_ref, g_all, gate_all, up_all, down_all, raw_ref, merged_ref, o_ref, qa_ref, ka_ref, kt_ref, vt_ref, inv_ref,
                      x_ref, w_ref, part_ref, sibling_ref, passing_ref, final_ref, rs_send, rs_recv,
-                     ag_send, ag_recv, load_sem):
+                     ag_send, ag_recv, load_sem, own_sem, z_send, z_recv):
     place = Place()
     blocks, tok, model = x_ref.shape
+    slabs = ((gate_hbm, gate_all), (up_hbm, up_all), (down_hbm, down_all))
+    keep_slabs = [pltpu.make_async_copy(own, every.at[place.row], own_sem.at[i]) for i, (own, every) in enumerate(slabs)]
+    for copy in keep_slabs:
+        copy.start()
     load_w = pltpu.make_async_copy(w_hbm, w_ref, load_sem.at[blocks])
     load_w.start()
     loads = [pltpu.make_async_copy(x_hbm.at[b], x_ref.at[b], load_sem.at[b]) for b in range(blocks)]
@@ -555,9 +678,13 @@
         copy.start()
     keep_own = pltpu.make_async_copy(g_hbm, g_all.at[place.me], load_sem.at[blocks + 1])
     keep_own.start()
-    place.greet()
+    place.greet(4)
     gather = Gather(place, g_hbm, g_all, ag_send, ag_recv)
     scatter = Scatter(place, part_ref, sibling_ref, passing_ref, final_ref, rs_send, rs_recv)
+    line = Line(place)
+    weights = [RowGather(line, own, every, z_send.at[i], z_recv.at[i]) for i, (own, every) in enumerate(slabs)]
+    for one in weights:
+        one.start()
     gather.start()
     forward = Forward(heads, place.me, table_ref, gq_ref, gk_ref, raw_ref, merged_ref, o_ref, qa_ref, ka_ref, kt_ref,
                       vt_ref, inv_ref)
@@ -596,12 +723,14 @@
     scatter.first1.start()
     gather.chip1()
     gather.chip2()
+    weights[0].forward()
     compute(2)
     scatter.combine(2)
     scatter.first2.start()
     gather.diagonal()
     compute(0)
     scatter.combine(0)
+    weights[1].forward()
     scatter.finish_two()
     gather.chip3()
     scatter.arrive()
@@ -612,43 +741,53 @@
         return 0
 
     lax.fori_loop(0, tok // 32, finish, 0)
+    weights[2].forward()
+    for one in weights:
+        one.finish()
+        one.close()
+    for copy in keep_slabs:
+        copy.wait()
     keep_own.wait()
     gather.close()
     scatter.close()
 
 
-def attention_phase(heads, x_all, g, w, table, gq, gk):
+def attention_phase(heads, x_all, g, w, slabs, table, gq, gk):
     blocks, tok, model = x_all.shape
     dma = pltpu.SemaphoreType.DMA
     lead = 256 - heads.wide
     kept = kept_shapes(heads, blocks * tok, lead)
     return pl.pallas_call(
         functools.partial(attention_kernel, heads),
-        out_shape=(jax.ShapeDtypeStruct((tok, model), F32), jax.ShapeDtypeStruct((blocks, tok, model), BF16)) + kept,
-        in_specs=[ANY_SPEC] * 3 + [VMEM_SPEC] * 3,
-        out_specs=(VMEM_SPEC, ANY_SPEC) + (VMEM_SPEC,) * len(kept),
+        out_shape=(jax.ShapeDtypeStruct((tok, model), F32), jax.ShapeDtypeStruct((blocks, tok, model), BF16))
+        + tuple(jax.ShapeDtypeStruct((4,) + slab.shape, BF16) for slab in slabs) + kept,
+        in_specs=[ANY_SPEC] * 6 + [VMEM_SPEC] * 3,
+        out_specs=(VMEM_SPEC,) + (ANY_SPEC,) * 4 + (VMEM_SPEC,) * len(kept),
         scratch_shapes=[
             pltpu.VMEM((blocks, tok, model), BF16),
             pltpu.VMEM((model, heads.columns), BF16),
             *scatter_scratch(tok, model),
             dma((GATHER_SLOTS,)), dma((GATHER_SLOTS,)), dma((blocks + 2,)),
+            dma((3,)), dma((3, ROW_SLOTS)), dma((3, ROW_SLOTS)),
         ],
         compiler_params=pltpu.CompilerParams(collective_id=1, has_side_effects=True, vmem_limit_bytes=VMEM_LIMIT),
         cost_estimate=pl.CostEstimate(flops=40 << 30, bytes_accessed=64 << 20, transcendentals=0),
-    )(x_all, g, w, table, gq, gk)
+    )(x_all, g, w, *slabs, table, gq, gk)
 
 
 def ffn_kernel(res_ref, gain_ref, g_hbm, gate_hbm, up_hbm, down_hbm,
                out_hbm, rgrad_ref, branch_ref, gain_grad_ref, gate_grad_hbm, up_grad_hbm, down_grad_hbm,
                two_ref, g_ref, gate_ref, up_ref, down_ref, hid_ref, gu_ref, stage_ref, wstage_ref,
                part_ref, sibling_ref, passing_ref, final_ref, rs_send, rs_recv,
-               ag_send, ag_recv, load_sem, stage_sem, wstage_sem):
+               ag_send, ag_recv, load_sem, stage_sem, wstage_sem, down_sem):
     place = Place()
     _, tok, model = g_ref.shape
     ff = gate_ref.shape[1]
     tile = 256
+    share = model // 4
     loads = [pltpu.make_async_copy(src, dst, load_sem.at[i]) for i, (src, dst) in enumerate(
-        ((gate_hbm, gate_ref), (up_hbm, up_ref), (g_hbm, g_ref), (down_hbm, down_ref)))]
+        [(gate_hbm, gate_ref), (up_hbm, up_ref), (g_hbm, g_ref)]
+        + [(down_hbm.at[r], down_ref.at[:, r * share:(r + 1) * share]) for r in range(4)])]
     for copy in loads:
         copy.start()
 
@@ -735,9 +874,8 @@
     blocks = two_ref.shape[0]
 
     def wstage_copies(i, slot):
-        rows = pl.ds(pl.multiple_of(i * tile, tile), tile)
-        return (pltpu.make_async_copy(wstage_ref.at[slot, :, 0:ff], gate_grad_hbm.at[rows], wstage_sem.at[slot, 0]),
-                pltpu.make_async_copy(wstage_ref.at[slot, :, ff:2 * ff], up_grad_hbm.at[rows], wstage_sem.at[slot, 1]))
+        return (pltpu.make_async_copy(wstage_ref.at[slot, :, 0:ff], gate_grad_hbm.at[i], wstage_sem.at[slot, 0]),
+                pltpu.make_async_copy(wstage_ref.at[slot, :, ff:2 * ff], up_grad_hbm.at[i], wstage_sem.at[slot, 1]))
 
     def gate_up_rows(i, _):
         cols = pl.ds(pl.multiple_of(i * tile, tile), tile)
@@ -779,8 +917,9 @@
         return 0
 
     lax.fori_loop(0, ff // tile, down_rows, 0)
-    down_out = [pltpu.make_async_copy(stage_ref.at[0, i], down_grad_hbm.at[pl.ds(i * tile, tile)], stage_sem.at[i])
-                for i in range(ff // tile)]
+    down_out = [pltpu.make_async_copy(stage_ref.at[0, i, :, r * share:(r + 1) * share],
+                                      down_grad_hbm.at[r, i * tile:(i + 1) * tile], down_sem.at[4 * i + r])
+                for i in range(ff // tile) for r in range(4)]
     for copy in down_out:
         copy.start()
 
@@ -818,9 +957,9 @@
             jax.ShapeDtypeStruct((tok, model), F32),
             jax.ShapeDtypeStruct((tok, model), BF16),
             jax.ShapeDtypeStruct((1, model), F32),
-            jax.ShapeDtypeStruct((model, ff), BF16),
-            jax.ShapeDtypeStruct((model, ff), BF16),
-            jax.ShapeDtypeStruct((ff, model), BF16),
+            jax.ShapeDtypeStruct((model // 256, 256, ff), BF16),
+            jax.ShapeDtypeStruct((model // 256, 256, ff), BF16),
+            jax.ShapeDtypeStruct((4, ff, model // 4), BF16),
         ),
         in_specs=[vmem, vmem] + [any_spec] * 4,
         out_specs=(any_spec, vmem, vmem, vmem, any_spec, any_spec, any_spec),
@@ -837,22 +976,26 @@
             *scatter_scratch(tok, model),
             pltpu.SemaphoreType.DMA((GATHER_SLOTS,)),
             pltpu.SemaphoreType.DMA((GATHER_SLOTS,)),
-            pltpu.SemaphoreType.DMA((4,)),
+            pltpu.SemaphoreType.DMA((7,)),
             pltpu.SemaphoreType.DMA((2,)),
             pltpu.SemaphoreType.DMA((2, 2)),
+            pltpu.SemaphoreType.DMA((8,)),
         ],
         compiler_params=pltpu.CompilerParams(collective_id=2, has_side_effects=True, vmem_limit_bytes=60 * 1024 * 1024),
         cost_estimate=pl.CostEstimate(flops=18 * blocks * tok * model * ff, bytes_accessed=64 << 20, transcendentals=0),
     )(res, gain, g_all, gate, up, down)
 
 
-def backward_kernel(heads, branch_hbm, out_hbm, x_hbm, w_hbm, table_ref, gq_ref, gk_ref, merged_hbm,
+def backward_kernel(heads, branch_hbm, out_hbm, x_hbm, w_hbm, gate_grad, up_grad, down_grad,
+                    table_ref, gq_ref, gk_ref, small_in, merged_hbm,
                     raw_ref, o_ref, qa_ref, ka_ref, kt_ref, vt_ref, inv_ref,
-                    ysum_ref, outsum_ref, grad_hbm, gains_ref,
+                    ysum_ref, outsum_ref, grad_hbm, gate_recv, up_recv, down_recv, attn_recv, attn_merge, pieces_out, small_out,
                     every_ref, w_ref, pg_ref, merged_ref, xt_ref, wstage_ref,
                     doa_ref, dopad_ref, qpad_ref, va_ref, dq_ref, acc_ref,
                     part_ref, sibling_ref, passing_ref, final_ref, rs_send, rs_recv, rs2_send, rs2_recv,
-                    ag_send, ag_recv, load_sem, xt_sem, wstage_sem, ready_sem):
+                    ag_send, ag_recv, load_sem, xt_sem, wstage_sem, ready_sem,
+                    ffn_merge, ffn_own, z_send, z_recv, own_sem, small_ref, small_row, small_mid, small_last,
+                    s_send, s_recv, t_send, t_recv, p_send, p_recv):
     place = Place()
     blocks, tok, model = every_ref.shape
     load_w = pltpu.make_async_copy(w_hbm, w_ref, load_sem.at[0])
@@ -863,9 +1006,34 @@
     load_w.start()
     load_out.start()
     load_merged.start()
-    place.greet()
+    place.greet_all(4)
     gather = Gather(place, branch_hbm, every_ref, ag_send, ag_recv)
     gather.start()
+    line = Line(place)
+    ffn = [RowScatter(line, part, recv, ffn_merge.at[i], ffn_merge.at[i], z_send.at[i], z_recv.at[i])
+           for i, (part, recv) in enumerate(((gate_grad, gate_recv), (up_grad, up_recv), (down_grad, down_recv)))]
+    for one in ffn:
+        one.start_over()
+    for one in ffn:
+        one.start()
+
+    def ffn_add(i):
+        own = (gate_grad, up_grad, down_grad)[i]
+
+        def work():
+            load = pltpu.make_async_copy(own.at[line.c], ffn_own, own_sem.at[0])
+            load.start()
+            load.wait()
+
+            def add(n, _):
+                rows = span(n * 64, 64)
+                ffn_merge[i, rows, :] = (ffn_merge[i, rows, :].astype(F32) + ffn_own[rows, :].astype(F32)).astype(BF16)
+                return 0
+
+            lax.fori_loop(0, ffn_own.shape[0] // 64, add, 0)
+
+        ffn[i].add(work)
+
     first = Scatter(place, part_ref, sibling_ref, passing_ref, final_ref, rs_send, rs_recv)
     second = Scatter(place, part_ref, sibling_ref, passing_ref, final_ref, rs2_send, rs2_recv)
     back = Backward(heads, place.me, table_ref, gq_ref, gk_ref, raw_ref, o_ref, qa_ref, ka_ref, kt_ref, vt_ref, inv_ref,
@@ -901,17 +1069,20 @@
     first.combine(3)
     first.pass1.start()
     first.pass2.start()
+    ffn_add(0)
     gather.chip1()
     compute(1)
     first.combine(1)
     first.first1.start()
     gather.chip2()
+    ffn_add(1)
     compute(2)
     first.combine(2)
     first.first2.start()
     gather.diagonal()
     first.combine(0)
     gather.chip3()
+    ffn_add(2)
     compute(3)
     first.finish_two()
 
@@ -925,8 +1096,18 @@
 
     zero = jnp.zeros((D, tok), F32)
     sum_q, sum_k = lax.fori_loop(0, blocks, finish, (zero, zero))
-    gains_ref[0:D, :] = jnp.broadcast_to(jnp.sum(sum_q, axis=1, keepdims=True), (D, 128))
-    gains_ref[D:2 * D, :] = jnp.broadcast_to(jnp.sum(sum_k, axis=1, keepdims=True), (D, 128))
+    head_gains = jnp.sum(jnp.transpose(jnp.concatenate([sum_q, sum_k], axis=0)), axis=0, keepdims=True)
+    row8 = lax.broadcasted_iota(jnp.int32, (8, 128), 0)
+    for r in range(4):
+        for n in range(PLANE):
+            small_ref[r, n] = jnp.where(row8 == 1, head_gains, small_in[r, n])
+    small_sends = []
+    for j in range(1, 4):
+        other = lax.rem(place.row + j, 4)
+        small_sends.append(line.send(small_ref.at[other], small_row.at[place.row], s_send, j, s_recv, j, other))
+    for copy in small_sends:
+        copy.start()
+    small_row[place.row] = small_ref[place.row]
     load_merged.wait()
 
     tile = 256
@@ -936,7 +1117,7 @@
         return pltpu.make_async_copy(x_hbm.at[:, :, span(i * tile, tile)], xt_ref.at[slot], xt_sem.at[slot])
 
     def grad_copy(i, slot):
-        return pltpu.make_async_copy(wstage_ref.at[slot], grad_hbm.at[span(i * tile, tile)], wstage_sem.at[slot])
+        return pltpu.make_async_copy(wstage_ref.at[slot], grad_hbm.at[i // 2, lax.rem(i, 2)], wstage_sem.at[slot])
 
     x_copy(0, 0).start()
 
@@ -962,6 +1143,16 @@
         return 0
 
     lax.fori_loop(0, count, weight_rows, 0)
+    for i in (count - 2, count - 1):
+        grad_copy(i, i % 2).wait()
+    columns = heads.columns
+    gather.close()
+    merged_term = every_ref.at[0:2, :, 0:columns]
+    attn = RowScatter(line, grad_hbm, attn_recv, attn_merge, merged_term, z_send.at[3], z_recv.at[3])
+    attn.start_over()
+    attn.start()
+    own_term = pltpu.make_async_copy(grad_hbm.at[place.row], every_ref.at[6:8, :, 0:columns], own_sem.at[1])
+    own_term.start()
     first.arrive()
 
     def take(out_ref, scatter):
@@ -989,6 +1180,25 @@
 
         lax.fori_loop(0, model // 512, model_tile, 0)
         second.exchange[k].start()
+
+    def add_blocks(target, source):
+        def add(n, _):
+            b, rows = n // 4, span(lax.rem(n, 4) * 64, 64)
+            every_ref[target + b, rows, 0:columns] = (
+                every_ref[target + b, rows, 0:columns].astype(F32) + every_ref[source + b, rows, 0:columns].astype(F32)
+            ).astype(BF16)
+            return 0
+
+        lax.fori_loop(0, 8, add, 0)
+
+    def attn_work():
+        loads = [pltpu.make_async_copy(src, every_ref.at[2 * n:2 * n + 2, :, 0:columns], own_sem.at[2 + n])
+                 for n, src in enumerate((attn_merge, grad_hbm.at[line.c]))]
+        for copy in loads:
+            copy.start()
+        for copy in loads:
+            copy.wait()
+        add_blocks(0, 2)
 
     project(3)
     project(1)
@@ -996,22 +1206,71 @@
     second.pass1.start()
     second.pass2.start()
     project(2)
+    attn.add(attn_work)
     second.combine(1)
     second.first1.start()
     project(0)
     second.combine(2)
     second.first2.start()
     second.combine(0)
-    for i in (count - 2, count - 1):
-        grad_copy(i, i % 2).wait()
     second.finish_two()
+    for copy in small_sends:
+        copy.wait_recv()
+    small_mid[...] = (small_row[0] + small_row[1]) + (small_row[2] + small_row[3])
+    plane_sends = []
+    for j in range(1, PLANE):
+        other = lax.rem(place.me + j, PLANE)
+        plane_sends.append(place.send(small_mid.at[other], small_last.at[place.me], t_send, t_recv, j, other))
+    for copy in plane_sends:
+        copy.start()
+    small_last[place.me] = small_mid[place.me]
     second.arrive()
     take(ysum_ref, second)
-    gather.close()
+    for one in ffn:
+        one.finish()
+        one.close()
+    for copy in plane_sends:
+        copy.wait_recv()
+    total = small_last[0]
+    for n in range(1, PLANE):
+        total = total + small_last[n]
+    small_out[...] = total
+    own_term.wait()
+    attn.finish()
+
+    def fold(slot):
+        load = pltpu.make_async_copy(attn_recv.at[slot], every_ref.at[4:6, :, 0:columns], own_sem.at[4 + slot])
+        load.start()
+        load.wait()
+        add_blocks(6, 4)
+
+    fold(0)
+    fold(2)
+
+    @pl.when(line.middle)
+    def _():
+        fold(1)
+
+    def piece(n):
+        return every_ref.at[6 + n // 4, span(lax.rem(n, 4) * 64, 64), 0:columns]
+
+    keep = pltpu.make_async_copy(piece(place.me), pieces_out.at[place.me], own_sem.at[7])
+    keep.start()
+    for j in range(1, PLANE):
+        other = lax.rem(place.me + j, PLANE)
+        copy = place.send(piece(other), pieces_out.at[place.me], p_send, p_recv, j, other)
+        copy.start()
+        plane_sends.append(copy)
+    for copy in plane_sends[PLANE - 1:]:
+        copy.wait_recv()
+    keep.wait()
+    for copy in plane_sends + small_sends:
+        copy.wait_send()
+    attn.close()
     second.close()
 
 
-def backward_phase(heads, branch, out_part, x_all, w, table, gq, gk, kept):
+def backward_phase(heads, branch, out_part, x_all, w, weight_grads, table, gq, gk, small, kept):
     blocks, tok, model = x_all.shape
     length = blocks * tok
     dma = pltpu.SemaphoreType.DMA
@@ -1021,11 +1280,15 @@
         out_shape=(
             jax.ShapeDtypeStruct((tok, model), F32),
             jax.ShapeDtypeStruct((tok, model), F32),
-            jax.ShapeDtypeStruct((model, heads.columns), BF16),
-            jax.ShapeDtypeStruct((2 * D, 128), F32),
+            jax.ShapeDtypeStruct((4, 2, 256, heads.columns), BF16),
+            *(jax.ShapeDtypeStruct((3,) + grad.shape[1:], BF16) for grad in weight_grads),
+            jax.ShapeDtypeStruct((3, 2, 256, heads.columns), BF16),
+            jax.ShapeDtypeStruct((2, 256, heads.columns), BF16),
+            jax.ShapeDtypeStruct((PLANE, 64, heads.columns), BF16),
+            jax.ShapeDtypeStruct((8, 128), F32),
         ),
-        in_specs=[ANY_SPEC] * 4 + [VMEM_SPEC] * 3 + [ANY_SPEC] + [VMEM_SPEC] * (1 + len(rest)),
-        out_specs=(VMEM_SPEC, VMEM_SPEC, ANY_SPEC, VMEM_SPEC),
+        in_specs=[ANY_SPEC] * 7 + [VMEM_SPEC] * 4 + [ANY_SPEC] + [VMEM_SPEC] * (1 + len(rest)),
+        out_specs=(VMEM_SPEC, VMEM_SPEC) + (ANY_SPEC,) * 7 + (VMEM_SPEC,),
         scratch_shapes=[
             pltpu.VMEM((blocks, tok, model), BF16),
             pltpu.VMEM((model, heads.columns), BF16),
@@ -1038,10 +1301,18 @@
             dma((SCATTER_SLOTS,)), dma((SCATTER_SLOTS,)),
             dma((GATHER_SLOTS,)), dma((GATHER_SLOTS,)), dma((4,)), dma((2,)), dma((2,)),
             pltpu.SemaphoreType.REGULAR,
+            pltpu.VMEM((3,) + weight_grads[0].shape[1:], BF16),
+            pltpu.VMEM(weight_grads[0].shape[1:], BF16),
+            dma((4, ROW_SLOTS)), dma((4, ROW_SLOTS)), dma((8,)),
+            pltpu.VMEM((4, PLANE, 8, 128), F32),
+            pltpu.VMEM((4, PLANE, 8, 128), F32),
+            pltpu.VMEM((PLANE, 8, 128), F32),
+            pltpu.VMEM((PLANE, 8, 128), F32),
+            dma((4,)), dma((4,)), dma((PLANE,)), dma((PLANE,)), dma((PLANE,)), dma((PLANE,)),
         ],
         compiler_params=pltpu.CompilerParams(collective_id=3, has_side_effects=True, vmem_limit_bytes=62 * 1024 * 1024),
         cost_estimate=pl.CostEstimate(flops=60 << 30, bytes_accessed=64 << 20, transcendentals=0),
-    )(branch, out_part, x_all, w, table, gq, gk, merged, raw, *rest)
+    )(branch, out_part, x_all, w, *weight_grads, table, gq, gk, small, merged, raw, *rest)
 
 
 def norm_back(grad_normed, values_in, inv_rms, gain):
@@ -1171,15 +1442,12 @@
     heads = Heads(seq)
     depth = w_qkv.shape[0]
     tok, model = tokens.shape[1:]
-    plane = seq == PLANE
-
-    gate_slab = lax.all_gather(w_gate, "rows", axis=0, tiled=True)
-    up_slab = lax.all_gather(w_up, "rows", axis=0, tiled=True)
-    down_slab = lax.all_gather(w_down, "rows", axis=1, tiled=True)
+    plane = seq == PLANE and rows == 4
+    row = lax.axis_index("rows")
+
     gq = gain_q.astype(F32)[:, None]
     gk = gain_k.astype(F32)[:, None]
     x = tokens[0].astype(F32)
-
     scaled = (w_qkv.astype(F32) * gain_attn.astype(F32)[:, None]).astype(BF16)
     pieces = attention_pieces(heads, scaled, w_out)
     gain = jnp.pad(gain_ffn.astype(F32)[None], ((0, 7), (0, 128 - depth)))
@@ -1187,37 +1455,57 @@
         rows, tokens[0], rotary_table(x, positions[0], segments[0]), pieces, gain)
     w = w.reshape(model, heads.columns)
     gain_two = gains[:, :, 0, :depth].reshape(1, model)
-
-    residual, g_all, *kept = (attention_phase if plane else attention_wide)(heads, x_all, cotangent[0], w, table, gq, gk)
-    out_part, residual_grad, branch, gain_two_grad, gate_wgrad, up_wgrad, down_wgrad = (
-        feed_forward if plane else feed_forward_wide)(residual, gain_two, g_all, gate_slab, up_slab, down_slab)
-    grad_gate = lax.psum_scatter(gate_wgrad, "rows", scatter_dimension=0, tiled=True).astype(F32)
-    grad_up = lax.psum_scatter(up_wgrad, "rows", scatter_dimension=0, tiled=True).astype(F32)
-    grad_down = lax.psum_scatter(down_wgrad, "rows", scatter_dimension=1, tiled=True).astype(F32)
-    y_sum, out_sum, attn_grad, head_gains = (backward_phase if plane else backward_wide)(
-        heads, branch, out_part, x_all, w, table, gq, gk, kept)
+    inv = norm_inverse(x)
+
+    if plane:
+        residual, g_all, gate, up, down, *kept = attention_phase(
+            heads, x_all, cotangent[0], w, (w_gate, w_up, w_down), table, gq, gk)
+        out_part, residual_grad, branch, gain_two_grad, *weight_grads = feed_forward(
+            residual, gain_two, g_all, gate.reshape(model, -1), up.reshape(model, -1), down)
+        weight_grads = [grad.reshape((4,) + w_gate.shape) for grad in weight_grads]
+        small = jnp.pad(gain_two_grad.reshape(rows, seq, 1, depth), ((0, 0), (0, 0), (0, 7), (0, 128 - depth)))
+        y_sum, out_sum, _, gate_recv, up_recv, down_recv, _, _, attn_grad, small = backward_phase(
+            heads, branch, out_part, x_all, w, weight_grads, table, gq, gk, small, kept)
+        middle = (row + 1) // 2 == 1
+
+        def row_total(part, recv):
+            own = lax.dynamic_index_in_dim(part, row, 0, keepdims=False).astype(F32)
+            return own + recv[0].astype(F32) + recv[2].astype(F32) + jnp.where(middle, recv[1].astype(F32), 0.0)
+
+        grad_gate, grad_up, grad_down = (
+            row_total(part, recv) for part, recv in zip(weight_grads, (gate_recv, up_recv, down_recv)))
+        grad_gain_ffn, head_gains = small[0, :depth], small[1]
+    else:
+        gate_slab = lax.all_gather(w_gate, "rows", axis=0, tiled=True)
+        up_slab = lax.all_gather(w_up, "rows", axis=0, tiled=True)
+        down_slab = lax.all_gather(w_down, "rows", axis=1, tiled=True)
+        residual, g_all, *kept = attention_wide(heads, x_all, cotangent[0], w, table, gq, gk)
+        out_part, residual_grad, branch, gain_two_grad, gate_wgrad, up_wgrad, down_wgrad = feed_forward_wide(
+            residual, gain_two, g_all, gate_slab, up_slab, down_slab)
+        grad_gate = lax.psum_scatter(gate_wgrad, "rows", scatter_dimension=0, tiled=True).astype(F32)
+        grad_up = lax.psum_scatter(up_wgrad, "rows", scatter_dimension=0, tiled=True).astype(F32)
+        grad_down = lax.psum_scatter(down_wgrad, "rows", scatter_dimension=1, tiled=True).astype(F32)
+        y_sum, out_sum, attn_grad, head_gains = backward_wide(heads, branch, out_part, x_all, w, table, gq, gk, kept)
+        attn_grad = lax.psum_scatter(attn_grad, "rows", scatter_dimension=0, tiled=True)
+        attn_grad = lax.all_to_all(attn_grad.reshape(seq, depth, heads.columns), "seq", 0, 0, tiled=False)
+        small = lax.psum(jnp.concatenate([gain_two_grad[0], head_gains[:, 0]]), ("rows", "seq"))
+        grad_gain_ffn = lax.dynamic_slice_in_dim(small, (row * seq + lax.axis_index("seq")) * depth, depth)
+        head_gains = small[model:]
 
     layer_out = (residual + out_sum).astype(BF16)
-    inv = norm_inverse(x)
     grad_tokens = residual_grad + y_sum - x * (inv * inv * jnp.mean(y_sum * x, axis=-1, keepdims=True))
-
-    attn_grad = lax.psum_scatter(attn_grad, "rows", scatter_dimension=0, tiled=True)
-    attn_grad = lax.all_to_all(attn_grad.reshape(seq, depth, heads.columns), "seq", 0, 0, tiled=False).astype(F32)
-    unscaled, grad_out = attention_sums(heads, attn_grad)
+    unscaled, grad_out = attention_sums(heads, attn_grad.astype(F32))
     grad_gain_attn = jnp.sum(unscaled * w_qkv.astype(F32), axis=1)
     grad_qkv = unscaled * gain_attn.astype(F32)[:, None]
-
-    small = lax.psum(jnp.concatenate([gain_two_grad[0], head_gains[:, 0]]), ("rows", "seq"))
-    start = (lax.axis_index("rows") * seq + lax.axis_index("seq")) * depth
     return (
         layer_out[None],
         grad_tokens[None],
         grad_gain_attn,
         grad_qkv,
-        small[model:model + D],
-        small[model + D:],
+        head_gains[:D],
+        head_gains[D:],
         grad_out.T,
-        lax.dynamic_slice_in_dim(small, start, depth),
+        grad_gain_ffn,
         grad_gate,
         grad_up,
         grad_down,

time: 633 us -> 478 us (0.76)
  waiting for transfers between devices: 149 us -> 0 us
  Pallas kernels: 378 us -> 436 us
  blocking collectives: 53.7 us -> 0 us
  between operations: 14.7 us -> 1.22 us
    reduce_scatter x4 -> x0, waiting for transfers between devices: 130 us -> none  [the longest x1 43.4 us: body(): lax.psum_scatter(down_wgrad, 'rows', scatter_dimension=1, tiled=True)]
    psum x1 -> x0, blocking collectives: 53.7 us -> none  [body(): lax.psum(jnp.concatenate([gain_two_grad[0], head_gains[:, 0]]), ('rows',...]
    pallas_call x1, Pallas kernels: 118 us -> 168 us  [backward_phase(): pl.pallas_call(functools.partial(backward_kernel, heads), out_shape=(jax....]
    pallas_call x1, Pallas kernels: 77.6 us -> 112 us  [attention_phase(): pl.pallas_call(functools.partial(attention_kernel, heads), out_shape=(jax...]
    pallas_call x1, Pallas kernels: 86.9 us -> 60.8 us  [start_phase(): pl.pallas_call(start_kernel, out_shape=(jax.ShapeDtypeStruct((PLANE, tok,...]
    all_gather x3 -> x0, waiting for transfers between devices: 15.2 us -> none  [the longest x1 15.2 us: body(): down_slab = lax.all_gather(w_down, 'rows', axis=1, tiled=True)]
    add x0 -> x3, other arithmetic: none -> 7.67 us  [row_total(): own + recv[0].astype(F32) + recv[2].astype(F32)]
    convert_element_type x4 -> x1, other arithmetic: 6.53 us -> 0.09 us  [body(): unscaled, grad_out = attention_sums(heads, attn_grad.astype(F32))]
  transfers between devices with their start and end apart: 8 -> 0, of which waited for: 5 -> 0; matrix products, arithmetic and copies ran while one was open for 3% -> 0% of each run, Pallas kernels for 26% -> 0%
where the time goes in v4:
time: 478 us; the launch traced here: 469 us
  Pallas kernels  436 us (91%)
  other arithmetic  20.5 us (4%)
  local copies, waits for them, and re-layouts  11.8 us (2%)
    pallas_call x1, Pallas kernels, backward_phase(): pl.pallas_call(functools.partial(backward_kernel, heads), out_shape=(jax....  168 us
    pallas_call x1, Pallas kernels, attention_phase(): pl.pallas_call(functools.partial(attention_kernel, heads), out_shape=(jax...  112 us
    pallas_call x1, Pallas kernels, feed_forward(): pl.pallas_call(ffn_kernel, out_shape=(jax.ShapeDtypeStruct((4, 2, tok, mo...  94.6 us
    pallas_call x1, Pallas kernels, start_phase(): pl.pallas_call(start_kernel, out_shape=(jax.ShapeDtypeStruct((PLANE, tok,...  60.8 us

profile of v4, /device:TPU:0, one launch (start us, length us, event | category | flops | bytes accessed | tf_op | source)
XLA Modules:
  0.0 469.2 jit_solution(2934679745482306347)
XLA Ops:
  0.7 0.0 copy-start
  0.7 0.7 convert_element_type.88
  1.4 1.1 fusion.5
  2.5 0.0 copy-start.15
  2.5 1.1 fusion.36
  3.6 0.1 fusion.37
  3.7 0.1 fusion.15
  3.8 0.1 fusion.18
  3.9 0.1 fusion.19
  4.0 0.1 fusion.20
  4.2 0.1 fusion.9
  4.3 0.1 fusion.12
  4.4 0.1 fusion.21
  4.5 0.1 fusion.35
  4.6 0.1 concatenate.49
  4.8 0.2 multiply_cosine_fusion
  5.0 0.3 fusion
  5.3 0.6 select_maximum_fusion.table_hbm
  6.0 0.6 pad_convert_fusion.gain_hbm
  6.6 60.8 %shard_map.212 = (bf16[8,256,2048]{2,1,0:T(8,128)(2,1)}, f32[8,80,256]{2,1,0:T(8,128)}, bf16[4,8,64,640]{3,2,1,0:T(8,128)(2,1)}, f32[4,8,8,128]{3,2,1,0:T(8,128)}) custom-call(bf16[256,2048]{1,0:T(8,128)(2,1)} %bitcast.188, f32[80,256]{1,0:T(8,128)} %select_maximum_fusion.table_hbm, bf16[8,64,640]{2,1,0:T(8,128)(2,1)} %copy-done.9, ...), custom_call_target="tpu_custom_call" | custom-call | bytes 167772160 | tf_op jit(solution)/shard_map/pallas_call | solution.py:404
  67.4 0.7 copy.24.gq_ref
  68.1 0.7 copy.25.gk_ref
  68.8 112.0 %shard_map.213 = (f32[256,2048]{1,0:T(8,128)}, bf16[8,256,2048]{2,1,0:T(8,128)(2,1)}, bf16[4,512,512]{2,1,0:T(8,128)(2,1)}, bf16[4,512,512]{2,1,0:T(8,128)(2,1)}...) custom-call(bf16[8,256,2048]{2,1,0:T(8,128)(2,1)} %get-tuple-element, ...), custom_call_target="tpu_custom_call" | custom-call | flops 42949672960 | bytes 67108864 | tf_op jit(solution)/shard_map/pallas_call | solution.py:760
  180.8 0.9 slice_reduce_fusion
  181.8 0.7 reshape_squeeze.3.gain_ref
  182.5 94.6 %shard_map.214 = (bf16[4,2,256,2048]{3,2,1,0:T(8,128)(2,1)}, f32[256,2048]{1,0:T(8,128)}, bf16[256,2048]{1,0:T(8,128)(2,1)}, f32[1,2048]{1,0:T(1,128)}, bf16[8,2...) custom-call(f32[256,2048]{1,0:T(8,128)} %get-tuple-element.45.res_ref, ...), custom_call_target="tpu_custom_call" | custom-call | flops 38654705664 | bytes 67108864 | tf_op jit(solution)/shard_map/pallas_call | solution.py:953
  277.1 0.5 broadcast.90
  277.6 1.4 reduce.7
  279.0 0.1 reshape.136
  279.0 0.7 pad.17.small_in
  279.7 168.3 %shard_map.215 = (f32[256,2048]{1,0:T(8,128)}, f32[256,2048]{1,0:T(8,128)}, bf16[4,2,256,640]{3,2,1,0:T(8,128)(2,1)}, bf16[3,512,512]{2,1,0:T(8,128)(2,1)}, bf16...) custom-call(bf16[256,2048]{1,0:T(8,128)(2,1)} %get-tuple-element.51., ...), custom_call_target="tpu_custom_call" | custom-call | flops 64424509440 | bytes 67108864 | tf_op jit(solution)/shard_map/pallas_call | solution.py:1278
  448.1 2.9 add_bitcast_fusion
  451.0 2.4 add_bitcast_fusion.1
  453.4 2.4 add_bitcast_fusion.2
  455.8 0.1 convert_element_type.91
  455.9 0.2 slice_bitcast_fusion
  456.0 0.2 slice_bitcast_fusion.12
  456.2 0.2 slice_bitcast_fusion.5
  456.4 0.9 concatenate.51
  457.3 0.7 slice_bitcast_fusion.27
  458.0 0.7 slice_bitcast_fusion.46
  458.7 1.2 concatenate.50
  460.0 1.5 broadcast_multiply_fusion
  461.5 1.9 fusion.1
  463.5 1.9 fusion.3
  465.4 1.1 copy-done.4
  466.4 1.2 fusion.4
  467.7 1.4 slice_bitcast_fusion.48
  (46 shorter events, 0.1 us)
Async XLA Ops:
  0.6 4.1 copy-start.16
  0.7 4.3 copy-start
  1.4 1.1 copy-start.13
  2.5 2.8 copy-start.15
  2.5 3.4 copy-start.17
  4.1 63.2 %copy-start.18 = (bf16[64]{0:T(256)(128)(2,1)S(1)}, bf16[64]{0:T(256)(128)(2,1)}, u32[]{:S(2)}) copy-start(bf16[64]{0:T(256)(128)(2,1)} %param.19) | copy-start | bytes 388
  4.2 64.0 %copy-start.19 = (bf16[64]{0:T(256)(128)(2,1)S(1)}, bf16[64]{0:T(256)(128)(2,1)}, u32[]{:S(2)}) copy-start(bf16[64]{0:T(256)(128)(2,1)} %param.20) | copy-start | bytes 388
  4.7 1.8 copy-start.9
  5.3 0.7 copy-start.11
  448.1 2.9 copy-start.7
  451.0 2.4 copy-start.6
  453.4 2.4 copy-start.10
  456.4 3.6 copy-start.8
  456.4 3.6 copy-start.14
  457.3 4.2 copy-start.1
  460.0 3.5 copy-start.12
  460.0 3.5 copy-start.2
  460.0 3.5 copy-start.5
  463.4 1.9 copy-start.3
  463.5 3.0 copy-start.4

commit v5 on v4

--- a/solution.py
+++ b/solution.py
@@ -127,10 +127,9 @@
 
 
 class RowGather:
-    def __init__(self, line, own, every, send_sem, recv_sem):
+    def __init__(self, line, own, at, send_sem, recv_sem):
         self.line = line
-        mine = every.at[line.place.row]
-        passed = every.at[line.c]
+        mine, passed = at(line.place.row), at(line.c)
         self.to_a = line.send(own, mine, send_sem, 0, recv_sem, 0, line.a)
         self.to_c = line.send(own, mine, send_sem, 1, recv_sem, 1, line.c)
         self.to_b = line.send(own, mine, send_sem, 2, recv_sem, 2, line.b)
@@ -303,8 +302,7 @@
         def one(i, _):
             rows = pl.ds(pl.multiple_of(start + i * step, step), step)
             from_rows = pl.ds(pl.multiple_of(offset + i * step, step), step)
-            total = self.part[k, core, rows, :].astype(F32) + term[from_rows, :].astype(F32)
-            self.part[k, core, rows, :] = total.astype(BF16)
+            self.part[k, core, rows, :] = self.part[k, core, rows, :] + term[from_rows, :]
             return 0
 
         lax.fori_loop(0, size // step, one, 0)
@@ -345,25 +343,25 @@
     ]
 
 
-def start_kernel(x_hbm, table_hbm, pieces_hbm, gain_hbm, x_all, table_all, w_all, gain_all,
+def start_kernel(x_ref, table_ref, pieces_ref, gain_ref, x_all, table_all, w_all, gain_all,
                  x_send, x_recv, t_send, t_recv, p_send, p_recv, g_send, g_recv, z_send, z_recv, w_send, w_recv, local_sem):
     place = Place()
     rows = w_all.shape[0]
     me, row = place.me, place.row
     local = [pltpu.make_async_copy(src, dst, local_sem.at[i]) for i, (src, dst) in enumerate((
-        (pieces_hbm.at[me], w_all.at[row, me]), (gain_hbm, gain_all.at[row, me]),
-        (x_hbm, x_all.at[me]), (table_hbm, table_all.at[me])))]
+        (pieces_ref.at[me], w_all.at[row, me]), (gain_ref, gain_all.at[row, me]),
+        (x_ref, x_all.at[me]), (table_ref, table_all.at[me])))]
     for copy in local:
         copy.start()
     place.greet_all(rows)
     exchange = []
     for j in range(1, PLANE):
         other = lax.rem(me + j, PLANE)
-        exchange.append(place.send(pieces_hbm.at[other], w_all.at[row, me], p_send, p_recv, j, other))
-        exchange.append(place.send(gain_hbm, gain_all.at[row, me], g_send, g_recv, j, other))
+        exchange.append(place.send(pieces_ref.at[other], w_all.at[row, me], p_send, p_recv, j, other))
+        exchange.append(place.send(gain_ref, gain_all.at[row, me], g_send, g_recv, j, other))
     for copy in exchange:
         copy.start()
-    gathers = (Gather(place, x_hbm, x_all, x_send, x_recv), Gather(place, table_hbm, table_all, t_send, t_recv))
+    gathers = (Gather(place, x_ref, x_all, x_send, x_recv), Gather(place, table_ref, table_all, t_send, t_recv))
     gathers[1].start()
     gathers[0].start()
     for copy in local[:2]:
@@ -371,7 +369,7 @@
     for copy in exchange:
         copy.wait_recv()
     line = Line(place)
-    weights = RowGather(line, w_all.at[row], w_all, w_send, w_recv)
+    weights = RowGather(line, w_all.at[row], lambda r: w_all.at[r], w_send, w_recv)
     weights.start()
     along = []
     for j in range(1, rows):
@@ -409,7 +407,7 @@
             jax.ShapeDtypeStruct((rows,) + pieces.shape, BF16),
             jax.ShapeDtypeStruct((rows, PLANE) + gain.shape, F32),
         ),
-        in_specs=[ANY_SPEC] * 4,
+        in_specs=[VMEM_SPEC] * 4,
         out_specs=(ANY_SPEC,) * 4,
         scratch_shapes=[dma((GATHER_SLOTS,))] * 4 + [dma((PLANE,))] * 4 + [dma((rows,))] * 2 + [dma((ROW_SLOTS,))] * 2 + [dma((4,))],
         compiler_params=pltpu.CompilerParams(collective_id=0, has_side_effects=True),
@@ -661,28 +659,24 @@
     gains_ref[D:2 * D, :] = jnp.broadcast_to(jnp.sum(sum_k, axis=1, keepdims=True), (D, 128))
 
 
-def attention_kernel(heads, x_hbm, g_hbm, w_hbm, gate_hbm, up_hbm, down_hbm, table_ref, gq_ref, gk_ref,
-                     res_ref, g_all, gate_all, up_all, down_all, raw_ref, merged_ref, o_ref, qa_ref, ka_ref, kt_ref, vt_ref, inv_ref,
-                     x_ref, w_ref, part_ref, sibling_ref, passing_ref, final_ref, rs_send, rs_recv,
-                     ag_send, ag_recv, load_sem, own_sem, z_send, z_recv):
+def attention_kernel(heads, x_hbm, g_hbm, w_hbm, gate_hbm, up_hbm, table_ref, gq_ref, gk_ref, gain_ref,
+                     res_ref, two_ref, g_all, gate_all, up_all, raw_hbm, merged_hbm, o_hbm, qa_hbm, ka_hbm, kt_hbm, vt_hbm, inv_hbm,
+                     raw_ref, merged_ref, o_ref, qa_ref, ka_ref, kt_ref, vt_ref, inv_ref, kept_sem, x_ref, w_ref, part_ref, sibling_ref, passing_ref, final_ref, rs_send, rs_recv,
+                     ag_send, ag_recv, load_sem, z_send, z_recv):
     place = Place()
     blocks, tok, model = x_ref.shape
-    slabs = ((gate_hbm, gate_all), (up_hbm, up_all), (down_hbm, down_all))
-    keep_slabs = [pltpu.make_async_copy(own, every.at[place.row], own_sem.at[i]) for i, (own, every) in enumerate(slabs)]
-    for copy in keep_slabs:
-        copy.start()
+    slabs = ((gate_hbm, gate_all), (up_hbm, up_all))
     load_w = pltpu.make_async_copy(w_hbm, w_ref, load_sem.at[blocks])
     load_w.start()
     loads = [pltpu.make_async_copy(x_hbm.at[b], x_ref.at[b], load_sem.at[b]) for b in range(blocks)]
     for copy in loads:
         copy.start()
-    keep_own = pltpu.make_async_copy(g_hbm, g_all.at[place.me], load_sem.at[blocks + 1])
-    keep_own.start()
     place.greet(4)
     gather = Gather(place, g_hbm, g_all, ag_send, ag_recv)
     scatter = Scatter(place, part_ref, sibling_ref, passing_ref, final_ref, rs_send, rs_recv)
     line = Line(place)
-    weights = [RowGather(line, own, every, z_send.at[i], z_recv.at[i]) for i, (own, every) in enumerate(slabs)]
+    weights = [RowGather(line, own, lambda r, every=every: every.at[r], z_send.at[i], z_recv.at[i])
+               for i, (own, every) in enumerate(slabs)]
     for one in weights:
         one.start()
     gather.start()
@@ -729,6 +723,11 @@
     scatter.first2.start()
     gather.diagonal()
     compute(0)
+    keep = [pltpu.make_async_copy(src, dst, kept_sem.at[i]) for i, (src, dst) in enumerate((
+        (raw_ref, raw_hbm), (merged_ref, merged_hbm), (o_ref, o_hbm), (qa_ref, qa_hbm), (ka_ref, ka_hbm),
+        (kt_ref, kt_hbm), (vt_ref, vt_hbm), (inv_ref, inv_hbm)))]
+    for copy in keep:
+        copy.start()
     scatter.combine(0)
     weights[1].forward()
     scatter.finish_two()
@@ -737,148 +736,171 @@
 
     def finish(i, _):
         rows = span(i * 32, 32)
-        res_ref[rows, :] = x_ref[place.me, rows, :].astype(F32) + scatter.total(rows)
+        res = x_ref[place.me, rows, :].astype(F32) + scatter.total(rows)
+        res_ref[rows, :] = res
+        two_ref[rows, :] = (res * norm_inverse(res) * gain_ref[...]).astype(BF16)
         return 0
 
     lax.fori_loop(0, tok // 32, finish, 0)
-    weights[2].forward()
     for one in weights:
         one.finish()
         one.close()
-    for copy in keep_slabs:
+    for copy in keep:
         copy.wait()
-    keep_own.wait()
     gather.close()
     scatter.close()
 
 
-def attention_phase(heads, x_all, g, w, slabs, table, gq, gk):
+def attention_phase(heads, x_all, g, w, slabs, table, gq, gk, gain):
     blocks, tok, model = x_all.shape
     dma = pltpu.SemaphoreType.DMA
     lead = 256 - heads.wide
     kept = kept_shapes(heads, blocks * tok, lead)
     return pl.pallas_call(
         functools.partial(attention_kernel, heads),
-        out_shape=(jax.ShapeDtypeStruct((tok, model), F32), jax.ShapeDtypeStruct((blocks, tok, model), BF16))
+        out_shape=(jax.ShapeDtypeStruct((tok, model), F32), jax.ShapeDtypeStruct((tok, model), BF16),
+                   jax.ShapeDtypeStruct((blocks, tok, model), BF16))
         + tuple(jax.ShapeDtypeStruct((4,) + slab.shape, BF16) for slab in slabs) + kept,
-        in_specs=[ANY_SPEC] * 6 + [VMEM_SPEC] * 3,
-        out_specs=(VMEM_SPEC,) + (ANY_SPEC,) * 4 + (VMEM_SPEC,) * len(kept),
+        in_specs=[ANY_SPEC] * 5 + [VMEM_SPEC] * 4,
+        out_specs=(VMEM_SPEC, VMEM_SPEC) + (ANY_SPEC,) * (3 + len(kept)),
         scratch_shapes=[
+            *(pltpu.VMEM(array.shape, array.dtype) for array in kept),
+            dma((len(kept),)),
             pltpu.VMEM((blocks, tok, model), BF16),
             pltpu.VMEM((model, heads.columns), BF16),
             *scatter_scratch(tok, model),
-            dma((GATHER_SLOTS,)), dma((GATHER_SLOTS,)), dma((blocks + 2,)),
-            dma((3,)), dma((3, ROW_SLOTS)), dma((3, ROW_SLOTS)),
+            dma((GATHER_SLOTS,)), dma((GATHER_SLOTS,)), dma((blocks + 1,)),
+            dma((2, ROW_SLOTS)), dma((2, ROW_SLOTS)),
         ],
         compiler_params=pltpu.CompilerParams(collective_id=1, has_side_effects=True, vmem_limit_bytes=VMEM_LIMIT),
         cost_estimate=pl.CostEstimate(flops=40 << 30, bytes_accessed=64 << 20, transcendentals=0),
-    )(x_all, g, w, *slabs, table, gq, gk)
-
-
-def ffn_kernel(res_ref, gain_ref, g_hbm, gate_hbm, up_hbm, down_hbm,
-               out_hbm, rgrad_ref, branch_ref, gain_grad_ref, gate_grad_hbm, up_grad_hbm, down_grad_hbm,
-               two_ref, g_ref, gate_ref, up_ref, down_ref, hid_ref, gu_ref, stage_ref, wstage_ref,
+    )(x_all, g, w, *slabs, table, gq, gk, gain)
+
+
+def ffn_kernel(res_ref, gain_ref, two_hbm, g_own, g_hbm, gate_own, gate_hbm, up_own, up_hbm, down_hbm,
+               out_hbm, rgrad_ref, branch_ref, gain_grad_ref, gate_grad_hbm, up_grad_hbm,
+               gate_grad_own, up_grad_own, down_own, down_recv,
+               two_ref, g_ref, weight_ref, down_ref, hid_ref, gu_ref, stage_ref, wstage_ref, dsum_ref, dgrad_ref, merge_ref,
                part_ref, sibling_ref, passing_ref, final_ref, rs_send, rs_recv,
-               ag_send, ag_recv, load_sem, stage_sem, wstage_sem, down_sem):
+               ag_send, ag_recv, load_sem, g_sem, stage_sem, wstage_sem, own_sem, za_send, za_recv, zr_send, zr_recv):
     place = Place()
-    _, tok, model = g_ref.shape
-    ff = gate_ref.shape[1]
+    blocks, tok, model = g_ref.shape
+    ff = weight_ref.shape[1] // 2
+    share = model // 4
     tile = 256
-    share = model // 4
-    loads = [pltpu.make_async_copy(src, dst, load_sem.at[i]) for i, (src, dst) in enumerate(
-        [(gate_hbm, gate_ref), (up_hbm, up_ref), (g_hbm, g_ref)]
-        + [(down_hbm.at[r], down_ref.at[:, r * share:(r + 1) * share]) for r in range(4)])]
-    for copy in loads:
+    def down_at(r):
+        return down_ref.at[:, span(r * share, share)]
+
+    loads, g_loads = [], []
+    for i, (own, every) in enumerate(((gate_own, gate_hbm), (up_own, up_hbm))):
+        for j in range(4):
+            r = lax.rem(place.row + j, 4)
+            loads.append(pltpu.make_async_copy(
+                every.at[r] if j else own, weight_ref.at[span(r * share, share), i * ff:(i + 1) * ff], load_sem.at[4 * i + j]))
+    for j in range(blocks):
+        b = lax.rem(place.me + j, blocks)
+        g_loads.append(pltpu.make_async_copy(g_hbm.at[b] if j else g_own, g_ref.at[b], g_sem.at[j]))
+    own_loads = [pltpu.make_async_copy(two_hbm, two_ref.at[place.me], load_sem.at[8]),
+                 pltpu.make_async_copy(down_hbm, down_at(place.row), load_sem.at[9])]
+    for copy in own_loads + loads + g_loads:
         copy.start()
-
-    def norm_rows(i, _):
-        rows = pl.ds(pl.multiple_of(i * 32, 32), 32)
-        res = res_ref[rows, :]
-        inv = lax.rsqrt(jnp.mean(res * res, axis=-1, keepdims=True) + EPSILON)
-        two_ref[place.me, rows, :] = (res * inv * gain_ref[...]).astype(BF16)
-        return 0
-
-    lax.fori_loop(0, tok // 32, norm_rows, 0)
-    place.greet()
-    gather = Gather(place, two_ref.at[place.me], two_ref, ag_send, ag_recv)
+    place.greet(4)
+    line = Line(place)
+    gather = Gather(place, two_hbm, two_ref, ag_send, ag_recv)
     scatter = Scatter(place, part_ref, sibling_ref, passing_ref, final_ref, rs_send, rs_recv)
+    downs = RowGather(line, down_hbm, down_at, za_send, za_recv)
+    down_sum = RowScatter(line, dgrad_ref, down_recv, merge_ref, merge_ref, zr_send, zr_recv)
     gather.start()
-    for copy in loads:
+    downs.start()
+    for copy in loads + own_loads:
         copy.wait()
 
-    def stage_copy(k):
-        return pltpu.make_async_copy(stage_ref.at[k % 2], out_hbm.at[k], stage_sem.at[k % 2])
-
-    def compute(k):
-        m = place.chips[k]
-        pair = pl.ds(2 * m, 2)
+    def forward(k):
+        pair = pl.ds(2 * place.chips[k], 2)
 
         def hidden_tile(h, _):
-            cols = pl.ds(pl.multiple_of(h * tile, tile), tile)
-            cols2 = pl.ds(pl.multiple_of(ff + h * tile, tile), tile)
+            cols, cols2 = span(h * tile, tile), span(ff + h * tile, tile)
             x = two_ref[pair].reshape(2 * tok, model)
-            gate = dot(x, gate_ref[:, cols])
-            up = dot(x, up_ref[:, cols])
-            back = dot_nt(g_ref[pair].reshape(2 * tok, model), down_ref[cols, :])
+            gate = dot(x, weight_ref[:, cols])
+            up = dot(x, weight_ref[:, cols2])
             s = 1.0 / (1.0 + jnp.exp(-gate))
             act = gate * s
             hid_ref[pair, :, cols] = (act * up).astype(BF16).reshape(2, tok, tile)
-            gu_ref[pair, :, cols] = (back * up * s * (1.0 + gate * (1.0 - s))).astype(BF16).reshape(2, tok, tile)
-            gu_ref[pair, :, cols2] = (back * act).astype(BF16).reshape(2, tok, tile)
+            gu_ref[pair, :, cols] = (up * s * (1.0 + gate * (1.0 - s))).astype(BF16).reshape(2, tok, tile)
+            gu_ref[pair, :, cols2] = act.astype(BF16).reshape(2, tok, tile)
             return 0
 
         lax.fori_loop(0, ff // tile, hidden_tile, 0)
-        if k >= 2:
-            stage_copy(k - 2).wait()
+
+    def backward(k):
+        pair = pl.ds(2 * place.chips[k], 2)
+
+        def hidden_tile(h, _):
+            cols, cols2 = span(h * tile, tile), span(ff + h * tile, tile)
+            back = dot_nt(g_ref[pair].reshape(2 * tok, model), down_ref[cols, :])
+            for where in (cols, cols2):
+                factor = gu_ref[pair, :, where].reshape(2 * tok, tile).astype(F32)
+                gu_ref[pair, :, where] = (back * factor).astype(BF16).reshape(2, tok, tile)
+            return 0
+
+        lax.fori_loop(0, ff // tile, hidden_tile, 0)
 
         def model_tile(n, _):
-            cols = pl.ds(pl.multiple_of(n * tile, tile), tile)
-            gg = gu_ref[pair, :, 0:ff].reshape(2 * tok, ff)
-            ug = gu_ref[pair, :, ff:2 * ff].reshape(2 * tok, ff)
-            back = dot_nt(gg, gate_ref[cols, :]) + dot_nt(ug, up_ref[cols, :])
+            cols = span(n * tile, tile)
+            back = dot_nt(gu_ref[pair].reshape(2 * tok, 2 * ff), weight_ref[cols, :])
             part_ref[k, :, :, cols] = back.astype(BF16).reshape(2, tok, tile)
             return 0
 
         lax.fori_loop(0, model // tile, model_tile, 0)
         scatter.exchange[k].start()
 
-        def out_tile(n, _):
-            cols = pl.ds(pl.multiple_of(n * tile, tile), tile)
-            hid = hid_ref[pair].reshape(2 * tok, ff)
-            out = dot(hid, down_ref[:, cols])
-            stage_ref[k % 2, :, :, cols] = out.astype(BF16).reshape(2, tok, tile)
+    def stage_copy(n):
+        slot = lax.rem(n, 2)
+        return pltpu.make_async_copy(stage_ref.at[slot], out_hbm.at[n // 4, :, :, span(lax.rem(n, 4) * share, share)],
+                                     stage_sem.at[slot])
+
+    def out_tile(n, _):
+        @pl.when(n >= 2)
+        def _():
+            stage_copy(n - 2).wait()
+
+        k, r = n // 4, lax.rem(n, 4)
+        chip = place.chip
+        m = jnp.where(k == 0, chip, jnp.where(k == 1, place.chips[1], jnp.where(k == 2, place.chips[2], place.chips[3])))
+        out = dot(hid_ref[pl.ds(2 * m, 2)].reshape(2 * tok, ff), down_ref[:, span(r * share, share)])
+        stage_ref[lax.rem(n, 2)] = out.astype(BF16).reshape(2, tok, share)
+        stage_copy(n).start()
+        return 0
+
+    def down_grad(k):
+        pair = pl.ds(2 * place.chips[k], 2)
+
+        def down_rows(n, _):
+            rows, r = span(lax.rem(n, ff // tile) * tile, tile), n // (ff // tile)
+            h = hid_ref[pair, :, rows].reshape(2 * tok, tile)
+            g = g_ref[pair, :, span(r * share, share)].reshape(2 * tok, share)
+            term = dot_tn(h, g)
+            if k:
+                term = dsum_ref[r, rows, :] + term
+            if k < 3:
+                dsum_ref[r, rows, :] = term
+            else:
+                dgrad_ref[r, rows, :] = term.astype(BF16)
             return 0
 
-        lax.fori_loop(0, model // tile, out_tile, 0)
-        stage_copy(k).start()
-
-    gather.own_chip()
-    compute(0)
-    gather.neighbours()
-    gather.chip1()
-    compute(1)
-    gather.chip2()
-    scatter.combine(1)
-    scatter.first1.start()
-    compute(2)
-    gather.diagonal()
-    scatter.combine(2)
-    scatter.first2.start()
-    gather.chip3()
-    compute(3)
-    scatter.combine(3)
-    scatter.pass1.start()
-    scatter.pass2.start()
-    scatter.combine(0)
-
-    blocks = two_ref.shape[0]
+        lax.fori_loop(0, 4 * (ff // tile), down_rows, 0)
 
     def wstage_copies(i, slot):
         return (pltpu.make_async_copy(wstage_ref.at[slot, :, 0:ff], gate_grad_hbm.at[i], wstage_sem.at[slot, 0]),
                 pltpu.make_async_copy(wstage_ref.at[slot, :, ff:2 * ff], up_grad_hbm.at[i], wstage_sem.at[slot, 1]))
 
+    def own_copies(half, slot):
+        rows = span(half * tile, tile)
+        return (pltpu.make_async_copy(wstage_ref.at[slot, :, 0:ff], gate_grad_own.at[rows], own_sem.at[0]),
+                pltpu.make_async_copy(wstage_ref.at[slot, :, ff:2 * ff], up_grad_own.at[rows], own_sem.at[1]))
+
     def gate_up_rows(i, _):
-        cols = pl.ds(pl.multiple_of(i * tile, tile), tile)
+        cols = span(i * tile, tile)
         slot = lax.rem(i, 2)
 
         @pl.when(i >= 2)
@@ -890,45 +912,76 @@
         wstage_ref[slot] = dot_tn(x, gu_ref[...].reshape(blocks * tok, 2 * ff)).astype(BF16)
         for copy in wstage_copies(i, slot):
             copy.start()
+
+        @pl.when(i // 2 == place.row)
+        def _():
+            for copy in own_copies(lax.rem(i, 2), slot):
+                copy.start()
+
+        out_tile(2 * i, 0)
+        out_tile(2 * i + 1, 0)
+
+        @pl.when(i // 2 == place.row)
+        def _():
+            for copy in own_copies(lax.rem(i, 2), slot):
+                copy.wait()
+
         return 0
 
+    gather.own_chip()
+    forward(0)
+    for copy in g_loads:
+        copy.wait()
+    down_grad(0)
+    gather.neighbours()
+    downs.forward()
+    gather.chip1()
+    forward(1)
+    down_grad(1)
+    gather.chip2()
+    forward(2)
+    down_grad(2)
+    gather.diagonal()
+    gather.chip3()
+    forward(3)
+    downs.finish()
+    backward(3)
+    down_grad(3)
+    down_sum.start_over()
+    down_sum.start()
+    own_down = pltpu.make_async_copy(dgrad_ref.at[place.row], down_own, load_sem.at[10])
+    own_down.start()
+    scatter.combine(3)
+    scatter.pass1.start()
+    scatter.pass2.start()
+    backward(1)
+    backward(2)
+    scatter.combine(1)
+    scatter.first1.start()
+    scatter.combine(2)
+    scatter.first2.start()
+    backward(0)
+    scatter.finish_two()
+    scatter.combine(0)
     count = model // tile
     lax.fori_loop(0, count // 2, gate_up_rows, 0)
-    scatter.finish_two()
+
+    def merge():
+        def add(n, _):
+            rows = span(n * 64, 64)
+            merge_ref[rows, :] = (merge_ref[rows, :].astype(F32) + dgrad_ref[line.c, rows, :].astype(F32)).astype(BF16)
+            return 0
+
+        lax.fori_loop(0, ff // 64, add, 0)
+
+    down_sum.add(merge)
     lax.fori_loop(count // 2, count, gate_up_rows, 0)
-    for i in (count - 2, count - 1):
-        for copy in wstage_copies(i, i % 2):
-            copy.wait()
-
-    stage_copy(2).wait()
-    stage_copy(3).wait()
-
-    def down_rows(i, _):
-        rows = pl.ds(pl.multiple_of(i * tile, tile), tile)
-        h = hid_ref[:, :, rows].reshape(blocks * tok, tile)
-
-        def down_cols(n, _):
-            cols = pl.ds(pl.multiple_of(n * 512, 512), 512)
-            g = g_ref[:, :, cols].reshape(blocks * tok, 512)
-            stage_ref[0, i, :, cols] = dot_tn(h, g).astype(BF16)
-            return 0
-
-        lax.fori_loop(0, model // 512, down_cols, 0)
-        return 0
-
-    lax.fori_loop(0, ff // tile, down_rows, 0)
-    down_out = [pltpu.make_async_copy(stage_ref.at[0, i, :, r * share:(r + 1) * share],
-                                      down_grad_hbm.at[r, i * tile:(i + 1) * tile], down_sem.at[4 * i + r])
-                for i in range(ff // tile) for r in range(4)]
-    for copy in down_out:
-        copy.start()
-
     scatter.arrive()
 
     def finish(i, sums):
-        rows = pl.ds(pl.multiple_of(i * 32, 32), 32)
+        rows = span(i * 32, 32)
         res = res_ref[rows, :]
-        inv = lax.rsqrt(jnp.mean(res * res, axis=-1, keepdims=True) + EPSILON)
+        inv = norm_inverse(res)
         grad = scatter.total(rows)
         v = grad * gain_ref[...]
         mean = jnp.mean(v * res, axis=-1, keepdims=True)
@@ -938,18 +991,24 @@
         return sums + jnp.sum(grad * res * inv, axis=0, keepdims=True)
 
     gain_grad_ref[...] = lax.fori_loop(0, tok // 32, finish, jnp.zeros((1, model), F32))
-    for copy in down_out:
-        copy.wait()
+    for i in (count - 2, count - 1):
+        for copy in wstage_copies(i, i % 2):
+            copy.wait()
+    for n in (14, 15):
+        stage_copy(n).wait()
+    own_down.wait()
+    down_sum.finish()
+    down_sum.close()
+    downs.close()
     gather.close()
     scatter.close()
 
 
-def feed_forward(res, gain, g_all, gate, up, down):
+def feed_forward(res, gain, two, g, g_all, slabs):
     tok, model = res.shape
-    ff = gate.shape[1]
+    ff = slabs[0].shape[1]
     blocks = g_all.shape[0]
-    any_spec = pl.BlockSpec(memory_space=pl.ANY)
-    vmem = pl.BlockSpec(memory_space=pltpu.VMEM)
+    dma = pltpu.SemaphoreType.DMA
     return pl.pallas_call(
         ffn_kernel,
         out_shape=(
@@ -959,66 +1018,82 @@
             jax.ShapeDtypeStruct((1, model), F32),
             jax.ShapeDtypeStruct((model // 256, 256, ff), BF16),
             jax.ShapeDtypeStruct((model // 256, 256, ff), BF16),
-            jax.ShapeDtypeStruct((4, ff, model // 4), BF16),
+            jax.ShapeDtypeStruct((model // 4, ff), BF16),
+            jax.ShapeDtypeStruct((model // 4, ff), BF16),
+            jax.ShapeDtypeStruct((ff, model // 4), BF16),
+            jax.ShapeDtypeStruct((3, ff, model // 4), BF16),
         ),
-        in_specs=[vmem, vmem] + [any_spec] * 4,
-        out_specs=(any_spec, vmem, vmem, vmem, any_spec, any_spec, any_spec),
+        in_specs=[VMEM_SPEC, VMEM_SPEC] + [ANY_SPEC] * 8,
+        out_specs=(ANY_SPEC, VMEM_SPEC, VMEM_SPEC, VMEM_SPEC) + (ANY_SPEC,) * 6,
         scratch_shapes=[
             pltpu.VMEM((blocks, tok, model), BF16),
             pltpu.VMEM((blocks, tok, model), BF16),
-            pltpu.VMEM((model, ff), BF16),
-            pltpu.VMEM((model, ff), BF16),
+            pltpu.VMEM((model, 2 * ff), BF16),
             pltpu.VMEM((ff, model), BF16),
             pltpu.VMEM((blocks, tok, ff), BF16),
             pltpu.VMEM((blocks, tok, 2 * ff), BF16),
-            pltpu.VMEM((2, 2, tok, model), BF16),
+            pltpu.VMEM((2, 2, tok, model // 4), BF16),
             pltpu.VMEM((2, 256, 2 * ff), BF16),
+            pltpu.VMEM((4, ff, model // 4), F32),
+            pltpu.VMEM((4, ff, model // 4), BF16),
+            pltpu.VMEM((ff, model // 4), BF16),
             *scatter_scratch(tok, model),
-            pltpu.SemaphoreType.DMA((GATHER_SLOTS,)),
-            pltpu.SemaphoreType.DMA((GATHER_SLOTS,)),
-            pltpu.SemaphoreType.DMA((7,)),
-            pltpu.SemaphoreType.DMA((2,)),
-            pltpu.SemaphoreType.DMA((2, 2)),
-            pltpu.SemaphoreType.DMA((8,)),
+            dma((GATHER_SLOTS,)), dma((GATHER_SLOTS,)), dma((11,)), dma((blocks,)), dma((2,)), dma((2, 2)), dma((2,)),
+            dma((ROW_SLOTS,)), dma((ROW_SLOTS,)), dma((ROW_SLOTS,)), dma((ROW_SLOTS,)),
         ],
-        compiler_params=pltpu.CompilerParams(collective_id=2, has_side_effects=True, vmem_limit_bytes=60 * 1024 * 1024),
+        compiler_params=pltpu.CompilerParams(collective_id=2, has_side_effects=True, vmem_limit_bytes=62 * 1024 * 1024),
         cost_estimate=pl.CostEstimate(flops=18 * blocks * tok * model * ff, bytes_accessed=64 << 20, transcendentals=0),
-    )(res, gain, g_all, gate, up, down)
-
-
-def backward_kernel(heads, branch_hbm, out_hbm, x_hbm, w_hbm, gate_grad, up_grad, down_grad,
-                    table_ref, gq_ref, gk_ref, small_in, merged_hbm,
-                    raw_ref, o_ref, qa_ref, ka_ref, kt_ref, vt_ref, inv_ref,
-                    ysum_ref, outsum_ref, grad_hbm, gate_recv, up_recv, down_recv, attn_recv, attn_merge, pieces_out, small_out,
-                    every_ref, w_ref, pg_ref, merged_ref, xt_ref, wstage_ref,
+    )(res, gain, two, g, g_all, *slabs)
+
+
+def backward_kernel(heads, branch_hbm, out_hbm, x_hbm, w_hbm, gate_grad, up_grad, merged_hbm,
+                    table_ref, gq_ref, gk_ref, gain_grad_ref, qkv_ref, gain_ref,
+                    raw_hbm, o_hbm, qa_hbm, ka_hbm, kt_hbm, vt_hbm, inv_hbm,
+                    ysum_ref, outsum_ref, grad_qkv_ref, grad_out_ref, grad_gain_ref, small_out,
+                    grad_hbm, gate_recv, up_recv, attn_recv,
+                    raw_ref, o_ref, qa_ref, ka_ref, kt_ref, vt_ref, inv_ref, kept_sem,
+                    every_ref, w_ref, pg_ref, merged_ref, xt_ref, wstage_ref, gwo_ref,
                     doa_ref, dopad_ref, qpad_ref, va_ref, dq_ref, acc_ref,
                     part_ref, sibling_ref, passing_ref, final_ref, rs_send, rs_recv, rs2_send, rs2_recv,
                     ag_send, ag_recv, load_sem, xt_sem, wstage_sem, ready_sem,
-                    ffn_merge, ffn_own, z_send, z_recv, own_sem, small_ref, small_row, small_mid, small_last,
+                    ffn_merge, ffn_own, z_send, z_recv, own_sem, small_ref, small_row, small_mid, small_last, pieces_ref, amerge_ref, aown_ref,
                     s_send, s_recv, t_send, t_recv, p_send, p_recv):
     place = Place()
-    blocks, tok, model = every_ref.shape
+    blocks, tok, model = every_ref.shape[0] * every_ref.shape[1], every_ref.shape[2], every_ref.shape[3]
+    branch_all = every_ref.reshape(blocks, tok, model)
+    columns = heads.columns
+    lead = 256 - heads.wide
     load_w = pltpu.make_async_copy(w_hbm, w_ref, load_sem.at[0])
     load_out = pltpu.make_async_copy(out_hbm, part_ref, load_sem.at[1])
-    load_own = pltpu.make_async_copy(branch_hbm, every_ref.at[place.me], load_sem.at[2])
+    load_own = pltpu.make_async_copy(branch_hbm, branch_all.at[place.me], load_sem.at[2])
     load_merged = pltpu.make_async_copy(merged_hbm, merged_ref, load_sem.at[3])
+    load_out.start()
     load_own.start()
     load_w.start()
-    load_out.start()
+    load_kept = [pltpu.make_async_copy(src, dst, kept_sem.at[i]) for i, (src, dst) in enumerate((
+        (qa_hbm, qa_ref), (vt_hbm, vt_ref), (o_hbm, o_ref), (ka_hbm, ka_ref), (kt_hbm, kt_ref), (raw_hbm, raw_ref),
+        (inv_hbm, inv_ref)))]
+    for copy in load_kept:
+        copy.start()
     load_merged.start()
     place.greet_all(4)
-    gather = Gather(place, branch_hbm, every_ref, ag_send, ag_recv)
+    gather = Gather(place, branch_hbm, branch_all, ag_send, ag_recv)
     gather.start()
     line = Line(place)
     ffn = [RowScatter(line, part, recv, ffn_merge.at[i], ffn_merge.at[i], z_send.at[i], z_recv.at[i])
-           for i, (part, recv) in enumerate(((gate_grad, gate_recv), (up_grad, up_recv), (down_grad, down_recv)))]
+           for i, (part, recv) in enumerate(((gate_grad, gate_recv), (up_grad, up_recv)))]
     for one in ffn:
         one.start_over()
     for one in ffn:
         one.start()
+    first = Scatter(place, part_ref, sibling_ref, passing_ref, final_ref, rs_send, rs_recv)
+    second = Scatter(place, every_ref, sibling_ref, passing_ref, final_ref, rs2_send, rs2_recv)
+    load_out.wait()
+    for copy in first.exchange:
+        copy.start()
 
     def ffn_add(i):
-        own = (gate_grad, up_grad, down_grad)[i]
+        own = (gate_grad, up_grad)[i]
 
         def work():
             load = pltpu.make_async_copy(own.at[line.c], ffn_own, own_sem.at[0])
@@ -1027,27 +1102,27 @@
 
             def add(n, _):
                 rows = span(n * 64, 64)
-                ffn_merge[i, rows, :] = (ffn_merge[i, rows, :].astype(F32) + ffn_own[rows, :].astype(F32)).astype(BF16)
+                ffn_merge[i, rows, :] = ffn_merge[i, rows, :] + ffn_own[rows, :]
                 return 0
 
             lax.fori_loop(0, ffn_own.shape[0] // 64, add, 0)
 
         ffn[i].add(work)
 
-    first = Scatter(place, part_ref, sibling_ref, passing_ref, final_ref, rs_send, rs_recv)
-    second = Scatter(place, part_ref, sibling_ref, passing_ref, final_ref, rs2_send, rs2_recv)
+    def tell(n, others):
+        for other in others:
+            pl.semaphore_signal(ready_sem.at[n], inc=1, device_id=(place.row, other), device_id_type=MESH)
+
     back = Backward(heads, place.me, table_ref, gq_ref, gk_ref, raw_ref, o_ref, qa_ref, ka_ref, kt_ref, vt_ref, inv_ref,
                     doa_ref, dopad_ref, qpad_ref, va_ref, dq_ref, acc_ref)
-    lead = 256 - heads.wide
 
     def prepare(b, _):
         back.prepare(b)
         return 0
 
+    for copy in load_kept:
+        copy.wait()
     lax.fori_loop(0, blocks, prepare, 0)
-    load_out.wait()
-    for copy in first.exchange:
-        copy.start()
     load_w.wait()
     load_own.wait()
 
@@ -1056,7 +1131,7 @@
 
         def gradient(j, _):
             b = 2 * m + j
-            dm = dot(every_ref[b], w_ref[:, 384:640])
+            dm = dot(branch_all[b], w_ref[:, 384:640])
             back.gradient(b, dm[:, lead:])
             return 0
 
@@ -1081,11 +1156,27 @@
     first.first2.start()
     gather.diagonal()
     first.combine(0)
+    tell(0, (place.sib,))
     gather.chip3()
-    ffn_add(2)
     compute(3)
     first.finish_two()
-
+    tell(1, place.same[1:3])
+    load_merged.wait()
+    tile = 256
+    count = model // tile
+
+    def x_copy(i, slot):
+        return pltpu.make_async_copy(x_hbm.at[:, :, span(i * tile, tile)], xt_ref.at[slot], xt_sem.at[slot])
+
+    x_copy(0, 0).start()
+
+    def out_rows(i, _):
+        out = dot_tn(branch_all[:, :, span(i * tile, tile)].reshape(blocks * tok, tile), merged_ref[...])
+        gwo_ref[i] = out.astype(BF16)
+        return 0
+
+    lax.fori_loop(0, count, out_rows, 0)
+    gather.close()
     pad = 512 - heads.qkv
 
     def finish(b, sums):
@@ -1095,12 +1186,85 @@
         return sums
 
     zero = jnp.zeros((D, tok), F32)
-    sum_q, sum_k = lax.fori_loop(0, blocks, finish, (zero, zero))
-    head_gains = jnp.sum(jnp.transpose(jnp.concatenate([sum_q, sum_k], axis=0)), axis=0, keepdims=True)
+    sums = lax.fori_loop(0, blocks, finish, (zero, zero))
+
+    def grad_copy(i, slot):
+        return pltpu.make_async_copy(wstage_ref.at[slot], grad_hbm.at[i // 2, lax.rem(i, 2)], wstage_sem.at[slot])
+
+    def weight_rows(i, _):
+        slot = lax.rem(i, 2)
+
+        @pl.when(i + 1 < count)
+        def _():
+            x_copy(i + 1, 1 - slot).start()
+
+        @pl.when(i >= 2)
+        def _():
+            grad_copy(i - 2, slot).wait()
+
+        x_copy(i, slot).wait()
+        x = xt_ref[slot].reshape(blocks * tok, tile)
+        qkv = dot_tn(x, pg_ref[...].reshape(blocks * tok, 512))
+        wstage_ref[slot, :, 0:heads.qkv] = qkv[:, 0:heads.qkv].astype(BF16)
+        wstage_ref[slot, :, heads.qkv:columns] = gwo_ref[i, :, lead:]
+        grad_copy(i, slot).start()
+        return 0
+
+    lax.fori_loop(0, count, weight_rows, 0)
+    for i in (count - 2, count - 1):
+        grad_copy(i, i % 2).wait()
+
+    def block(n):
+        return part_ref.at[n, :, :, 0:columns]
+
+    attn = RowScatter(line, grad_hbm, attn_recv, amerge_ref, amerge_ref, z_send.at[2], z_recv.at[2])
+    attn.start_over()
+    attn.start()
+    load_passed = pltpu.make_async_copy(grad_hbm.at[line.c], aown_ref, own_sem.at[2])
+    load_passed.start()
+
+    def attn_work():
+        def add(n, _):
+            b, rows = n // 4, span(lax.rem(n, 4) * 64, 64)
+            amerge_ref[b, rows, :] = amerge_ref[b, rows, :] + aown_ref[b, rows, :]
+            return 0
+
+        lax.fori_loop(0, 8, add, 0)
+
+    def project(k):
+        m = place.chips[k]
+
+        def model_tile(n, _):
+            cols = span(n * 512, 512)
+            out = dot_nt(pg_ref[pl.ds(2 * m, 2)].reshape(2 * tok, 512), w_ref[cols, 0:512])
+            every_ref[k, :, :, cols] = out.astype(BF16).reshape(2, tok, 512)
+            return 0
+
+        lax.fori_loop(0, model // 512, model_tile, 0)
+        if k == 3:
+            pl.semaphore_wait(ready_sem.at[0], 1)
+        second.exchange[k].start()
+
+    project(3)
+    project(1)
+    second.combine(3)
+    pl.semaphore_wait(ready_sem.at[1], 2)
+    second.pass1.start()
+    second.pass2.start()
+    project(2)
+    second.combine(1)
+    load_passed.wait()
+    attn.add(attn_work)
+    project(0)
+    second.combine(2)
+
+    head_gains = jnp.sum(jnp.transpose(jnp.concatenate(sums, axis=0)), axis=0, keepdims=True)
     row8 = lax.broadcasted_iota(jnp.int32, (8, 128), 0)
     for r in range(4):
         for n in range(PLANE):
-            small_ref[r, n] = jnp.where(row8 == 1, head_gains, small_in[r, n])
+            start = (r * PLANE + n) * D
+            piece = jnp.concatenate([gain_grad_ref[:, start:start + D], jnp.zeros((1, 128 - D), F32)], axis=1)
+            small_ref[r, n] = jnp.where(row8 == 0, piece, jnp.where(row8 == 1, head_gains, 0.0))
     small_sends = []
     for j in range(1, 4):
         other = lax.rem(place.row + j, 4)
@@ -1108,52 +1272,6 @@
     for copy in small_sends:
         copy.start()
     small_row[place.row] = small_ref[place.row]
-    load_merged.wait()
-
-    tile = 256
-    count = model // tile
-
-    def x_copy(i, slot):
-        return pltpu.make_async_copy(x_hbm.at[:, :, span(i * tile, tile)], xt_ref.at[slot], xt_sem.at[slot])
-
-    def grad_copy(i, slot):
-        return pltpu.make_async_copy(wstage_ref.at[slot], grad_hbm.at[i // 2, lax.rem(i, 2)], wstage_sem.at[slot])
-
-    x_copy(0, 0).start()
-
-    def weight_rows(i, _):
-        slot = lax.rem(i, 2)
-        cols = span(i * tile, tile)
-
-        @pl.when(i + 1 < count)
-        def _():
-            x_copy(i + 1, 1 - slot).start()
-
-        @pl.when(i >= 2)
-        def _():
-            grad_copy(i - 2, slot).wait()
-
-        out = dot_tn(every_ref[:, :, cols].reshape(blocks * tok, tile), merged_ref[...])
-        x_copy(i, slot).wait()
-        x = xt_ref[slot].reshape(blocks * tok, tile)
-        qkv = dot_tn(x, pg_ref[...].reshape(blocks * tok, 512))
-        wstage_ref[slot, :, 0:heads.qkv] = qkv[:, 0:heads.qkv].astype(BF16)
-        wstage_ref[slot, :, heads.qkv:heads.columns] = out[:, lead:].astype(BF16)
-        grad_copy(i, slot).start()
-        return 0
-
-    lax.fori_loop(0, count, weight_rows, 0)
-    for i in (count - 2, count - 1):
-        grad_copy(i, i % 2).wait()
-    columns = heads.columns
-    gather.close()
-    merged_term = every_ref.at[0:2, :, 0:columns]
-    attn = RowScatter(line, grad_hbm, attn_recv, attn_merge, merged_term, z_send.at[3], z_recv.at[3])
-    attn.start_over()
-    attn.start()
-    own_term = pltpu.make_async_copy(grad_hbm.at[place.row], every_ref.at[6:8, :, 0:columns], own_sem.at[1])
-    own_term.start()
-    first.arrive()
 
     def take(out_ref, scatter):
         def one(i, _):
@@ -1163,56 +1281,25 @@
 
         lax.fori_loop(0, tok // 32, one, 0)
 
+    first.arrive()
     take(outsum_ref, first)
+    tell(2, place.same[1:3])
     first.close()
-    for other in (place.sib, place.same[1], place.same[2]):
-        pl.semaphore_signal(ready_sem, inc=1, device_id=(place.row, other), device_id_type=MESH)
-    pl.semaphore_wait(ready_sem, 3)
-
-    def project(k):
-        m = place.chips[k]
-
-        def model_tile(n, _):
-            cols = span(n * 512, 512)
-            out = dot_nt(pg_ref[pl.ds(2 * m, 2)].reshape(2 * tok, 512), w_ref[cols, 0:512])
-            part_ref[k, :, :, cols] = out.astype(BF16).reshape(2, tok, 512)
-            return 0
-
-        lax.fori_loop(0, model // 512, model_tile, 0)
-        second.exchange[k].start()
+    pl.semaphore_wait(ready_sem.at[2], 2)
+    second.first1.start()
+    second.first2.start()
+    second.combine(0)
+    own_term = pltpu.make_async_copy(grad_hbm.at[place.row], block(0), own_sem.at[1])
+    own_term.start()
 
     def add_blocks(target, source):
         def add(n, _):
             b, rows = n // 4, span(lax.rem(n, 4) * 64, 64)
-            every_ref[target + b, rows, 0:columns] = (
-                every_ref[target + b, rows, 0:columns].astype(F32) + every_ref[source + b, rows, 0:columns].astype(F32)
-            ).astype(BF16)
+            part_ref[target, b, rows, 0:columns] = part_ref[target, b, rows, 0:columns] + part_ref[source, b, rows, 0:columns]
             return 0
 
         lax.fori_loop(0, 8, add, 0)
 
-    def attn_work():
-        loads = [pltpu.make_async_copy(src, every_ref.at[2 * n:2 * n + 2, :, 0:columns], own_sem.at[2 + n])
-                 for n, src in enumerate((attn_merge, grad_hbm.at[line.c]))]
-        for copy in loads:
-            copy.start()
-        for copy in loads:
-            copy.wait()
-        add_blocks(0, 2)
-
-    project(3)
-    project(1)
-    second.combine(3)
-    second.pass1.start()
-    second.pass2.start()
-    project(2)
-    attn.add(attn_work)
-    second.combine(1)
-    second.first1.start()
-    project(0)
-    second.combine(2)
-    second.first2.start()
-    second.combine(0)
     second.finish_two()
     for copy in small_sends:
         copy.wait_recv()
@@ -1238,41 +1325,48 @@
     own_term.wait()
     attn.finish()
 
-    def fold(slot):
-        load = pltpu.make_async_copy(attn_recv.at[slot], every_ref.at[4:6, :, 0:columns], own_sem.at[4 + slot])
-        load.start()
-        load.wait()
-        add_blocks(6, 4)
-
-    fold(0)
-    fold(2)
+    def fold(slots):
+        loads = [pltpu.make_async_copy(attn_recv.at[slot], block(buffer), own_sem.at[4 + slot]) for slot, buffer in slots]
+        for copy in loads:
+            copy.start()
+        for copy in loads:
+            copy.wait()
+        for _, buffer in slots:
+            add_blocks(0, buffer)
+
+    fold(((0, 1), (2, 3)))
 
     @pl.when(line.middle)
     def _():
-        fold(1)
+        fold(((1, 1),))
 
     def piece(n):
-        return every_ref.at[6 + n // 4, span(lax.rem(n, 4) * 64, 64), 0:columns]
-
-    keep = pltpu.make_async_copy(piece(place.me), pieces_out.at[place.me], own_sem.at[7])
+        return part_ref.at[0, n // 4, span(lax.rem(n, 4) * 64, 64), 0:columns]
+
+    keep = pltpu.make_async_copy(piece(place.me), pieces_ref.at[place.me], own_sem.at[7])
     keep.start()
     for j in range(1, PLANE):
         other = lax.rem(place.me + j, PLANE)
-        copy = place.send(piece(other), pieces_out.at[place.me], p_send, p_recv, j, other)
+        copy = place.send(piece(other), pieces_ref.at[place.me], p_send, p_recv, j, other)
         copy.start()
         plane_sends.append(copy)
     for copy in plane_sends[PLANE - 1:]:
         copy.wait_recv()
     keep.wait()
+    unscaled, out_t = attention_sums(heads, lambda s: pieces_ref[s].astype(F32))
+    grad_gain_ref[...] = jnp.broadcast_to(jnp.sum(unscaled * qkv_ref[...].astype(F32), axis=1, keepdims=True), grad_gain_ref.shape)
+    grad_qkv_ref[...] = unscaled * gain_ref[...]
+    grad_out_ref[...] = jnp.transpose(out_t)
     for copy in plane_sends + small_sends:
         copy.wait_send()
     attn.close()
     second.close()
 
 
-def backward_phase(heads, branch, out_part, x_all, w, weight_grads, table, gq, gk, small, kept):
+def backward_phase(heads, branch, out_part, x_all, w, weight_grads, table, gq, gk, gain_grad, w_qkv, gain_attn, kept):
     blocks, tok, model = x_all.shape
     length = blocks * tok
+    depth = w_qkv.shape[0]
     dma = pltpu.SemaphoreType.DMA
     raw, merged, *rest = kept
     return pl.pallas_call(
@@ -1280,39 +1374,46 @@
         out_shape=(
             jax.ShapeDtypeStruct((tok, model), F32),
             jax.ShapeDtypeStruct((tok, model), F32),
+            jax.ShapeDtypeStruct(w_qkv.shape, F32),
+            jax.ShapeDtypeStruct((QUERY_HEADS * D, depth), F32),
+            jax.ShapeDtypeStruct((depth, 128), F32),
+            jax.ShapeDtypeStruct((8, 128), F32),
             jax.ShapeDtypeStruct((4, 2, 256, heads.columns), BF16),
             *(jax.ShapeDtypeStruct((3,) + grad.shape[1:], BF16) for grad in weight_grads),
             jax.ShapeDtypeStruct((3, 2, 256, heads.columns), BF16),
-            jax.ShapeDtypeStruct((2, 256, heads.columns), BF16),
-            jax.ShapeDtypeStruct((PLANE, 64, heads.columns), BF16),
-            jax.ShapeDtypeStruct((8, 128), F32),
         ),
-        in_specs=[ANY_SPEC] * 7 + [VMEM_SPEC] * 4 + [ANY_SPEC] + [VMEM_SPEC] * (1 + len(rest)),
-        out_specs=(VMEM_SPEC, VMEM_SPEC) + (ANY_SPEC,) * 7 + (VMEM_SPEC,),
+        in_specs=[ANY_SPEC] * 7 + [VMEM_SPEC] * 6 + [ANY_SPEC] * (1 + len(rest)),
+        out_specs=(VMEM_SPEC,) * 6 + (ANY_SPEC,) * 4,
         scratch_shapes=[
-            pltpu.VMEM((blocks, tok, model), BF16),
+            *(pltpu.VMEM(array.shape, array.dtype) for array in (raw, *rest)),
+            dma((7,)),
+            pltpu.VMEM((4, 2, tok, model), BF16),
             pltpu.VMEM((model, heads.columns), BF16),
             pltpu.VMEM((blocks, tok, 512), BF16),
             pltpu.VMEM(merged.shape, BF16),
             pltpu.VMEM((2, blocks, tok, 256), BF16),
             pltpu.VMEM((2, 256, heads.columns), BF16),
+            pltpu.VMEM((model // 256, 256, 256), BF16),
             *backward_scratch(heads, length),
             *scatter_scratch(tok, model),
             dma((SCATTER_SLOTS,)), dma((SCATTER_SLOTS,)),
             dma((GATHER_SLOTS,)), dma((GATHER_SLOTS,)), dma((4,)), dma((2,)), dma((2,)),
-            pltpu.SemaphoreType.REGULAR,
-            pltpu.VMEM((3,) + weight_grads[0].shape[1:], BF16),
+            pltpu.SemaphoreType.REGULAR((3,)),
+            pltpu.VMEM((2,) + weight_grads[0].shape[1:], BF16),
             pltpu.VMEM(weight_grads[0].shape[1:], BF16),
-            dma((4, ROW_SLOTS)), dma((4, ROW_SLOTS)), dma((8,)),
+            dma((3, ROW_SLOTS)), dma((3, ROW_SLOTS)), dma((8,)),
             pltpu.VMEM((4, PLANE, 8, 128), F32),
             pltpu.VMEM((4, PLANE, 8, 128), F32),
             pltpu.VMEM((PLANE, 8, 128), F32),
             pltpu.VMEM((PLANE, 8, 128), F32),
+            pltpu.VMEM((PLANE, depth, heads.columns), BF16),
+            pltpu.VMEM((2, 256, heads.columns), BF16),
+            pltpu.VMEM((2, 256, heads.columns), BF16),
             dma((4,)), dma((4,)), dma((PLANE,)), dma((PLANE,)), dma((PLANE,)), dma((PLANE,)),
         ],
-        compiler_params=pltpu.CompilerParams(collective_id=3, has_side_effects=True, vmem_limit_bytes=62 * 1024 * 1024),
+        compiler_params=pltpu.CompilerParams(collective_id=3, has_side_effects=True, vmem_limit_bytes=63 * 1024 * 1024),
         cost_estimate=pl.CostEstimate(flops=60 << 30, bytes_accessed=64 << 20, transcendentals=0),
-    )(branch, out_part, x_all, w, *weight_grads, table, gq, gk, small, merged, raw, *rest)
+    )(branch, out_part, x_all, w, *weight_grads, merged, table, gq, gk, gain_grad, w_qkv, gain_attn, raw, *rest)
 
 
 def norm_back(grad_normed, values_in, inv_rms, gain):
@@ -1418,9 +1519,9 @@
     return jnp.stack(pieces)
 
 
-def attention_sums(heads, pieces):
-    depth = pieces.shape[1]
-    cut = lambda s, start, n: pieces[s, :, start + n * D:start + (n + 1) * D]
+def attention_sums(heads, piece):
+    pieces = [piece(s) for s in range(heads.seq)]
+    cut = lambda s, start, n: pieces[s][:, start + n * D:start + (n + 1) * D]
     queries = [cut(n // heads.queries, 0, n % heads.queries) for n in range(QUERY_HEADS)]
     outs = [cut(n // heads.queries, heads.qkv, n % heads.queries) for n in range(QUERY_HEADS)]
 
@@ -1458,22 +1559,22 @@
     inv = norm_inverse(x)
 
     if plane:
-        residual, g_all, gate, up, down, *kept = attention_phase(
-            heads, x_all, cotangent[0], w, (w_gate, w_up, w_down), table, gq, gk)
-        out_part, residual_grad, branch, gain_two_grad, *weight_grads = feed_forward(
-            residual, gain_two, g_all, gate.reshape(model, -1), up.reshape(model, -1), down)
+        residual, two, g_all, gate, up, *kept = attention_phase(
+            heads, x_all, cotangent[0], w, (w_gate, w_up), table, gq, gk, gain_two)
+        out_part, residual_grad, branch, gain_two_grad, *weight_grads, gate_own, up_own, down_own, down_recv = feed_forward(
+            residual, gain_two, two, cotangent[0], g_all, (w_gate, gate, w_up, up, w_down))
         weight_grads = [grad.reshape((4,) + w_gate.shape) for grad in weight_grads]
-        small = jnp.pad(gain_two_grad.reshape(rows, seq, 1, depth), ((0, 0), (0, 0), (0, 7), (0, 128 - depth)))
-        y_sum, out_sum, _, gate_recv, up_recv, down_recv, _, _, attn_grad, small = backward_phase(
-            heads, branch, out_part, x_all, w, weight_grads, table, gq, gk, small, kept)
+        y_sum, out_sum, grad_qkv, grad_out, grad_gain_attn, small, _, gate_recv, up_recv, _ = backward_phase(
+            heads, branch, out_part, x_all, w, weight_grads, table, gq, gk, gain_two_grad, w_qkv,
+            gain_attn.astype(F32)[:, None], kept)
+        grad_gain_attn = grad_gain_attn[:, 0]
         middle = (row + 1) // 2 == 1
 
-        def row_total(part, recv):
-            own = lax.dynamic_index_in_dim(part, row, 0, keepdims=False).astype(F32)
-            return own + recv[0].astype(F32) + recv[2].astype(F32) + jnp.where(middle, recv[1].astype(F32), 0.0)
+        def row_total(own, recv):
+            return own.astype(F32) + recv[0].astype(F32) + recv[2].astype(F32) + jnp.where(middle, recv[1].astype(F32), 0.0)
 
         grad_gate, grad_up, grad_down = (
-            row_total(part, recv) for part, recv in zip(weight_grads, (gate_recv, up_recv, down_recv)))
+            row_total(own, recv) for own, recv in ((gate_own, gate_recv), (up_own, up_recv), (down_own, down_recv)))
         grad_gain_ffn, head_gains = small[0, :depth], small[1]
     else:
         gate_slab = lax.all_gather(w_gate, "rows", axis=0, tiled=True)
@@ -1491,12 +1592,14 @@
         small = lax.psum(jnp.concatenate([gain_two_grad[0], head_gains[:, 0]]), ("rows", "seq"))
         grad_gain_ffn = lax.dynamic_slice_in_dim(small, (row * seq + lax.axis_index("seq")) * depth, depth)
         head_gains = small[model:]
+        attn_grad = attn_grad.astype(F32)
+        unscaled, grad_out = attention_sums(heads, lambda s: attn_grad[s])
+        grad_out = grad_out.T
+        grad_gain_attn = jnp.sum(unscaled * w_qkv.astype(F32), axis=1)
+        grad_qkv = unscaled * gain_attn.astype(F32)[:, None]
 
     layer_out = (residual + out_sum).astype(BF16)
     grad_tokens = residual_grad + y_sum - x * (inv * inv * jnp.mean(y_sum * x, axis=-1, keepdims=True))
-    unscaled, grad_out = attention_sums(heads, attn_grad.astype(F32))
-    grad_gain_attn = jnp.sum(unscaled * w_qkv.astype(F32), axis=1)
-    grad_qkv = unscaled * gain_attn.astype(F32)[:, None]
     return (
         layer_out[None],
         grad_tokens[None],
@@ -1504,7 +1607,7 @@
         grad_qkv,
         head_gains[:D],
         head_gains[D:],
-        grad_out.T,
+        grad_out,
         grad_gain_ffn,
         grad_gate,
         grad_up,

time: 478 us -> 416 us (0.87)
  Pallas kernels: 436 us -> 381 us
  other arithmetic: 20.5 us -> 14.5 us
    pallas_call x1, Pallas kernels: 112 us -> 80 us  [attention_phase(): pl.pallas_call(functools.partial(attention_kernel, heads), out_shape=(jax...]
    pallas_call x1, Pallas kernels: 168 us -> 137 us  [backward_phase(): pl.pallas_call(functools.partial(backward_kernel, heads), out_shape=(jax....]
    pallas_call x1, Pallas kernels: 94.6 us -> 102 us  [feed_forward(): pl.pallas_call(ffn_kernel, out_shape=(jax.ShapeDtypeStruct((4, 2, tok, mo...]
where the time goes in v5:
time: 416 us; the launch traced here: 408 us
  Pallas kernels  381 us (92%)
  other arithmetic  14.5 us (3%)
  local copies, waits for them, and re-layouts  11.6 us (3%)
    pallas_call x1, Pallas kernels, backward_phase(): pl.pallas_call(functools.partial(backward_kernel, heads), out_shape=(jax....  137 us
    pallas_call x1, Pallas kernels, feed_forward(): pl.pallas_call(ffn_kernel, out_shape=(jax.ShapeDtypeStruct((4, 2, tok, mo...  102 us
    pallas_call x1, Pallas kernels, attention_phase(): pl.pallas_call(functools.partial(attention_kernel, heads), out_shape=(jax...  80 us
    pallas_call x1, Pallas kernels, start_phase(): pl.pallas_call(start_kernel, out_shape=(jax.ShapeDtypeStruct((PLANE, tok,...  62.1 us

profile of v5, /device:TPU:0, one launch (start us, length us, event | category | flops | bytes accessed | tf_op | source)
XLA Modules:
  0.0 408.4 jit_solution(2386708421798801690)
XLA Ops:
  0.7 0.0 copy-start
  0.7 0.7 convert_bitcast_fusion
  1.4 1.1 multiply_convert_fusion
  2.5 0.0 copy-start.15
  2.5 0.0 copy-start.17
  2.5 1.1 fusion.25
  3.6 0.1 fusion.26
  3.7 0.1 fusion.16
  3.8 0.1 fusion.19
  3.9 0.1 fusion.20
  4.0 0.1 fusion.21
  4.1 0.0 copy-start.18
  4.1 0.0 copy-start.19
  4.1 0.1 fusion.10
  4.2 0.1 fusion.13
  4.3 0.1 fusion.22
  4.4 0.1 fusion.24
  4.5 0.1 concatenate.43
  4.7 0.0 copy-start.7
  4.7 0.2 multiply_cosine_fusion
  4.9 0.3 fusion
  5.3 0.6 select_maximum_fusion.table_ref
  5.9 0.0 copy-done.17
  5.9 0.6 pad_convert_fusion.gain_ref
  6.5 0.0 copy-done.7
  6.5 62.1 %shard_map.212 = (bf16[8,256,2048]{2,1,0:T(8,128)(2,1)}, f32[8,80,256]{2,1,0:T(8,128)}, bf16[4,8,64,640]{3,2,1,0:T(8,128)(2,1)}, f32[4,8,8,128]{3,2,1,0:T(8,128)}) custom-call(bf16[256,2048]{1,0:T(8,128)(2,1)} %bitcast.85, f32[80,256]{1,0:T(8,128)} %select_maximum_fusion.table_ref, bf16[8,64,640]{2,1,0:T(8,128)(2,1)} %copy-done.7, ...), custom_call_target="tpu_custom_call" | custom-call | bytes 167772160 | tf_op jit(solution)/shard_map/pallas_call | solution.py:402
  68.6 0.9 slice_reduce_fusion.1
  69.5 0.7 reshape_squeeze.3.gain_ref
  70.2 0.7 copy.30.gq_ref
  70.9 0.7 copy.31.gk_ref
  71.6 80.0 %shard_map.213 = (f32[256,2048]{1,0:T(8,128)}, bf16[256,2048]{1,0:T(8,128)(2,1)}, bf16[8,256,2048]{2,1,0:T(8,128)(2,1)}, bf16[4,512,512]{2,1,0:T(8,128)(2,1)}, b...) custom-call(bf16[8,256,2048]{2,1,0:T(8,128)(2,1)} %get-tuple-element, ...), custom_call_target="tpu_custom_call" | custom-call | flops 42949672960 | bytes 67108864 | tf_op jit(solution)/shard_map/pallas_call | solution.py:759
  151.7 101.9 %shard_map.214 = (bf16[4,2,256,2048]{3,2,1,0:T(8,128)(2,1)}, f32[256,2048]{1,0:T(8,128)}, bf16[256,2048]{1,0:T(8,128)(2,1)}, f32[1,2048]{1,0:T(1,128)}, bf16[8,2...) custom-call(f32[256,2048]{1,0:T(8,128)} %get-tuple-element.50.res_re, ...), custom_call_target="tpu_custom_call" | custom-call | flops 38654705664 | bytes 67108864 | tf_op jit(solution)/shard_map/pallas_call | solution.py:1012
  253.5 2.8 fusion.5
  256.3 0.7 copy.34.gain_ref
  257.0 137.3 %shard_map.215 = (f32[256,2048]{1,0:T(8,128)}, f32[256,2048]{1,0:T(8,128)}, f32[64,2304]{1,0:T(8,128)}, f32[1536,64]{1,0:T(8,128)}, f32[64,128]{1,0:T(8,128)}, /...) custom-call(bf16[256,2048]{1,0:T(8,128)(2,1)} %get-tuple-element.55., ...), custom_call_target="tpu_custom_call" | custom-call | flops 64424509440 | bytes 67108864 | tf_op jit(solution)/shard_map/pallas_call | solution.py:1372
  394.3 0.0 copy-start.6
  394.3 2.8 fusion.6
  397.1 1.3 fusion.7
  398.4 1.0 copy-done.2
  399.4 0.3 fusion.1
  399.7 0.5 copy-done.5
  400.2 1.9 fusion.3
  402.0 1.1 copy-done.4
  403.1 1.2 fusion.4
  404.4 1.0 copy.35
  405.4 1.4 slice_bitcast_fusion
  406.8 0.6 slice_reduce_fusion
  407.4 0.8 copy.44
  (37 shorter events, 0.1 us)
Async XLA Ops:
  0.6 4.0 copy-start.16
  0.7 4.3 %copy-start = (bf16[1,256,2048]{2,1,0:T(8,128)(2,1)S(1)}, bf16[1,256,2048]{2,1,0:T(8,128)(2,1)}, u32[]{:S(2)}) copy-start(bf16[1,256,2048]{2,1,0:T(8,128)(2,1)} %param.13) | copy-start | bytes 3145732
  2.5 2.7 copy-start.15
  2.5 3.4 copy-start.17
  4.1 66.1 %copy-start.18 = (bf16[64]{0:T(256)(128)(2,1)S(1)}, bf16[64]{0:T(256)(128)(2,1)}, u32[]{:S(2)}) copy-start(bf16[64]{0:T(256)(128)(2,1)} %param.19) | copy-start | bytes 388
  4.1 66.8 %copy-start.19 = (bf16[64]{0:T(256)(128)(2,1)S(1)}, bf16[64]{0:T(256)(128)(2,1)}, u32[]{:S(2)}) copy-start(bf16[64]{0:T(256)(128)(2,1)} %param.20) | copy-start | bytes 388
  4.7 1.8 copy-start.7
  5.2 0.7 copy-start.13
  257.0 137.3 %copy-start.11 = (bf16[512,512]{1,0:T(8,128)(2,1)S(1)}, bf16[512,512]{1,0:T(8,128)(2,1)}, u32[]{:S(2)}) copy-start(bf16[512,512]{1,0:T(8,128)(2,1)} %get-tuple-element.77) | copy-start | bytes 1572868
  394.3 2.8 copy-start.6
  394.3 2.8 copy-start.10
  397.1 1.3 copy-start.1
  397.1 2.3 copy-start.2
  398.4 1.3 copy-start.14
  398.4 1.8 copy-start.5
  400.2 1.9 copy-start.3
  400.2 3.0 copy-start.4
  403.1 1.2 copy-start.8
  403.1 3.6 copy-start.12
  403.1 4.2 %copy-start.9 = (f32[64,2304]{1,0:T(8,128)S(1)}, f32[64,2304]{1,0:T(8,128)}, u32[]{:S(2)}) copy-start(f32[64,2304]{1,0:T(8,128)} %get-tuple-element.160) | copy-start | bytes 1769476
